TPU v7x, 32 devices: a whole 2x2x4 slice. The times are simulated.
32 devices in a mesh: row: 4 (over x, core), col: 8 (over z, y).
Axes of the slice: x: 2, y: 2, z: 4, core: 2. Of those that a mesh axis runs over, the one named last changes fastest.
Arguments:
- ao_ints: bfloat16 [5120, 15360], P(('row', 'col')), may hold values from -6 to 6
- vir_coef: bfloat16 [5120, 128], P(('row', 'col')), may hold values from -0.15625 to 0.15625
- naf_vectors: bfloat16 [15360, 7168], P('row', 'col'), may hold values from -0.046875 to 0.046875
Outputs:
- gram: float32 [15360, 15360], P('row', 'col')
- naf_ints: float32 [128, 7168], P('row', 'col')
All inputs are finite; a program needn't handle non-finite values.
Results may differ from a plain program's by a relative error of at most 0.004.
Values may be sent and summed in bfloat16 or wider, within the bound.
No kernel may reach another device: no remote copies, remote signals or barrier semaphores. Data moves between devices by JAX's collectives and lax.ppermute only.
A program may use at most 128 MiB of HBM per device.

v0:
```python
import jax
import jax.numpy as jnp
from jax import lax
from jax.sharding import PartitionSpec as P


def contract_first(lhs, rhs):
    return lax.dot_general(lhs, rhs, (((0,), (0,)), ((), ())), preferred_element_type=jnp.float32)


def contract_second(lhs, rhs):
    return lax.dot_general(lhs, rhs, (((1,), (1,)), ((), ())), preferred_element_type=jnp.float32)


def shards(ao_ints, vir_coef, naf_vectors):
    n_row = lax.axis_size("row")
    n_col = lax.axis_size("col")
    virtuals = vir_coef.shape[1]
    aux_total = ao_ints.shape[1]
    row_width = aux_total // n_row
    col_width = aux_total // n_col
    row_index = lax.axis_index("row")
    col_index = lax.axis_index("col")
    owned_rows = lax.psum_scatter(
        contract_first(ao_ints, vir_coef), ("row", "col"), scatter_dimension=0, tiled=True
    ).astype(jnp.bfloat16)
    gathered = lax.all_gather(owned_rows, ("row", "col"), axis=0, tiled=True)
    panel_rows = lax.dynamic_slice_in_dim(gathered, row_index * row_width, row_width, 0)
    panel_cols = lax.dynamic_slice_in_dim(gathered, col_index * col_width, col_width, 0)
    tile_sum = contract_second(panel_rows, panel_cols)
    projection = contract_first(panel_rows, naf_vectors)
    naf_ints = lax.psum_scatter(projection, "row", scatter_dimension=0, tiled=True)
    return (tile_sum * (1.0 / virtuals), naf_ints)


def solution(mesh):
    in_specs = (P(("row", "col"), None), P(("row", "col"), None), P("row", "col"))
    out_specs = (P("row", "col"), P("row", "col"))
    return jax.shard_map(shards, mesh=mesh, in_specs=in_specs, out_specs=out_specs, check_vma=False)
```

profile of v0, /device:TPU:0, one launch (start us, length us, event | category | flops | bytes accessed | tf_op | source)
XLA Modules:
  0.0 237.4 jit_solution(12231669206767626190)
XLA Ops:
  7.2 0.0 copy-start
  7.2 0.0 reduce-scatter.3.cloned.1.call-start
  7.2 0.7 copy-done
  7.9 7.9 %fusion.6 = f32[15360,128]{1,0:T(8,128)} fusion(bf16[160,15360]{1,0:T(8,128)(2,1)} %param.3, bf16[160,128]{1,0:T(8,128)(2,1)S(1)} %copy-done), kind=kOutput, calls=%fused_computation.7 | convolution fusion | flops 629145600 | bytes 12820480 | tf_op jit(solution)/shard_map/dot_general | solution.py:8
  15.9 0.0 reduce-scatter.3.cloned.1.call-update
  15.9 0.0 all-gather.2.cloned.1.call-start
  15.9 125.2 %reduce-scatter.3.cloned.1.call-done = f32[480,128]{1,0:T(8,128)} async-done(((f32[15360,128]{1,0:T(8,128)}), f32[480,128]{1,0:T(8,128)}) %reduce-scatter.3.cloned.1.call-update) | async-done | bytes 245776 | tf_op jit(solution)/shard_map/reduce_scatter | solution.py:24
  141.2 1.6 convert_element_type.3
  142.8 0.0 all-gather.2.cloned.1.call-update
  142.8 0.0 reduce-scatter.5.cloned.1.call-start
  142.9 62.6 %all-gather.2.cloned.1.call-done = bf16[15360,128]{1,0:T(8,128)(2,1)} async-done(((bf16[480,128]{1,0:T(8,128)(2,1)}), bf16[15360,128]{1,0:T(8,128)(2,1)}) %all-gather.2.cloned.1.call-update) | async-done | bytes 3932176 | tf_op jit(solution)/shard_map/all_gather | solution.py:27
  205.5 5.3 %fusion = f32[128,896]{1,0:T(8,128)} fusion(bf16[3840,896]{1,0:T(8,128)(2,1)} %param.5, bf16[15360,128]{1,0:T(8,128)(2,1)} %all-gather.2.cloned.1.call-done, s32[]{:T(128)S(6)} %select_n.6), kind=kOutput, calls=%fused_computation.1 | convolution fusion | flops 880803840 | bytes 8323076 | tf_op jit(solution)/shard_map/dot_general | solution.py:8
  210.8 0.0 reduce-scatter.5.cloned.1.call-update
  210.8 15.7 %convolution_multiply_fusion = f32[3840,1920]{1,0:T(8,128)} fusion(bf16[15360,128]{1,0:T(8,128)(2,1)} %all-gather.2.cloned.1.call-done, s32[]{:T(128)S(6)} %select_n.6, s32[]{:T(128)S(6)} %select_n.7), kind=kOutput, calls=%fused_computation | convolution fusion | flops 1894809600 | bytes 30965768 | tf_op jit(solution)/shard_map/dot_general | solution.py:12
  226.5 4.4 %reduce-scatter.5.cloned.1.call-done = f32[32,896]{1,0:T(8,128)} async-done(((f32[128,896]{1,0:T(8,128)}), f32[32,896]{1,0:T(8,128)}) %reduce-scatter.5.cloned.1.call-update) | async-done | bytes 114704 | tf_op jit(solution)/shard_map/reduce_scatter | solution.py:32
Async XLA Ops:
  7.2 0.8 copy-start
  7.2 134.0 %reduce-scatter.3.cloned.1.call-start = ((), (), s32[]{:S(2)}) async-start(), calls=%async_computation.2 | async-start | bytes 8110080 | tf_op jit(solution)/shard_map/reduce_scatter | solution.py:24
  15.9 189.6 %all-gather.2.cloned.1.call-start = ((), (), s32[]{:S(2)}) async-start(), calls=%async_computation.3 | async-start | bytes 4055040 | tf_op jit(solution)/shard_map/all_gather | solution.py:27
  142.8 88.0 %reduce-scatter.5.cloned.1.call-start = ((), (), s32[]{:S(2)}) async-start(), calls=%async_computation.4 | async-start | bytes 573440 | tf_op jit(solution)/shard_map/reduce_scatter | solution.py:32
Sparse Core Ops, SparseCore 0:
  16.0 125.1 reduce-scatter.2
  145.1 60.3 all-gather.1
  210.9 19.8 reduce-scatter.4
where the time goes:
time: 238 us; the launch traced here: 237 us
  waiting for transfers between devices  192 us (81%)
  matrix products  28.9 us (12%)
  between operations  13.8 us (6%)
    reduce_scatter x1, waiting for transfers between devices, shards(): lax.psum_scatter(contract_first(ao_ints, vir_coef), ('row', 'col'), scatt...  125 us
    all_gather x1, waiting for transfers between devices, shards(): gathered = lax.all_gather(owned_rows, ('row', 'col'), axis=0, tiled=True)  62.6 us
    dot_general x1, matrix products, contract_second(): lax.dot_general(lhs, rhs, (((1,), (1,)), ((), ())), preferred_element_typ...  15.7 us
    dot_general x2, matrix products, contract_first(): lax.dot_general(lhs, rhs, (((0,), (0,)), ((), ())), preferred_element_typ...  13.2 us
  transfers between devices with their start and end apart: 3, of which 3 were waited for; matrix products, arithmetic and copies ran while one was open for 7% of the time, Pallas kernels for 0%

commit v1 on v0

--- a/solution.py
+++ b/solution.py
@@ -1,7 +1,17 @@
+import functools
+
 import jax
 import jax.numpy as jnp
 from jax import lax
+from jax.experimental import pallas as pl
+from jax.experimental.pallas import tpu as pltpu
 from jax.sharding import PartitionSpec as P
+
+AXES = ("row", "col")
+GROUPS = 1
+TURNS = 3
+HEAD = 16
+VMEM_LIMIT = 48 * 2**20
 
 
 def contract_first(lhs, rhs):
@@ -33,7 +43,253 @@
     return (tile_sum * (1.0 / virtuals), naf_ints)
 
 
+ORDERS = (("x", "y", "z0"), ("y", "z0", "x"), ("z0", "x", "y"))
+FLIPS = {"core": (1, 0), "x": (2, 0), "y": (0, 1), "z0": (0, 2), "z1": (0, 4), "yz0": (0, 3), "xcore": (3, 0)}
+
+
+def swap(value, direction):
+    over_row, over_col = FLIPS[direction]
+    pairs = [(r * 8 + c, (r ^ over_row) * 8 + (c ^ over_col)) for r in range(4) for c in range(8)]
+    return lax.ppermute(value, AXES, pairs)
+
+
+def half_kernel(nb, bits, vir, ao, *outs):
+    acc = contract_first(ao[...], vir[...])
+    pieces, bound = outs[:-1], outs[-1]
+    width = 2 * nb
+    for n, out in enumerate(pieces):
+        turn, group = divmod(n, GROUPS)
+        start = (turn * GROUPS + group) * width
+        rows = acc[start : start + width]
+        if turn == 0:
+            out[0, 0] = rows
+        elif turn == 1:
+            out[0, 0, 0] = rows[:nb]
+            out[0, 1, 0] = rows[nb:]
+        else:
+            out[0, 0, 0] = rows[:nb]
+            out[1, 0, 0] = rows[nb:]
+    largest = jnp.max(jnp.max(jnp.abs(acc), axis=0, keepdims=True), axis=1, keepdims=True)
+    largest = jnp.broadcast_to(largest, bound.shape)
+
+    @pl.when(pl.program_id(0) == 0)
+    def _():
+        bound[...] = largest
+
+    @pl.when(pl.program_id(0) > 0)
+    def _():
+        bound[...] = jnp.maximum(bound[...], largest)
+
+
+def half_pieces(ao_ints, vir_coef, core):
+    naos, aux = ao_ints.shape
+    virtuals = vir_coef.shape[1]
+    width = aux // 8
+    nb = width // (2 * TURNS * GROUPS)
+    shapes, specs = [], []
+    for turn in range(TURNS):
+        if turn == 0:
+            shape, block, where = (2, 2, 2 * nb, virtuals), (1, 1, 2 * nb, virtuals), lambda i, b: (i // 2, i % 2, 0, 0)
+        elif turn == 1:
+            shape, block, where = (2, 2, 2, nb, virtuals), (1, 2, 1, nb, virtuals), lambda i, b: (i % 2, 0, i // 2, 0, 0)
+        else:
+            shape, block, where = (2, 2, 2, nb, virtuals), (2, 1, 1, nb, virtuals), lambda i, b: (0, i // 2, i % 2, 0, 0)
+        shapes += [jax.ShapeDtypeStruct(shape, jnp.float32)] * GROUPS
+        specs += [pl.BlockSpec(block, where)] * GROUPS
+    shapes.append(jax.ShapeDtypeStruct((8, virtuals), jnp.float32))
+    specs.append(pl.BlockSpec((8, virtuals), lambda i, b: (0, 0)))
+    *pieces, bound = pl.pallas_call(
+        functools.partial(half_kernel, nb),
+        grid_spec=pltpu.PrefetchScalarGridSpec(
+            num_scalar_prefetch=1,
+            grid=(4,),
+            in_specs=[
+                pl.BlockSpec((naos, virtuals), lambda i, b: (0, 0)),
+                pl.BlockSpec((naos, width), lambda i, b: (0, 4 * (i // 2) + 2 * b[0] + i % 2)),
+            ],
+            out_specs=specs,
+        ),
+        out_shape=shapes,
+        compiler_params=pltpu.CompilerParams(vmem_limit_bytes=VMEM_LIMIT),
+    )(core.reshape(1).astype(jnp.int32), vir_coef, ao_ints)
+    return [p.reshape(2, 2, 2, nb, virtuals) for p in pieces], bound[:1]
+
+
+def exponent_of(bound):
+    return jnp.ceil(jnp.log2(jnp.maximum(bound, 1e-30))) + 1.0
+
+
+def packed(value, exponent):
+    flat = (value * jnp.exp2(14.0 - exponent)).reshape(-1, value.shape[-1]).astype(jnp.float16)
+    head = jnp.broadcast_to(exponent, (HEAD, flat.shape[1])).astype(jnp.float16)
+    return jnp.concatenate([flat, head], axis=0)
+
+
+def opened(message, lead):
+    exponent = message[-1:].astype(jnp.float32)
+    body = message[:-HEAD]
+    return body.reshape(lead + (-1, body.shape[1])), exponent
+
+
+def pick(array, indices):
+    for index in indices:
+        array = lax.dynamic_index_in_dim(array, index, 0, keepdims=False)
+    return array
+
+
+def total(sources, indices):
+    acc = None
+    for array, exponent, taken in sources:
+        part = pick(array, indices[taken:])
+        if exponent is not None:
+            part = part.astype(jnp.float32) * jnp.exp2(exponent - 14.0)
+        acc = part if acc is None else acc + part
+    return acc
+
+
+def gram_kernel(nb, scale, bits, own, over_z, over_y, over_yz, col_own, col_other, out, cols):
+    step = pl.program_id(0)
+    width = 2 * nb
+
+    @pl.when(step == 0)
+    def _():
+        z0 = bits[1]
+        for n in range(TURNS * GROUPS):
+            first = pl.multiple_of(n * width + z0 * nb, 16)
+            second = pl.multiple_of(n * width + (1 - z0) * nb, 16)
+            cols[pl.ds(first, nb), :] = col_own[n * nb : (n + 1) * nb, :]
+            cols[pl.ds(second, nb), :] = col_other[n * nb : (n + 1) * nb, :]
+
+    n = TURNS * GROUPS
+    for source, rows in enumerate((own, over_z, over_y, over_yz)):
+
+        @pl.when(step // n == source)
+        def _(rows=rows):
+            start = pl.multiple_of((step % n) * nb, 16)
+            out[...] = contract_second(rows[pl.ds(start, nb), :], cols[...]) * scale
+
+
+def block_of(i, bits):
+    n = TURNS * GROUPS
+    source = i // n
+    y = (bits[0] + source // 2) % 2
+    z0 = (bits[1] + source) % 2
+    return (y * n + i % n) * 2 + z0
+
+
+def gram_tile(bits, panels, col_own, col_other, nb):
+    rows, virtuals = panels[0].shape
+    whole = lambda a: pl.BlockSpec(a.shape, lambda i, b: (0, 0))
+    col_width = 2 * rows
+    return pl.pallas_call(
+        functools.partial(gram_kernel, nb, 1.0 / virtuals),
+        grid_spec=pltpu.PrefetchScalarGridSpec(
+            num_scalar_prefetch=1,
+            grid=(4 * rows // nb,),
+            in_specs=[whole(a) for a in (*panels, col_own, col_other)],
+            out_specs=pl.BlockSpec((nb, col_width), lambda i, b: (block_of(i, b), 0)),
+            scratch_shapes=[pltpu.VMEM((col_width, virtuals), jnp.bfloat16)],
+        ),
+        out_shape=jax.ShapeDtypeStruct((4 * rows, col_width), jnp.float32),
+        compiler_params=pltpu.CompilerParams(vmem_limit_bytes=VMEM_LIMIT),
+    )(bits, *panels, col_own, col_other)
+
+
+def naf_kernel(nb, bits, own, over_z, over_y, over_yz, naf, out):
+    step = pl.program_id(0)
+    n = TURNS * GROUPS
+
+    @pl.when(step == 0)
+    def _():
+        out[...] = jnp.zeros_like(out)
+
+    for source, rows in enumerate((own, over_z, over_y, over_yz)):
+
+        @pl.when(step // n == source)
+        def _(rows=rows):
+            start = pl.multiple_of((step % n) * nb, 16)
+            out[...] += contract_first(rows[pl.ds(start, nb), :], naf[...])
+
+
+def projection_of(bits, panels, naf_vectors, nb):
+    rows, virtuals = panels[0].shape
+    whole = lambda a: pl.BlockSpec(a.shape, lambda i, b: (0, 0))
+    nnaf = naf_vectors.shape[1]
+    return pl.pallas_call(
+        functools.partial(naf_kernel, nb),
+        grid_spec=pltpu.PrefetchScalarGridSpec(
+            num_scalar_prefetch=1,
+            grid=(4 * rows // nb,),
+            in_specs=[whole(a) for a in panels] + [pl.BlockSpec((nb, nnaf), lambda i, b: (block_of(i, b), 0))],
+            out_specs=pl.BlockSpec((virtuals, nnaf), lambda i, b: (0, 0)),
+        ),
+        out_shape=jax.ShapeDtypeStruct((virtuals, nnaf), jnp.float32),
+        compiler_params=pltpu.CompilerParams(vmem_limit_bytes=VMEM_LIMIT),
+    )(bits, *panels, naf_vectors)
+
+
+def shards_4x8(ao_ints, vir_coef, naf_vectors):
+    virtuals = vir_coef.shape[1]
+    row_index = lax.axis_index("row")
+    col_index = lax.axis_index("col")
+    core = row_index % 2
+    place = {"x": row_index // 2, "y": col_index % 2, "z0": col_index // 2 % 2}
+    z1 = col_index // 4
+
+    away, away_bound = half_pieces(ao_ints, vir_coef, 1 - core)
+    away_exponent = exponent_of(away_bound)
+    arrived = [swap(packed(p, away_exponent), "core") for p in away]
+    kept, kept_bound = half_pieces(ao_ints, vir_coef, core)
+    kept_exponent = exponent_of(kept_bound)
+    nb = kept[0].shape[3]
+
+    summed = []
+    for n, (keep, message) in enumerate(zip(kept, arrived)):
+        order = ORDERS[n // GROUPS]
+        body, exponent = opened(message, (2, 2, 2))
+        sources = [(keep, None, 0), (body, exponent, 0)]
+        level = jnp.maximum(kept_exponent, exponent) + 1.0
+        indices = []
+        for step, direction in enumerate(order):
+            out = packed(total(sources, indices + [1 - place[direction]]), level)
+            indices = indices + [place[direction]]
+            body, exponent = opened(swap(out, direction), (2,) * (2 - step))
+            sources.append((body, exponent, step + 1))
+            level = jnp.maximum(level, exponent) + 1.0
+        summed.append((total(sources, indices), level))
+
+    blocks = []
+    for value, level in summed:
+        mine = packed(value, level)
+        theirs = swap(mine, "z1")
+        parts = [opened(m, ()) for m in (mine, theirs)]
+        blocks.append(sum(b.astype(jnp.float32) * jnp.exp2(e - 14.0) for b, e in parts).astype(jnp.bfloat16))
+    own = jnp.concatenate(blocks, axis=0)
+
+    over_z = swap(own, "z0")
+    over_y = swap(own, "y")
+    over_yz = swap(own, "yz0")
+
+    local = jnp.concatenate([own, over_z], axis=0)
+    across = [((z // 2 * 2 + z % 2) * 8 + z * 2 + y, ((1 - z // 2) * 2 + z % 2) * 8 + z * 2 + y) for z in range(4) for y in range(2)]
+    columns = jnp.where(place["x"] == z1, local, lax.ppermute(local, AXES, across))
+    beside = [((x * 2 + z % 2) * 8 + z * 2 + y, (x * 2 + 1 - z % 2) * 8 + z * 2 + y) for x in range(2) for z in range(4) for y in range(2)]
+    columns = jnp.where(core == place["z0"], columns, lax.ppermute(columns, AXES, beside))
+    rows = own.shape[0]
+    col_own, col_other = columns[:rows], columns[rows:]
+
+    bits = jnp.stack([place["y"], place["z0"]]).astype(jnp.int32)
+    panels = (own, over_z, over_y, over_yz)
+    partial = projection_of(bits, panels, naf_vectors, nb).reshape(4, virtuals // 4, -1)
+    naf_ints = pick(partial, [row_index])
+    for flip, direction in ((1, "core"), (2, "x"), (3, "xcore")):
+        naf_ints = naf_ints + swap(pick(partial, [row_index ^ flip]), direction)
+    gram = gram_tile(bits, panels, col_own, col_other, nb)
+    return gram, naf_ints
+
+
 def solution(mesh):
     in_specs = (P(("row", "col"), None), P(("row", "col"), None), P("row", "col"))
     out_specs = (P("row", "col"), P("row", "col"))
-    return jax.shard_map(shards, mesh=mesh, in_specs=in_specs, out_specs=out_specs, check_vma=False)
+    plan = shards_4x8 if (mesh.shape["row"], mesh.shape["col"]) == (4, 8) else shards
+    return jax.shard_map(plan, mesh=mesh, in_specs=in_specs, out_specs=out_specs, check_vma=False)

time: 238 us -> 112 us (0.47)
  waiting for transfers between devices: 192 us -> 37.7 us
  Pallas kernels: 0 us -> 31.5 us
  matrix products: 28.9 us -> 0 us
  starting transfers between devices: 0.12 us -> 25.1 us
  between operations: 13.8 us -> 1.37 us
  local copies, waits for them, and re-layouts: 0.73 us -> 8.87 us
  other arithmetic: 1.6 us -> 6.79 us
    reduce_scatter x2 -> x0, waiting for transfers between devices: 130 us -> none  [the longest x1 125 us: shards(): lax.psum_scatter(contract_first(ao_ints, vir_coef), ('row', 'col'), scatt...]
    all_gather x1 -> x0, waiting for transfers between devices: 62.6 us -> none  [shards(): gathered = lax.all_gather(owned_rows, ('row', 'col'), axis=0, tiled=True)]
    ppermute x0 -> x23, waiting for transfers between devices: none -> 37.7 us  [the longest x21 31.9 us: swap(): return lax.ppermute(value, AXES, pairs)]
    pallas_call x0 -> x4, Pallas kernels: none -> 31.5 us  [the longest x1 13.2 us: gram_tile(): pl.pallas_call(functools.partial(gram_kernel, nb, 1.0 / virtuals), grid_s...]
    dot_general x3 -> x0, matrix products: 28.9 us -> none  [the longest x1 15.7 us: contract_second(): lax.dot_general(lhs, rhs, (((1,), (1,)), ((), ())), preferred_element_typ...]
    ppermute x0 -> x23, starting transfers between devices: none -> 25.1 us  [the longest x21 20.3 us: swap(): return lax.ppermute(value, AXES, pairs)]
    slice x0 -> x10, local copies, waits for them, and re-layouts: none -> 3.99 us  [the longest x9 3.96 us: opened(): body = message[:-HEAD]]
  transfers between devices with their start and end apart: 3 -> 23, of which waited for: 3 -> 15; matrix products, arithmetic and copies ran while one was open for 7% -> 7% of each run, Pallas kernels for 0% -> 13%
where the time goes in v1:
time: 112 us; the launch traced here: 111 us
  waiting for transfers between devices  37.7 us (34%)
  Pallas kernels  31.5 us (28%)
  starting transfers between devices  25.1 us (22%)
  local copies, waits for them, and re-layouts  8.87 us (8%)
  other arithmetic  6.79 us (6%)
  between operations  1.37 us (1%)
    ppermute x21, waiting for transfers between devices, swap(): return lax.ppermute(value, AXES, pairs)  31.9 us
    ppermute x21, starting transfers between devices, swap(): return lax.ppermute(value, AXES, pairs)  20.3 us
    pallas_call x1, Pallas kernels, gram_tile(): pl.pallas_call(functools.partial(gram_kernel, nb, 1.0 / virtuals), grid_s...  13.2 us
    pallas_call x1, Pallas kernels, projection_of(): pl.pallas_call(functools.partial(naf_kernel, nb), grid_spec=pltpu.Prefetc...  9.9 us
    pallas_call x2, Pallas kernels, half_pieces(): pl.pallas_call(functools.partial(half_kernel, nb), grid_spec=pltpu.Prefet...  8.32 us
    ppermute x1, waiting for transfers between devices, shards_4x8(): lax.ppermute(local, AXES, across)  5.75 us
    slice x9, local copies, waits for them, and re-layouts, opened(): body = message[:-HEAD]  3.96 us
    ppermute x1, starting transfers between devices, shards_4x8(): lax.ppermute(local, AXES, across)  3.43 us
  transfers between devices with their start and end apart: 23, of which 15 were waited for; matrix products, arithmetic and copies ran while one was open for 7% of the time, Pallas kernels for 13%

profile of v1, /device:TPU:0, one launch (start us, length us, event | category | flops | bytes accessed | tf_op | source)
XLA Modules:
  0.0 111.3 jit_solution(16239649891254484247)
XLA Ops:
  1.4 4.2 %shard_map.51 = (f32[2,2,640,128]{3,2,1,0:T(8,128)S(1)}, f32[2,2,2,320,128]{4,3,2,1,0:T(8,128)S(1)}, f32[2,2,2,320,128]{4,3,2,1,0:T(8,128)S(1)}, f32[8,128]{1,0:T(8,128)S(1)}) custom-call(s32[1]{0:T(128)} %bitcast.5.bits, bf16[160,128]{1,0:T(8,128)(2,1)S(1)} %copy-done.2, bf16[160,15360]{1,0:T(8,128)(2,1)} %ao.3), custom_call_target="tpu_custom_call" | custom-call | tf_op jit(solution)/shard_map/pallas_call | solution.py:101
  6.1 1.6 %pad_maximum_fusion.1 = (f16[2576,128]{1,0:T(8,128)(2,1)}, f16[2576,128]{1,0:T(8,128)(2,1)}, f16[2576,128]{1,0:T(8,128)(2,1)}) fusion(f16[16,128]{1,0:T(8,128)(2,1)S(1)} %broadcast_in_dim.26, f16[2560,128]{1,0:T(8,128)(2,1)S(1)} %bitcast.244, f16[2560,128]{1,0:T(8,128)(2,1)S(1)} %bitcast.245, f16[2560,128]{1,0:T(8,128)(2,1)S(1)} %fusion), kind=kLoop, calls=%fused_computation.5 | loop fusion | flops 989184 | bytes 3948544 | tf_op jit(solution)/shard_map/concatenate | solution.py:125
  8.7 4.2 %shard_map.50 = (f32[2,2,640,128]{3,2,1,0:T(8,128)S(1)}, f32[2,2,2,320,128]{4,3,2,1,0:T(8,128)S(1)}, f32[2,2,2,320,128]{4,3,2,1,0:T(8,128)S(1)}, f32[8,128]{1,0:T(8,128)S(1)}) custom-call(s32[1]{0:T(128)} %bitcast.2.bits, bf16[160,128]{1,0:T(8,128)(2,1)S(1)} %copy-done.3, bf16[160,15360]{1,0:T(8,128)(2,1)} %ao.3), custom_call_target="tpu_custom_call" | custom-call | tf_op jit(solution)/shard_map/pallas_call | solution.py:101
  19.5 2.6 %collective-permute-start.11 = (f16[1296,128]{1,0:T(8,128)(2,1)S(1)}, f16[1296,128]{1,0:T(8,128)(2,1)S(1)}, u32[]{:S(2)}, u32[]{:S(2)}) collective-permute-start(f16[1296,128]{1,0:T(8,128)(2,1)S(1)} %pad_maximum_fusion.6), channel_id=1, source_target_pairs={{0,2},{1,3},{2,0},{3,1},{4,6},{5,7},{6,4},{7,5},{8,10},{9,11},{10,... | collective-permute-start | bytes 995336 | tf_op jit(solution)/shard_map/ppermute | solution.py:53
  23.7 1.6 %collective-permute-start.6 = (f16[1296,128]{1,0:T(8,128)(2,1)S(1)}, f16[1296,128]{1,0:T(8,128)(2,1)S(1)}, u32[]{:S(2)}, u32[]{:S(2)}) collective-permute-start(f16[1296,128]{1,0:T(8,128)(2,1)S(1)} %pad_maximum_fusion.5), channel_id=1, source_target_pairs={{0,1},{1,0},{2,3},{3,2},{4,5},{5,4},{6,7},{7,6},{8,9},{9,8},{10,11... | collective-permute-start | bytes 995336 | tf_op jit(solution)/shard_map/ppermute | solution.py:53
  26.9 1.6 %collective-permute-start.1 = (f16[1296,128]{1,0:T(8,128)(2,1)S(1)}, f16[1296,128]{1,0:T(8,128)(2,1)S(1)}, u32[]{:S(2)}, u32[]{:S(2)}) collective-permute-start(f16[1296,128]{1,0:T(8,128)(2,1)S(1)} %pad_maximum_fusion.4), channel_id=1, source_target_pairs={{0,16},{1,17},{2,18},{3,19},{4,20},{5,21},{6,22},{7,23},{8,24},{9,... | collective-permute-start | bytes 995336 | tf_op jit(solution)/shard_map/ppermute | solution.py:53
  28.6 2.0 %collective-permute-done.11 = f16[1296,128]{1,0:T(8,128)(2,1)S(1)} collective-permute-done((f16[1296,128]{1,0:T(8,128)(2,1)S(1)}, f16[1296,128]{1,0:T(8,128)(2,1)S(1)}, u32[]{:S(2)}, u32[]{:S(2)}) %collective-permute-start.11) | collective-permute-done | bytes 331808 | tf_op jit(solution)/shard_map/ppermute | solution.py:53
  30.9 1.7 %collective-permute-start.12 = (f16[656,128]{1,0:T(8,128)(2,1)S(1)}, f16[656,128]{1,0:T(8,128)(2,1)S(1)}, u32[]{:S(2)}, u32[]{:S(2)}) collective-permute-start(f16[656,128]{1,0:T(8,128)(2,1)S(1)} %pad_maximum_fusion.10), channel_id=1, source_target_pairs={{0,16},{1,17},{2,18},{3,19},{4,20},{5,21},{6,22},{7,23},{8,24},{9,... | collective-permute-start | bytes 503816 | tf_op jit(solution)/shard_map/ppermute | solution.py:53
  34.7 2.9 %collective-permute-done.1 = f16[1296,128]{1,0:T(8,128)(2,1)S(1)} collective-permute-done((f16[1296,128]{1,0:T(8,128)(2,1)S(1)}, f16[1296,128]{1,0:T(8,128)(2,1)S(1)}, u32[]{:S(2)}, u32[]{:S(2)}) %collective-permute-start.1) | collective-permute-done | bytes 331808 | tf_op jit(solution)/shard_map/ppermute | solution.py:53
  38.5 1.7 %collective-permute-done.12 = f16[656,128]{1,0:T(8,128)(2,1)S(1)} collective-permute-done((f16[656,128]{1,0:T(8,128)(2,1)S(1)}, f16[656,128]{1,0:T(8,128)(2,1)S(1)}, u32[]{:S(2)}, u32[]{:S(2)}) %collective-permute-start.12) | collective-permute-done | bytes 167968 | tf_op jit(solution)/shard_map/ppermute | solution.py:53
  41.2 1.6 %collective-permute-start.8 = (f16[336,128]{1,0:T(8,128)(2,1)S(1)}, f16[336,128]{1,0:T(8,128)(2,1)S(1)}, u32[]{:S(2)}, u32[]{:S(2)}) collective-permute-start(f16[336,128]{1,0:T(8,128)(2,1)S(1)} %pad_maximum_fusion.13), channel_id=1, source_target_pairs={{0,16},{1,17},{2,18},{3,19},{4,20},{5,21},{6,22},{7,23},{8,24},{9,... | collective-permute-start | bytes 258056 | tf_op jit(solution)/shard_map/ppermute | solution.py:53
  42.7 1.6 %collective-permute-done.2 = f16[656,128]{1,0:T(8,128)(2,1)S(1)} collective-permute-done((f16[656,128]{1,0:T(8,128)(2,1)S(1)}, f16[656,128]{1,0:T(8,128)(2,1)S(1)}, u32[]{:S(2)}, u32[]{:S(2)}) %collective-permute-start.2) | collective-permute-done | bytes 167968 | tf_op jit(solution)/shard_map/ppermute | solution.py:53
  45.4 2.7 %collective-permute-start.14 = (f16[336,128]{1,0:T(8,128)(2,1)S(1)}, f16[336,128]{1,0:T(8,128)(2,1)S(1)}, u32[]{:S(2)}, u32[]{:S(2)}) collective-permute-start(f16[336,128]{1,0:T(8,128)(2,1)S(1)} %pad_maximum_fusion.16), channel_id=1, source_target_pairs={{0,4},{1,5},{2,6},{3,7},{4,0},{5,1},{6,2},{7,3},{8,12},{9,13},{10,... | collective-permute-start | bytes 258056 | tf_op jit(solution)/shard_map/ppermute | solution.py:53
  50.3 2.4 %collective-permute-start.4 = (f16[336,128]{1,0:T(8,128)(2,1)S(1)}, f16[336,128]{1,0:T(8,128)(2,1)S(1)}, u32[]{:S(2)}, u32[]{:S(2)}) collective-permute-start(f16[336,128]{1,0:T(8,128)(2,1)S(1)} %pad_maximum_fusion.12), channel_id=1, source_target_pairs={{0,4},{1,5},{2,6},{3,7},{4,0},{5,1},{6,2},{7,3},{8,12},{9,13},{10,... | collective-permute-start | bytes 258056 | tf_op jit(solution)/shard_map/ppermute | solution.py:53
  52.8 3.3 %collective-permute-done.14 = f16[336,128]{1,0:T(8,128)(2,1)S(1)} collective-permute-done((f16[336,128]{1,0:T(8,128)(2,1)S(1)}, f16[336,128]{1,0:T(8,128)(2,1)S(1)}, u32[]{:S(2)}, u32[]{:S(2)}) %collective-permute-start.14) | collective-permute-done | bytes 86048 | tf_op jit(solution)/shard_map/ppermute | solution.py:53
  56.1 1.8 %collective-permute-done.9 = f16[336,128]{1,0:T(8,128)(2,1)S(1)} collective-permute-done((f16[336,128]{1,0:T(8,128)(2,1)S(1)}, f16[336,128]{1,0:T(8,128)(2,1)S(1)}, u32[]{:S(2)}, u32[]{:S(2)}) %collective-permute-start.9) | collective-permute-done | bytes 86048 | tf_op jit(solution)/shard_map/ppermute | solution.py:53
  59.4 7.4 %collective-permute-done.15.over_z = bf16[960,128]{1,0:T(8,128)(2,1)S(1)} collective-permute-done((bf16[960,128]{1,0:T(8,128)(2,1)S(1)}, bf16[960,128]{1,0:T(8,128)(2,1)S(1)}, u32[]{:S(2)}, u32[]{:S(2)}) %collective-permute-start.15) | collective-permute-done | bytes 245792 | tf_op jit(solution)/shard_map/ppermute | solution.py:53
  66.8 3.4 %collective-permute-start.18 = (bf16[1920,128]{1,0:T(8,128)(2,1)S(1)}, bf16[1920,128]{1,0:T(8,128)(2,1)S(1)}, u32[]{:S(2)}, u32[]{:S(2)}) collective-permute-start(bf16[1920,128]{1,0:T(8,128)(2,1)S(1)} %pad_maximum_fusion.3), channel_id=1, source_target_pairs={{0,16},{1,17},{10,26},{11,27},{20,4},{21,5},{30,14},{31,15}} | collective-permute-start | bytes 1474568 | tf_op jit(solution)/shard_map/ppermute | solution.py:275
  70.8 5.8 %collective-permute-done.18 = bf16[1920,128]{1,0:T(8,128)(2,1)S(1)} collective-permute-done((bf16[1920,128]{1,0:T(8,128)(2,1)S(1)}, bf16[1920,128]{1,0:T(8,128)(2,1)S(1)}, u32[]{:S(2)}, u32[]{:S(2)}) %collective-permute-start.18) | collective-permute-done | bytes 491552 | tf_op jit(solution)/shard_map/ppermute | solution.py:275
  79.3 9.9 %shard_map.53 = f32[128,896]{1,0:T(8,128)S(1)} custom-call(s32[2]{0:T(128)S(1)} %pad_add_fusion.bits, bf16[960,128]{1,0:T(8,128)(2,1)S(1)} %pad_maximum_fusion.7.own, bf16[960,128]{1,0:T(8,128)(2,1)S(1)} %collective-permute-done.15.over_z, bf16[960,128]{1,0:T(8,128)(2,1)S(1)} %collective-permute-done.16.over_y, ...), custom_call_target="tpu_custom_call" | custom-call | tf_op jit(solution)/shard_map/pallas_call | solution.py:218
  89.4 1.6 %collective-permute-start.21 = (f32[32,896]{1,0:T(8,128)S(1)}, f32[32,896]{1,0:T(8,128)S(1)}, u32[]{:S(2)}, u32[]{:S(2)}) collective-permute-start(f32[32,896]{1,0:T(8,128)S(1)} %get-tuple-element.52), channel_id=1, source_target_pairs={{0,16},{1,17},{2,18},{3,19},{4,20},{5,21},{6,22},{7,23},{8,24},{9,... | collective-permute-start | bytes 344072 | tf_op jit(solution)/shard_map/ppermute | solution.py:53
  91.2 3.5 %collective-permute-done.22 = f32[32,896]{1,0:T(8,128)S(1)} collective-permute-done((f32[32,896]{1,0:T(8,128)S(1)}, f32[32,896]{1,0:T(8,128)S(1)}, u32[]{:S(2)}, u32[]{:S(2)}) %collective-permute-start.22) | collective-permute-done | bytes 114720 | tf_op jit(solution)/shard_map/ppermute | solution.py:53
  94.7 2.5 %collective-permute-done.21 = f32[32,896]{1,0:T(8,128)S(1)} collective-permute-done((f32[32,896]{1,0:T(8,128)S(1)}, f32[32,896]{1,0:T(8,128)S(1)}, u32[]{:S(2)}, u32[]{:S(2)}) %collective-permute-start.21) | collective-permute-done | bytes 114720 | tf_op jit(solution)/shard_map/ppermute | solution.py:53
  98.0 13.2 %shard_map.52 = f32[3840,1920]{1,0:T(8,128)} custom-call(s32[2]{0:T(128)S(1)} %pad_add_fusion.bits, bf16[960,128]{1,0:T(8,128)(2,1)S(1)} %pad_maximum_fusion.7.own, bf16[960,128]{1,0:T(8,128)(2,1)S(1)} %collective-permute-done.15.over_z, bf16[960,128]{1,0:T(8,128)(2,1)S(1)} %collective-permute-done.16.over_y, ...), custom_call_target="tpu_custom_call" | custom-call | tf_op jit(solution)/shard_map/pallas_call | solution.py:184
  (137 shorter events, 25.2 us)
Async XLA Ops:
  6.1 2.6 %copy-start.3 = (bf16[160,128]{1,0:T(8,128)(2,1)S(1)}, bf16[160,128]{1,0:T(8,128)(2,1)}, u32[]{:S(2)}) copy-start(bf16[160,128]{1,0:T(8,128)(2,1)} %vir.3) | copy-start | bytes 122884
  7.7 8.7 %collective-permute-start = (f16[2576,128]{1,0:T(8,128)(2,1)}, f16[2576,128]{1,0:T(8,128)(2,1)}, u32[]{:S(2)}, u32[]{:S(2)}) collective-permute-start(f16[2576,128]{1,0:T(8,128)(2,1)} %get-tuple-element.64), channel_id=1, source_target_pairs={{0,8},{1,9},{2,10},{3,11},{4,12},{5,13},{6,14},{7,15},{8,0},{9,1},... | collective-permute-start | bytes 1978376 | tf_op jit(solution)/shard_map/ppermute | solution.py:53
  8.2 9.0 %collective-permute-start.10 = (f16[2576,128]{1,0:T(8,128)(2,1)}, f16[2576,128]{1,0:T(8,128)(2,1)}, u32[]{:S(2)}, u32[]{:S(2)}) collective-permute-start(f16[2576,128]{1,0:T(8,128)(2,1)} %get-tuple-element.63), channel_id=1, source_target_pairs={{0,8},{1,9},{2,10},{3,11},{4,12},{5,13},{6,14},{7,15},{8,0},{9,1},... | collective-permute-start | bytes 1978376 | tf_op jit(solution)/shard_map/ppermute | solution.py:53
  8.2 8.9 %collective-permute-start.5 = (f16[2576,128]{1,0:T(8,128)(2,1)}, f16[2576,128]{1,0:T(8,128)(2,1)}, u32[]{:S(2)}, u32[]{:S(2)}) collective-permute-start(f16[2576,128]{1,0:T(8,128)(2,1)} %get-tuple-element.62), channel_id=1, source_target_pairs={{0,8},{1,9},{2,10},{3,11},{4,12},{5,13},{6,14},{7,15},{8,0},{9,1},... | collective-permute-start | bytes 1978376 | tf_op jit(solution)/shard_map/ppermute | solution.py:53
  19.5 11.1 %collective-permute-start.11 = (f16[1296,128]{1,0:T(8,128)(2,1)S(1)}, f16[1296,128]{1,0:T(8,128)(2,1)S(1)}, u32[]{:S(2)}, u32[]{:S(2)}) collective-permute-start(f16[1296,128]{1,0:T(8,128)(2,1)S(1)} %pad_maximum_fusion.6), channel_id=1, source_target_pairs={{0,2},{1,3},{2,0},{3,1},{4,6},{5,7},{6,4},{7,5},{8,10},{9,11},{10,... | collective-permute-start | bytes 995336 | tf_op jit(solution)/shard_map/ppermute | solution.py:53
  23.7 10.0 %collective-permute-start.6 = (f16[1296,128]{1,0:T(8,128)(2,1)S(1)}, f16[1296,128]{1,0:T(8,128)(2,1)S(1)}, u32[]{:S(2)}, u32[]{:S(2)}) collective-permute-start(f16[1296,128]{1,0:T(8,128)(2,1)S(1)} %pad_maximum_fusion.5), channel_id=1, source_target_pairs={{0,1},{1,0},{2,3},{3,2},{4,5},{5,4},{6,7},{7,6},{8,9},{9,8},{10,11... | collective-permute-start | bytes 995336 | tf_op jit(solution)/shard_map/ppermute | solution.py:53
  26.9 10.7 %collective-permute-start.1 = (f16[1296,128]{1,0:T(8,128)(2,1)S(1)}, f16[1296,128]{1,0:T(8,128)(2,1)S(1)}, u32[]{:S(2)}, u32[]{:S(2)}) collective-permute-start(f16[1296,128]{1,0:T(8,128)(2,1)S(1)} %pad_maximum_fusion.4), channel_id=1, source_target_pairs={{0,16},{1,17},{2,18},{3,19},{4,20},{5,21},{6,22},{7,23},{8,24},{9,... | collective-permute-start | bytes 995336 | tf_op jit(solution)/shard_map/ppermute | solution.py:53
  30.9 9.2 %collective-permute-start.12 = (f16[656,128]{1,0:T(8,128)(2,1)S(1)}, f16[656,128]{1,0:T(8,128)(2,1)S(1)}, u32[]{:S(2)}, u32[]{:S(2)}) collective-permute-start(f16[656,128]{1,0:T(8,128)(2,1)S(1)} %pad_maximum_fusion.10), channel_id=1, source_target_pairs={{0,16},{1,17},{2,18},{3,19},{4,20},{5,21},{6,22},{7,23},{8,24},{9,... | collective-permute-start | bytes 503816 | tf_op jit(solution)/shard_map/ppermute | solution.py:53
  34.0 6.9 %collective-permute-start.7 = (f16[656,128]{1,0:T(8,128)(2,1)S(1)}, f16[656,128]{1,0:T(8,128)(2,1)S(1)}, u32[]{:S(2)}, u32[]{:S(2)}) collective-permute-start(f16[656,128]{1,0:T(8,128)(2,1)S(1)} %pad_maximum_fusion.9), channel_id=1, source_target_pairs={{0,2},{1,3},{2,0},{3,1},{4,6},{5,7},{6,4},{7,5},{8,10},{9,11},{10,... | collective-permute-start | bytes 503816 | tf_op jit(solution)/shard_map/ppermute | solution.py:53
  38.0 6.3 %collective-permute-start.2 = (f16[656,128]{1,0:T(8,128)(2,1)S(1)}, f16[656,128]{1,0:T(8,128)(2,1)S(1)}, u32[]{:S(2)}, u32[]{:S(2)}) collective-permute-start(f16[656,128]{1,0:T(8,128)(2,1)S(1)} %pad_maximum_fusion.8), channel_id=1, source_target_pairs={{0,1},{1,0},{2,3},{3,2},{4,5},{5,4},{6,7},{7,6},{8,9},{9,8},{10,11... | collective-permute-start | bytes 503816 | tf_op jit(solution)/shard_map/ppermute | solution.py:53
  40.4 4.8 %collective-permute-start.13 = (f16[336,128]{1,0:T(8,128)(2,1)S(1)}, f16[336,128]{1,0:T(8,128)(2,1)S(1)}, u32[]{:S(2)}, u32[]{:S(2)}) collective-permute-start(f16[336,128]{1,0:T(8,128)(2,1)S(1)} %pad_maximum_fusion.15), channel_id=1, source_target_pairs={{0,1},{1,0},{2,3},{3,2},{4,5},{5,4},{6,7},{7,6},{8,9},{9,8},{10,11... | collective-permute-start | bytes 258056 | tf_op jit(solution)/shard_map/ppermute | solution.py:53
  41.2 6.9 %collective-permute-start.8 = (f16[336,128]{1,0:T(8,128)(2,1)S(1)}, f16[336,128]{1,0:T(8,128)(2,1)S(1)}, u32[]{:S(2)}, u32[]{:S(2)}) collective-permute-start(f16[336,128]{1,0:T(8,128)(2,1)S(1)} %pad_maximum_fusion.13), channel_id=1, source_target_pairs={{0,16},{1,17},{2,18},{3,19},{4,20},{5,21},{6,22},{7,23},{8,24},{9,... | collective-permute-start | bytes 258056 | tf_op jit(solution)/shard_map/ppermute | solution.py:53
  44.5 5.6 %collective-permute-start.3 = (f16[336,128]{1,0:T(8,128)(2,1)S(1)}, f16[336,128]{1,0:T(8,128)(2,1)S(1)}, u32[]{:S(2)}, u32[]{:S(2)}) collective-permute-start(f16[336,128]{1,0:T(8,128)(2,1)S(1)} %pad_maximum_fusion.11), channel_id=1, source_target_pairs={{0,2},{1,3},{2,0},{3,1},{4,6},{5,7},{6,4},{7,5},{8,10},{9,11},{10,... | collective-permute-start | bytes 258056 | tf_op jit(solution)/shard_map/ppermute | solution.py:53
  45.4 10.6 %collective-permute-start.14 = (f16[336,128]{1,0:T(8,128)(2,1)S(1)}, f16[336,128]{1,0:T(8,128)(2,1)S(1)}, u32[]{:S(2)}, u32[]{:S(2)}) collective-permute-start(f16[336,128]{1,0:T(8,128)(2,1)S(1)} %pad_maximum_fusion.16), channel_id=1, source_target_pairs={{0,4},{1,5},{2,6},{3,7},{4,0},{5,1},{6,2},{7,3},{8,12},{9,13},{10,... | collective-permute-start | bytes 258056 | tf_op jit(solution)/shard_map/ppermute | solution.py:53
  48.2 9.7 %collective-permute-start.9 = (f16[336,128]{1,0:T(8,128)(2,1)S(1)}, f16[336,128]{1,0:T(8,128)(2,1)S(1)}, u32[]{:S(2)}, u32[]{:S(2)}) collective-permute-start(f16[336,128]{1,0:T(8,128)(2,1)S(1)} %pad_maximum_fusion.14), channel_id=1, source_target_pairs={{0,4},{1,5},{2,6},{3,7},{4,0},{5,1},{6,2},{7,3},{8,12},{9,13},{10,... | collective-permute-start | bytes 258056 | tf_op jit(solution)/shard_map/ppermute | solution.py:53
  50.3 8.8 %collective-permute-start.4 = (f16[336,128]{1,0:T(8,128)(2,1)S(1)}, f16[336,128]{1,0:T(8,128)(2,1)S(1)}, u32[]{:S(2)}, u32[]{:S(2)}) collective-permute-start(f16[336,128]{1,0:T(8,128)(2,1)S(1)} %pad_maximum_fusion.12), channel_id=1, source_target_pairs={{0,4},{1,5},{2,6},{3,7},{4,0},{5,1},{6,2},{7,3},{8,12},{9,13},{10,... | collective-permute-start | bytes 258056 | tf_op jit(solution)/shard_map/ppermute | solution.py:53
  59.3 7.4 %collective-permute-start.15 = (bf16[960,128]{1,0:T(8,128)(2,1)S(1)}, bf16[960,128]{1,0:T(8,128)(2,1)S(1)}, u32[]{:S(2)}, u32[]{:S(2)}) collective-permute-start(bf16[960,128]{1,0:T(8,128)(2,1)S(1)} %pad_maximum_fusion.7.own), channel_id=1, source_target_pairs={{0,2},{1,3},{2,0},{3,1},{4,6},{5,7},{6,4},{7,5},{8,10},{9,11},{10,... | collective-permute-start | bytes 737288 | tf_op jit(solution)/shard_map/ppermute | solution.py:53
  66.8 9.7 %collective-permute-start.18 = (bf16[1920,128]{1,0:T(8,128)(2,1)S(1)}, bf16[1920,128]{1,0:T(8,128)(2,1)S(1)}, u32[]{:S(2)}, u32[]{:S(2)}) collective-permute-start(bf16[1920,128]{1,0:T(8,128)(2,1)S(1)} %pad_maximum_fusion.3), channel_id=1, source_target_pairs={{0,16},{1,17},{10,26},{11,27},{20,4},{21,5},{30,14},{31,15}} | collective-permute-start | bytes 1474568 | tf_op jit(solution)/shard_map/ppermute | solution.py:275
  70.3 9.1 %collective-permute-start.16 = (bf16[960,128]{1,0:T(8,128)(2,1)S(1)}, bf16[960,128]{1,0:T(8,128)(2,1)S(1)}, u32[]{:S(2)}, u32[]{:S(2)}) collective-permute-start(bf16[960,128]{1,0:T(8,128)(2,1)S(1)} %pad_maximum_fusion.7.own), channel_id=1, source_target_pairs={{0,1},{1,0},{2,3},{3,2},{4,5},{5,4},{6,7},{7,6},{8,9},{9,8},{10,11... | collective-permute-start | bytes 737288 | tf_op jit(solution)/shard_map/ppermute | solution.py:53
  70.8 8.5 %collective-permute-start.17 = (bf16[960,128]{1,0:T(8,128)(2,1)S(1)}, bf16[960,128]{1,0:T(8,128)(2,1)S(1)}, u32[]{:S(2)}, u32[]{:S(2)}) collective-permute-start(bf16[960,128]{1,0:T(8,128)(2,1)S(1)} %pad_maximum_fusion.7.own), channel_id=1, source_target_pairs={{0,3},{1,2},{2,1},{3,0},{4,7},{5,6},{6,5},{7,4},{8,11},{9,10},{10,... | collective-permute-start | bytes 737288 | tf_op jit(solution)/shard_map/ppermute | solution.py:53
  76.7 21.2 %collective-permute-start.19 = (bf16[1920,128]{1,0:T(8,128)(2,1)S(1)}, bf16[1920,128]{1,0:T(8,128)(2,1)S(1)}, u32[]{:S(2)}, u32[]{:S(2)}) collective-permute-start(bf16[1920,128]{1,0:T(8,128)(2,1)S(1)} %broadcast_select_fusion), channel_id=1, source_target_pairs={{0,8},{1,9},{10,2},{11,3},{4,12},{5,13},{14,6},{15,7},{16,24},{17,... | collective-permute-start | bytes 1474568 | tf_op jit(solution)/shard_map/ppermute | solution.py:277
  89.3 5.4 %collective-permute-start.22 = (f32[32,896]{1,0:T(8,128)S(1)}, f32[32,896]{1,0:T(8,128)S(1)}, u32[]{:S(2)}, u32[]{:S(2)}) collective-permute-start(f32[32,896]{1,0:T(8,128)S(1)} %get-tuple-element.51), channel_id=1, source_target_pairs={{0,24},{1,25},{2,26},{3,27},{4,28},{5,29},{6,30},{7,31},{8,16},{9,... | collective-permute-start | bytes 344072 | tf_op jit(solution)/shard_map/ppermute | solution.py:53
  89.4 7.9 %collective-permute-start.21 = (f32[32,896]{1,0:T(8,128)S(1)}, f32[32,896]{1,0:T(8,128)S(1)}, u32[]{:S(2)}, u32[]{:S(2)}) collective-permute-start(f32[32,896]{1,0:T(8,128)S(1)} %get-tuple-element.52), channel_id=1, source_target_pairs={{0,16},{1,17},{2,18},{3,19},{4,20},{5,21},{6,22},{7,23},{8,24},{9,... | collective-permute-start | bytes 344072 | tf_op jit(solution)/shard_map/ppermute | solution.py:53
  90.9 6.3 %collective-permute-start.20 = (f32[32,896]{1,0:T(8,128)S(1)}, f32[32,896]{1,0:T(8,128)S(1)}, u32[]{:S(2)}, u32[]{:S(2)}) collective-permute-start(f32[32,896]{1,0:T(8,128)S(1)} %get-tuple-element.50), channel_id=1, source_target_pairs={{0,8},{1,9},{2,10},{3,11},{4,12},{5,13},{6,14},{7,15},{8,0},{9,1},... | collective-permute-start | bytes 344072 | tf_op jit(solution)/shard_map/ppermute | solution.py:53
  (3 other events, 3.2 us)

commit v2 on v0

--- a/solution.py
+++ b/solution.py
@@ -1,7 +1,16 @@
+import functools
+
 import jax
 import jax.numpy as jnp
 from jax import lax
+from jax.experimental import pallas as pl
+from jax.experimental.pallas import tpu as pltpu
 from jax.sharding import PartitionSpec as P
+
+AXES = ("row", "col")
+TILE = 16
+SLOTS = 3
+VMEM_LIMIT = 11 * 2**20
 
 
 def contract_first(lhs, rhs):
@@ -33,7 +42,313 @@
     return (tile_sum * (1.0 / virtuals), naf_ints)
 
 
+X, Y, Z0, Z1 = (2, 0), (0, 1), (0, 2), (0, 4)
+ORDERS = (((X, Y, Z0), (Y, Z0, X)), ((Z0, X, Y), (Z0, X, Y)))
+
+
+def flipped(value, on_core0, on_core1):
+    pairs = []
+    for r in range(4):
+        over_row, over_col = on_core1 if r % 2 else on_core0
+        pairs += [(r * 8 + c, (r ^ over_row) * 8 + (c ^ over_col)) for c in range(8)]
+    return lax.ppermute(value, AXES, pairs)
+
+
+def half_kernel(sizes, bits, vir, ao, *outs):
+    h = pl.program_id(0)
+    b = bits[0]
+    acc = contract_first(ao[...], vir[...])
+    *pieces, bound = outs
+    half = acc.shape[0] // 2
+    for y in range(2):
+        start = y * half
+        for piece, (out, rows) in enumerate(zip(pieces, sizes)):
+            for z0 in range(2):
+                if piece == 0:
+                    place = h * (4 - 3 * b) + y * (2 + 2 * b) + z0 * (1 + b)
+                else:
+                    place = z0 * 4 + h * 2 + y
+                tiles = rows // TILE
+                value = acc[start : start + rows].reshape(tiles, TILE, acc.shape[1])
+                out[pl.ds(place * tiles, tiles)] = value
+                start += rows
+    largest = jnp.max(jnp.max(jnp.abs(acc), axis=0, keepdims=True), axis=1, keepdims=True)
+    largest = jnp.broadcast_to(largest, bound.shape)
+
+    @pl.when(h == 0)
+    def _():
+        bound[...] = largest
+        for out in pieces:
+            out[out.shape[0] - 1] = jnp.zeros(out.shape[1:], jnp.float32)
+
+    @pl.when(h > 0)
+    def _():
+        bound[...] = jnp.maximum(bound[...], largest)
+
+
+def half_pieces(ao_ints, vir_coef, core, sizes):
+    naos, aux = ao_ints.shape
+    virtuals = vir_coef.shape[1]
+    shapes = [pltpu.VMEM((8 * s // TILE + 1, TILE, virtuals), jnp.float32) for s in sizes]
+    shapes.append(pltpu.VMEM((8, virtuals), jnp.float32))
+    *pieces, bound = pl.pallas_call(
+        functools.partial(half_kernel, sizes),
+        grid_spec=pltpu.PrefetchScalarGridSpec(
+            num_scalar_prefetch=1,
+            grid=(2,),
+            in_specs=[
+                pl.BlockSpec((naos, virtuals), lambda i, b: (0, 0)),
+                pl.BlockSpec((naos, aux // 4), lambda i, b: (0, 2 * i + b[0])),
+            ],
+            out_specs=[pl.BlockSpec(memory_space=pltpu.VMEM)] * len(shapes),
+        ),
+        out_shape=shapes,
+        compiler_params=pltpu.CompilerParams(vmem_limit_bytes=6 * 2**20),
+        cost_estimate=pl.CostEstimate(flops=naos * aux * virtuals, bytes_accessed=naos * aux + 2 * aux * virtuals, transcendentals=0),
+    )(core.reshape(1).astype(jnp.int32), vir_coef, pltpu.with_memory_space_constraint(ao_ints, pltpu.HBM))
+    return pieces, bound[:1]
+
+
+def exponent_of(bound):
+    return jnp.ceil(jnp.log2(jnp.maximum(bound, 1e-30))) + 1.0
+
+
+def packed(value, exponent):
+    head = lax.broadcasted_iota(jnp.int32, value.shape, 0) == value.shape[0] - 1
+    return jnp.where(head, exponent, value * jnp.exp2(14.0 - exponent)).astype(jnp.float16)
+
+
+def exponent_in(message):
+    return message[-1, :1].astype(jnp.float32)
+
+
+def risen(level, messages):
+    for message in messages:
+        level = jnp.maximum(level, exponent_in(message))
+    return level + 1.0
+
+
+def joined(kept, message, start, tiles):
+    mine = lax.dynamic_slice_in_dim(kept, start, tiles + 1, 0)
+    theirs = lax.dynamic_slice_in_dim(message, start, tiles + 1, 0).astype(jnp.float32)
+    return mine + theirs * jnp.exp2(exponent_in(message) - 14.0)
+
+
+def row_start(place, rows, piece, sizes):
+    half = 2 * sum(sizes)
+    return pl.multiple_of(place // 2 * half + 2 * sum(sizes[:piece]) + place % 2 * rows, TILE)
+
+
+def blocks_of(sizes, places, array, first, count):
+    blocks, at = [], 0
+    for n in range(count):
+        for piece, rows in enumerate(sizes):
+            blocks.append((array, at, rows, row_start(places[first + n], rows, piece, sizes)))
+            at += rows
+    return blocks
+
+
+def gram_steps(sizes, scale, blocks, cols, out, buffers, sems):
+    rows = sizes[1]
+    copies = []
+    for ref, at, height, start in blocks:
+        for k in range(height // rows):
+            n = len(copies)
+            if n >= SLOTS:
+                copies[n - SLOTS].wait()
+            slot = n % SLOTS
+            buffers[slot] = contract_second(ref[at + k * rows : at + (k + 1) * rows], cols[...]) * scale
+            where = pl.ds(pl.multiple_of(start + k * rows, TILE), rows)
+            copies.append(pltpu.make_async_copy(buffers.at[slot], out.at[where, :], sems.at[slot]))
+            copies[n].start()
+    for copy in copies[-SLOTS:]:
+        copy.wait()
+
+
+def gram_first_kernel(sizes, scale, places, own, near, cols, naf, out, ahead, buffers, sems, naf_sems):
+    loads = []
+    for n, (_, at, rows, start) in enumerate(blocks_of(sizes, places, ahead, 1, 3)):
+        loads.append(pltpu.make_async_copy(naf.at[pl.ds(start, rows), :], ahead.at[pl.ds(at, rows), :], naf_sems.at[n]))
+        loads[n].start()
+    gram_steps(sizes, scale, blocks_of(sizes, places, own, 0, 1) + blocks_of(sizes, places, near, 1, 1), cols, out, buffers, sems)
+    for load in loads:
+        load.wait()
+
+
+def gram_rest_kernel(sizes, scale, places, far, cols, begun, out, buffers, sems):
+    gram_steps(sizes, scale, blocks_of(sizes, places, far, 2, 2), cols, out, buffers, sems)
+
+
+def gram_first(sizes, places, own, near, cols, naf_vectors):
+    in_vmem = pl.BlockSpec(memory_space=pltpu.VMEM)
+    in_hbm = pl.BlockSpec(memory_space=pl.ANY)
+    block, virtuals = own.shape
+    nnaf = naf_vectors.shape[1]
+    return pl.pallas_call(
+        functools.partial(gram_first_kernel, sizes, 1.0 / virtuals),
+        grid_spec=pltpu.PrefetchScalarGridSpec(
+            num_scalar_prefetch=1,
+            grid=(),
+            in_specs=[in_vmem, in_vmem, in_vmem, in_hbm],
+            out_specs=[in_hbm, in_vmem],
+            scratch_shapes=[
+                pltpu.VMEM((SLOTS, sizes[1], 2 * block), jnp.float32),
+                pltpu.SemaphoreType.DMA((SLOTS,)),
+                pltpu.SemaphoreType.DMA((6,)),
+            ],
+        ),
+        out_shape=[
+            jax.ShapeDtypeStruct((4 * block, 2 * block), jnp.float32),
+            pltpu.VMEM((3 * block, nnaf), jnp.bfloat16),
+        ],
+        compiler_params=pltpu.CompilerParams(vmem_limit_bytes=VMEM_LIMIT),
+        cost_estimate=pl.CostEstimate(flops=8 * block * block * virtuals, bytes_accessed=16 * block * block, transcendentals=0),
+    )(places, own, near, cols, pltpu.with_memory_space_constraint(naf_vectors, pltpu.HBM))
+
+
+def gram_rest(sizes, places, far, cols, begun):
+    in_vmem = pl.BlockSpec(memory_space=pltpu.VMEM)
+    in_hbm = pl.BlockSpec(memory_space=pl.ANY)
+    block, virtuals = far.shape[0] // 2, far.shape[1]
+    return pl.pallas_call(
+        functools.partial(gram_rest_kernel, sizes, 1.0 / virtuals),
+        grid_spec=pltpu.PrefetchScalarGridSpec(
+            num_scalar_prefetch=1,
+            grid=(),
+            in_specs=[in_vmem, in_vmem, in_hbm],
+            out_specs=in_hbm,
+            scratch_shapes=[pltpu.VMEM((SLOTS, sizes[1], 2 * block), jnp.float32), pltpu.SemaphoreType.DMA((SLOTS,))],
+        ),
+        out_shape=jax.ShapeDtypeStruct((4 * block, 2 * block), jnp.float32),
+        input_output_aliases={3: 0},
+        compiler_params=pltpu.CompilerParams(vmem_limit_bytes=VMEM_LIMIT),
+        cost_estimate=pl.CostEstimate(flops=8 * block * block * virtuals, bytes_accessed=16 * block * block, transcendentals=0),
+    )(places, far, cols, begun)
+
+
+def naf_first_kernel(sizes, places, own, naf, out, buffer, sems):
+    loads = []
+    for n, (_, at, rows, start) in enumerate(blocks_of(sizes, places, own, 0, 1)):
+        loads.append(pltpu.make_async_copy(naf.at[pl.ds(start, rows), :], buffer.at[pl.ds(at, rows), :], sems.at[n]))
+        loads[n].start()
+    for load in loads:
+        load.wait()
+    out[...] = contract_first(own[...], buffer[...])
+
+
+def naf_first(sizes, places, own, naf_vectors):
+    block, virtuals = own.shape
+    nnaf = naf_vectors.shape[1]
+    in_vmem = pl.BlockSpec(memory_space=pltpu.VMEM)
+    return pl.pallas_call(
+        functools.partial(naf_first_kernel, sizes),
+        grid_spec=pltpu.PrefetchScalarGridSpec(
+            num_scalar_prefetch=1,
+            grid=(),
+            in_specs=[in_vmem, pl.BlockSpec(memory_space=pl.ANY)],
+            out_specs=in_vmem,
+            scratch_shapes=[pltpu.VMEM((block, nnaf), jnp.bfloat16), pltpu.SemaphoreType.DMA((2,))],
+        ),
+        out_shape=pltpu.VMEM((virtuals, nnaf), jnp.float32),
+        compiler_params=pltpu.CompilerParams(vmem_limit_bytes=VMEM_LIMIT),
+        cost_estimate=pl.CostEstimate(flops=2 * block * nnaf * virtuals, bytes_accessed=2 * block * nnaf, transcendentals=0),
+    )(places, own, pltpu.with_memory_space_constraint(naf_vectors, pltpu.HBM))
+
+
+def naf_rest_kernel(near, far, naf, before, out):
+    block = near.shape[0]
+    out[...] = before[...] + contract_first(near[...], naf[:block]) + contract_first(far[...], naf[block:])
+
+
+def naf_rest(near, far, naf, before):
+    in_vmem = pl.BlockSpec(memory_space=pltpu.VMEM)
+    return pl.pallas_call(
+        naf_rest_kernel,
+        in_specs=[in_vmem] * 4,
+        out_specs=in_vmem,
+        out_shape=pltpu.VMEM(before.shape, jnp.float32),
+        compiler_params=pltpu.CompilerParams(vmem_limit_bytes=5 * 2**20),
+        cost_estimate=pl.CostEstimate(flops=2 * naf.shape[0] * before.size, bytes_accessed=0, transcendentals=0),
+    )(near, far, naf, before)
+
+
+def shards_4x8(ao_ints, vir_coef, naf_vectors):
+    virtuals = vir_coef.shape[1]
+    row_index = lax.axis_index("row")
+    col_index = lax.axis_index("col")
+    core, x = row_index % 2, row_index // 2
+    y, z0, z1 = col_index % 2, col_index // 2 % 2, col_index // 4
+    place = {X: x, Y: y, Z0: z0}
+    third = ao_ints.shape[1] // 48
+    sizes = (2 * third, third)
+
+    away, bound = half_pieces(ao_ints, vir_coef, 1 - core, sizes)
+    exponent = exponent_of(bound)
+    arrived = [flipped(packed(p, exponent), (1, 0), (1, 0)) for p in away]
+    kept, bound = half_pieces(ao_ints, vir_coef, core, sizes)
+    exponent = exponent_of(bound)
+
+    level = risen(exponent, arrived)
+    tiles = [8 * s // TILE for s in sizes]
+    for step in range(3):
+        sent, left = [], []
+        for piece, orders in enumerate(ORDERS):
+            tiles[piece] //= 2
+            own = jnp.where(core == 0, place[orders[0][step]], place[orders[1][step]])
+            other = joined(kept[piece], arrived[piece], (1 - own) * tiles[piece], tiles[piece])
+            out = packed(other, level)
+            sent.append(flipped(out, orders[0][step], orders[1][step]))
+            k, m, _ = lax.optimization_barrier((kept[piece], arrived[piece], out))
+            left.append(joined(k, m, own * tiles[piece], tiles[piece]))
+        kept, arrived = left, sent
+        level = risen(level, arrived)
+
+    last = [packed(joined(k, m, 0, n), level) for k, m, n in zip(kept, arrived, tiles)]
+    mine = jnp.concatenate([last[0][:-1], last[1]], axis=0)
+    theirs = flipped(mine, Z1, Z1)
+    near_place = jnp.where(core == 0, 2 * y + 1 - z0, 2 * (1 - y) + z0)
+    far_place = jnp.where(core == 0, 2 * (1 - y) + z0, 2 * y + 1 - z0)
+    places = jnp.stack([2 * y + z0, near_place, far_place, 2 * (1 - y) + 1 - z0]).astype(jnp.int32)
+    terms = [m[:-1].astype(jnp.float32) * jnp.exp2(exponent_in(m) - 14.0) for m in (mine, theirs)]
+    own = (terms[0] + terms[1]).astype(jnp.bfloat16).reshape(-1, virtuals)
+    block = sum(sizes)
+
+    def place_of(x, core, z1, z0, y):
+        return (x * 2 + core) * 8 + z1 * 4 + z0 * 2 + y
+
+    corners = [(a, b, c) for a in range(2) for b in range(2) for c in range(2)]
+    over_x = [(place_of(a, b, a, b, c), place_of(1 - a, b, a, b, c)) for a, b, c in corners]
+    over_x += [(place_of(a, b, a, 1 - b, c), place_of(1 - a, 1 - b, a, b, c)) for a, b, c in corners]
+    over_z = [(place_of(a, b, a, 1 - b, c), place_of(a, 1 - b, a, b, c)) for a, b, c in corners]
+    near = flipped(own, Z0, Y)
+    from_x = lax.ppermute(own, AXES, over_x)
+    from_z = lax.ppermute(own, AXES, over_z)
+    partial = naf_first(sizes, places, own, naf_vectors)
+    near, partial = lax.optimization_barrier((near, partial))
+    pair = jnp.concatenate([own, near], axis=0)
+    far = flipped(pair, Y, Z0)
+    from_x, from_z, _ = lax.optimization_barrier((from_x, from_z, pair))
+
+    part = jnp.where(x == z1, jnp.where(core == z0, own, from_z), from_x)
+    other_part = flipped(part, (1, 0), (1, 0))
+    halves = jnp.where(core == 0, part, other_part), jnp.where(core == 0, other_part, part)
+    cuts = (0, sizes[0]), (sizes[0], block)
+    columns = jnp.concatenate([half[a:b] for a, b in cuts for half in halves], axis=0)
+
+    gram, ahead = gram_first(sizes, places, own, near, columns, naf_vectors)
+    far, gram = lax.optimization_barrier((far, gram))
+    partial = naf_rest(near, far, ahead, partial)
+    partial = partial.reshape(4, virtuals // 4, -1)
+    share = lambda flip: lax.dynamic_index_in_dim(partial, row_index ^ flip, 0, keepdims=False)
+    parts = [flipped(share(flip), (flip, 0), (flip, 0)) for flip in (3, 2, 1)]
+    gram = gram_rest(sizes, places, far, columns, gram)
+    parts, gram = lax.optimization_barrier((parts, gram))
+    naf_ints = share(0) + parts[0] + parts[1] + parts[2]
+    return gram, naf_ints
+
+
 def solution(mesh):
     in_specs = (P(("row", "col"), None), P(("row", "col"), None), P("row", "col"))
     out_specs = (P("row", "col"), P("row", "col"))
-    return jax.shard_map(shards, mesh=mesh, in_specs=in_specs, out_specs=out_specs, check_vma=False)
+    plan = shards_4x8 if (mesh.shape["row"], mesh.shape["col"]) == (4, 8) else shards
+    return jax.shard_map(plan, mesh=mesh, in_specs=in_specs, out_specs=out_specs, check_vma=False)

time: 238 us -> 83.8 us (0.35)
  waiting for transfers between devices: 192 us -> 27.7 us
  matrix products: 28.9 us -> 0 us
  starting transfers between devices: 0.12 us -> 24.6 us
  Pallas kernels: 0 us -> 23.8 us
  between operations: 13.8 us -> 1.03 us
  other arithmetic: 1.6 us -> 5.39 us
    reduce_scatter x2 -> x0, waiting for transfers between devices: 130 us -> none  [the longest x1 125 us: shards(): lax.psum_scatter(contract_first(ao_ints, vir_coef), ('row', 'col'), scatt...]
    all_gather x1 -> x0, waiting for transfers between devices: 62.6 us -> none  [shards(): gathered = lax.all_gather(owned_rows, ('row', 'col'), axis=0, tiled=True)]
    dot_general x3 -> x0, matrix products: 28.9 us -> none  [the longest x1 15.7 us: contract_second(): lax.dot_general(lhs, rhs, (((1,), (1,)), ((), ())), preferred_element_typ...]
    ppermute x0 -> x17, waiting for transfers between devices: none -> 27.7 us  [the longest x15 27 us: flipped(): return lax.ppermute(value, AXES, pairs)]
    ppermute x0 -> x17, starting transfers between devices: none -> 24.6 us  [the longest x15 21.3 us: flipped(): return lax.ppermute(value, AXES, pairs)]
    pallas_call x0 -> x6, Pallas kernels: none -> 23.8 us  [the longest x1 7.79 us: gram_first(): pl.pallas_call(functools.partial(gram_first_kernel, sizes, 1.0 / virtuals...]
  transfers between devices with their start and end apart: 3 -> 17, of which waited for: 3 -> 10; matrix products, arithmetic and copies ran while one was open for 7% -> 3% of each run, Pallas kernels for 0% -> 24%
where the time goes in v2:
time: 83.8 us; the launch traced here: 83.3 us
  waiting for transfers between devices  27.7 us (33%)
  starting transfers between devices  24.6 us (29%)
  Pallas kernels  23.8 us (28%)
  other arithmetic  5.39 us (6%)
  between operations  1.03 us (1%)
  local copies, waits for them, and re-layouts  0.85 us (1%)
    ppermute x15, waiting for transfers between devices, flipped(): return lax.ppermute(value, AXES, pairs)  27 us
    ppermute x15, starting transfers between devices, flipped(): return lax.ppermute(value, AXES, pairs)  21.3 us
    pallas_call x1, Pallas kernels, gram_first(): pl.pallas_call(functools.partial(gram_first_kernel, sizes, 1.0 / virtuals...  7.79 us
    pallas_call x1, Pallas kernels, gram_rest(): pl.pallas_call(functools.partial(gram_rest_kernel, sizes, 1.0 / virtuals)...  6.34 us
    pallas_call x2, Pallas kernels, half_pieces(): pl.pallas_call(functools.partial(half_kernel, sizes), grid_spec=pltpu.Pre...  6.18 us
    convert_element_type x10, other arithmetic, packed(): jnp.where(head, exponent, value * jnp.exp2(14.0 - exponent))  3.6 us
    ppermute x1, starting transfers between devices, shards_4x8(): from_x = lax.ppermute(own, AXES, over_x)  2.63 us
    pallas_call x1, Pallas kernels, naf_first(): pl.pallas_call(functools.partial(naf_first_kernel, sizes), grid_spec=pltp...  2.44 us
  transfers between devices with their start and end apart: 17, of which 10 were waited for; matrix products, arithmetic and copies ran while one was open for 3% of the time, Pallas kernels for 24%

profile of v2, /device:TPU:0, one launch (start us, length us, event | category | flops | bytes accessed | tf_op | source)
XLA Modules:
  0.0 83.3 jit_solution(9992311340013971911)
XLA Ops:
  1.4 3.1 %shard_map.51 = (f32[321,16,128]{2,1,0:T(8,128)S(1)}, f32[161,16,128]{2,1,0:T(8,128)S(1)}, f32[8,128]{1,0:T(8,128)S(1)}) custom-call(s32[1]{0:T(128)} %bitcast.1.bits, bf16[160,128]{1,0:T(8,128)(2,1)S(1)} %copy-done, bf16[160,15360]{1,0:T(8,128)(2,1)} %ao.3), custom_call_target="tpu_custom_call" | custom-call | flops 314572800 | bytes 6389760 | tf_op jit(solution)/shard_map/pallas_call | solution.py:94
  4.6 1.1 %select_convert_fusion = f16[321,16,128]{2,1,0:T(8,128)(2,1)S(1)} fusion(f32[321,16,128]{2,1,0:T(8,128)S(1)} %get-tuple-element.34, f32[128]{0:T(128)S(1)} %get-tuple-element.70, f32[128]{0:T(128)S(1)} %bitcast.126, pred[321]{0:T(512)(128)(4,1)S(1)} %iota_compare_fusion), kind=kLoop, calls=%fused_computation | loop fusion | flops 1972224 | bytes 3945793 | tf_op jit(solution)/shard_map/convert_element_type | solution.py:118
  6.2 1.1 %select_convert_fusion.2 = f16[161,16,128]{2,1,0:T(8,128)(2,1)} fusion(f32[161,16,128]{2,1,0:T(8,128)S(1)} %get-tuple-element.35, f32[128]{0:T(128)S(1)} %get-tuple-element.70, f32[128]{0:T(128)S(1)} %bitcast.127, pred[161]{0:T(512)(128)(4,1)S(1)} %iota_compare_fusion.1), kind=kLoop, calls=%fused_computation.3 | loop fusion | flops 989184 | bytes 1979553 | tf_op jit(solution)/shard_map/convert_element_type | solution.py:118
  7.4 3.1 %shard_map.50 = (f32[321,16,128]{2,1,0:T(8,128)S(1)}, f32[161,16,128]{2,1,0:T(8,128)S(1)}, f32[8,128]{1,0:T(8,128)S(1)}) custom-call(s32[1]{0:T(128)} %bitcast.bits, bf16[160,128]{1,0:T(8,128)(2,1)S(1)} %copy-done.1, bf16[160,15360]{1,0:T(8,128)(2,1)} %ao.3), custom_call_target="tpu_custom_call" | custom-call | flops 314572800 | bytes 6389760 | tf_op jit(solution)/shard_map/pallas_call | solution.py:94
  10.8 3.1 %collective-permute-start.3 = (f16[81,16,128]{2,1,0:T(8,128)(2,1)S(1)}, f16[81,16,128]{2,1,0:T(8,128)(2,1)S(1)}, u32[]{:S(2)}, u32[]{:S(2)}) collective-permute-start(f16[81,16,128]{2,1,0:T(8,128)(2,1)S(1)} %select_convert_fusion.4), channel_id=1, source_target_pairs={{0,2},{1,3},{2,0},{3,1},{4,6},{5,7},{6,4},{7,5},{8,10},{9,11},{10,... | collective-permute-start | bytes 995336 | tf_op jit(solution)/shard_map/ppermute | solution.py:54
  14.2 1.6 %collective-permute-start.2 = (f16[161,16,128]{2,1,0:T(8,128)(2,1)S(1)}, f16[161,16,128]{2,1,0:T(8,128)(2,1)S(1)}, u32[]{:S(2)}, u32[]{:S(2)}) collective-permute-start(f16[161,16,128]{2,1,0:T(8,128)(2,1)S(1)} %select_convert_fusion.1), channel_id=1, source_target_pairs={{0,16},{1,17},{2,18},{3,19},{4,20},{5,21},{6,22},{7,23},{8,9},{9,8... | collective-permute-start | bytes 1978376 | tf_op jit(solution)/shard_map/ppermute | solution.py:54
  16.1 5.7 %collective-permute-done.3 = f16[81,16,128]{2,1,0:T(8,128)(2,1)S(1)} collective-permute-done((f16[81,16,128]{2,1,0:T(8,128)(2,1)S(1)}, f16[81,16,128]{2,1,0:T(8,128)(2,1)S(1)}, u32[]{:S(2)}, u32[]{:S(2)}) %collective-permute-start.3) | collective-permute-done | bytes 331808 | tf_op jit(solution)/shard_map/ppermute | solution.py:54
  21.8 3.1 %collective-permute-done.2 = f16[161,16,128]{2,1,0:T(8,128)(2,1)S(1)} collective-permute-done((f16[161,16,128]{2,1,0:T(8,128)(2,1)S(1)}, f16[161,16,128]{2,1,0:T(8,128)(2,1)S(1)}, u32[]{:S(2)}, u32[]{:S(2)}) %collective-permute-start.2) | collective-permute-done | bytes 659488 | tf_op jit(solution)/shard_map/ppermute | solution.py:54
  25.1 1.6 %collective-permute-start.5 = (f16[41,16,128]{2,1,0:T(8,128)(2,1)S(1)}, f16[41,16,128]{2,1,0:T(8,128)(2,1)S(1)}, u32[]{:S(2)}, u32[]{:S(2)}) collective-permute-start(f16[41,16,128]{2,1,0:T(8,128)(2,1)S(1)} %select_convert_fusion.6), channel_id=1, source_target_pairs={{0,16},{1,17},{2,18},{3,19},{4,20},{5,21},{6,22},{7,23},{8,24},{9,... | collective-permute-start | bytes 503816 | tf_op jit(solution)/shard_map/ppermute | solution.py:54
  26.9 1.6 %collective-permute-start.4 = (f16[81,16,128]{2,1,0:T(8,128)(2,1)S(1)}, f16[81,16,128]{2,1,0:T(8,128)(2,1)S(1)}, u32[]{:S(2)}, u32[]{:S(2)}) collective-permute-start(f16[81,16,128]{2,1,0:T(8,128)(2,1)S(1)} %select_convert_fusion.3), channel_id=1, source_target_pairs={{0,1},{1,0},{2,3},{3,2},{4,5},{5,4},{6,7},{7,6},{8,10},{9,11},{10,... | collective-permute-start | bytes 995336 | tf_op jit(solution)/shard_map/ppermute | solution.py:54
  28.6 1.9 %collective-permute-done.5 = f16[41,16,128]{2,1,0:T(8,128)(2,1)S(1)} collective-permute-done((f16[41,16,128]{2,1,0:T(8,128)(2,1)S(1)}, f16[41,16,128]{2,1,0:T(8,128)(2,1)S(1)}, u32[]{:S(2)}, u32[]{:S(2)}) %collective-permute-start.5) | collective-permute-done | bytes 167968 | tf_op jit(solution)/shard_map/ppermute | solution.py:54
  30.5 3.5 %collective-permute-done.4 = f16[81,16,128]{2,1,0:T(8,128)(2,1)S(1)} collective-permute-done((f16[81,16,128]{2,1,0:T(8,128)(2,1)S(1)}, f16[81,16,128]{2,1,0:T(8,128)(2,1)S(1)}, u32[]{:S(2)}, u32[]{:S(2)}) %collective-permute-start.4) | collective-permute-done | bytes 331808 | tf_op jit(solution)/shard_map/ppermute | solution.py:54
  34.2 1.6 %collective-permute-start.7 = (f16[21,16,128]{2,1,0:T(8,128)(2,1)S(1)}, f16[21,16,128]{2,1,0:T(8,128)(2,1)S(1)}, u32[]{:S(2)}, u32[]{:S(2)}) collective-permute-start(f16[21,16,128]{2,1,0:T(8,128)(2,1)S(1)} %select_convert_fusion.8), channel_id=1, source_target_pairs={{0,1},{1,0},{2,3},{3,2},{4,5},{5,4},{6,7},{7,6},{8,9},{9,8},{10,11... | collective-permute-start | bytes 258056 | tf_op jit(solution)/shard_map/ppermute | solution.py:54
  36.5 2.3 %collective-permute-done.7 = f16[21,16,128]{2,1,0:T(8,128)(2,1)S(1)} collective-permute-done((f16[21,16,128]{2,1,0:T(8,128)(2,1)S(1)}, f16[21,16,128]{2,1,0:T(8,128)(2,1)S(1)}, u32[]{:S(2)}, u32[]{:S(2)}) %collective-permute-start.7) | collective-permute-done | bytes 86048 | tf_op jit(solution)/shard_map/ppermute | solution.py:54
  38.7 2.6 %collective-permute-done.6 = f16[41,16,128]{2,1,0:T(8,128)(2,1)S(1)} collective-permute-done((f16[41,16,128]{2,1,0:T(8,128)(2,1)S(1)}, f16[41,16,128]{2,1,0:T(8,128)(2,1)S(1)}, u32[]{:S(2)}, u32[]{:S(2)}) %collective-permute-start.6) | collective-permute-done | bytes 167968 | tf_op jit(solution)/shard_map/ppermute | solution.py:54
  41.7 4.3 %collective-permute-start.8 = (f16[61,16,128]{2,1,0:T(8,128)(2,1)S(1)}, f16[61,16,128]{2,1,0:T(8,128)(2,1)S(1)}, u32[]{:S(2)}, u32[]{:S(2)}) collective-permute-start(f16[61,16,128]{2,1,0:T(8,128)(2,1)S(1)} %pad_maximum_fusion.2), channel_id=1, source_target_pairs={{0,4},{1,5},{2,6},{3,7},{4,0},{5,1},{6,2},{7,3},{8,12},{9,13},{10,... | collective-permute-start | bytes 749576 | tf_op jit(solution)/shard_map/ppermute | solution.py:54
  45.9 6.6 %collective-permute-done.8 = f16[61,16,128]{2,1,0:T(8,128)(2,1)S(1)} collective-permute-done((f16[61,16,128]{2,1,0:T(8,128)(2,1)S(1)}, f16[61,16,128]{2,1,0:T(8,128)(2,1)S(1)}, u32[]{:S(2)}, u32[]{:S(2)}) %collective-permute-start.8) | collective-permute-done | bytes 249888 | tf_op jit(solution)/shard_map/ppermute | solution.py:54
  53.5 2.6 %collective-permute-start.11 = (bf16[960,128]{1,0:T(8,128)(2,1)S(1)}, bf16[960,128]{1,0:T(8,128)(2,1)S(1)}, u32[]{:S(2)}, u32[]{:S(2)}) collective-permute-start(bf16[960,128]{1,0:T(8,128)(2,1)S(1)} %bitcast.111), channel_id=1, source_target_pairs={{0,16},{1,17},{10,26},{11,27},{20,4},{21,5},{30,14},{31,15},{2,24}... | collective-permute-start | bytes 737288 | tf_op jit(solution)/shard_map/ppermute | solution.py:324
  56.2 2.4 %shard_map.52.before = f32[128,896]{1,0:T(8,128)S(1)} custom-call(s32[4]{0:T(128)S(1)} %pad_add_fusion.places, bf16[960,128]{1,0:T(8,128)(2,1)S(1)} %bitcast.112, bf16[3840,896]{1,0:T(8,128)(2,1)} %naf.3), custom_call_target="tpu_custom_call" | custom-call | flops 220200960 | bytes 1720320 | tf_op jit(solution)/shard_map/pallas_call | solution.py:243
  59.7 3.0 %collective-permute-start.13 = (bf16[960,128]{1,0:T(8,128)(2,1)S(1)}, bf16[960,128]{1,0:T(8,128)(2,1)S(1)}, u32[]{:S(2)}, u32[]{:S(2)}) collective-permute-start(bf16[960,128]{1,0:T(8,128)(2,1)S(1)} %select_select_fusion), channel_id=1, source_target_pairs={{0,8},{1,9},{2,10},{3,11},{4,12},{5,13},{6,14},{7,15},{8,0},{9,1},... | collective-permute-start | bytes 737288 | tf_op jit(solution)/shard_map/ppermute | solution.py:54
  64.0 7.8 %shard_map.53 = (f32[3840,1920]{1,0:T(8,128)}, bf16[2880,896]{1,0:T(8,128)(2,1)S(1)}) custom-call(s32[4]{0:T(128)S(1)} %pad_add_fusion.places, bf16[960,128]{1,0:T(8,128)(2,1)S(1)} %bitcast.114, bf16[960,128]{1,0:T(8,128)(2,1)S(1)} %collective-permute-done.9.near, bf16[1920,128]{1,0:T(8,128)(2,1)S(1)} %pad_maximum_fusion.1.cols, bf16[3840,896]{1,0:T(8,128)(2,1)} %naf.3), custom_call_target="tpu_custom_call" | custom-call | flops 943718400 | bytes 14745600 | tf_op jit(solution)/shard_map/pallas_call | solution.py:187
  71.8 1.0 %shard_map.54 = f32[128,896]{1,0:T(8,128)S(1)} custom-call(bf16[960,128]{1,0:T(8,128)(2,1)S(1)} %collective-permute-done.9.near, bf16[1920,128]{1,0:T(8,128)(2,1)S(1)} %collective-permute-done.10.far, bf16[2880,896]{1,0:T(8,128)(2,1)S(1)} %get-tuple-element.55.naf, f32[128,896]{1,0:T(8,128)S(1)} %shard_map.52.before), custom_call_target="tpu_custom_call" | custom-call | flops 660602880 | tf_op jit(solution)/shard_map/pallas_call | solution.py:265
  73.4 2.9 %collective-permute-start.15 = (f32[32,896]{1,0:T(8,128)S(1)}, f32[32,896]{1,0:T(8,128)S(1)}, u32[]{:S(2)}, u32[]{:S(2)}) collective-permute-start(f32[32,896]{1,0:T(8,128)S(1)} %get-tuple-element.75), channel_id=1, source_target_pairs={{0,16},{1,17},{2,18},{3,19},{4,20},{5,21},{6,22},{7,23},{8,24},{9,... | collective-permute-start | bytes 344072 | tf_op jit(solution)/shard_map/ppermute | solution.py:54
  76.2 6.3 %shard_map.55 = f32[3840,1920]{1,0:T(8,128)} custom-call(s32[4]{0:T(128)S(1)} %pad_add_fusion.places, bf16[1920,128]{1,0:T(8,128)(2,1)S(1)} %collective-permute-done.10.far, bf16[1920,128]{1,0:T(8,128)(2,1)S(1)} %pad_maximum_fusion.1.cols, f32[3840,1920]{1,0:T(8,128)} %get-tuple-element.57.begun), custom_call_target="tpu_custom_call", output_to_operand_aliasing={{}: (3, {})} | custom-call | flops 943718400 | bytes 14745600 | tf_op jit(solution)/shard_map/pallas_call | solution.py:213
  (74 shorter events, 8.4 us)
Async XLA Ops:
  0.7 0.8 copy-start
  5.7 1.7 %copy-start.1 = (bf16[160,128]{1,0:T(8,128)(2,1)S(1)}, bf16[160,128]{1,0:T(8,128)(2,1)}, u32[]{:S(2)}) copy-start(bf16[160,128]{1,0:T(8,128)(2,1)} %vir.3) | copy-start | bytes 122884
  5.7 4.8 %collective-permute-start = (f16[321,16,128]{2,1,0:T(8,128)(2,1)S(1)}, f16[321,16,128]{2,1,0:T(8,128)(2,1)S(1)}, u32[]{:S(2)}, u32[]{:S(2)}) collective-permute-start(f16[321,16,128]{2,1,0:T(8,128)(2,1)S(1)} %select_convert_fusion), channel_id=1, source_target_pairs={{0,8},{1,9},{2,10},{3,11},{4,12},{5,13},{6,14},{7,15},{8,0},{9,1},... | collective-permute-start | bytes 3944456 | tf_op jit(solution)/shard_map/ppermute | solution.py:54
  7.3 3.2 %collective-permute-start.1 = (f16[161,16,128]{2,1,0:T(8,128)(2,1)}, f16[161,16,128]{2,1,0:T(8,128)(2,1)S(1)}, u32[]{:S(2)}, u32[]{:S(2)}) collective-permute-start(f16[161,16,128]{2,1,0:T(8,128)(2,1)} %select_convert_fusion.2), channel_id=1, source_target_pairs={{0,8},{1,9},{2,10},{3,11},{4,12},{5,13},{6,14},{7,15},{8,0},{9,1},... | collective-permute-start | bytes 1978376 | tf_op jit(solution)/shard_map/ppermute | solution.py:54
  10.8 11.1 %collective-permute-start.3 = (f16[81,16,128]{2,1,0:T(8,128)(2,1)S(1)}, f16[81,16,128]{2,1,0:T(8,128)(2,1)S(1)}, u32[]{:S(2)}, u32[]{:S(2)}) collective-permute-start(f16[81,16,128]{2,1,0:T(8,128)(2,1)S(1)} %select_convert_fusion.4), channel_id=1, source_target_pairs={{0,2},{1,3},{2,0},{3,1},{4,6},{5,7},{6,4},{7,5},{8,10},{9,11},{10,... | collective-permute-start | bytes 995336 | tf_op jit(solution)/shard_map/ppermute | solution.py:54
  14.2 10.7 %collective-permute-start.2 = (f16[161,16,128]{2,1,0:T(8,128)(2,1)S(1)}, f16[161,16,128]{2,1,0:T(8,128)(2,1)S(1)}, u32[]{:S(2)}, u32[]{:S(2)}) collective-permute-start(f16[161,16,128]{2,1,0:T(8,128)(2,1)S(1)} %select_convert_fusion.1), channel_id=1, source_target_pairs={{0,16},{1,17},{2,18},{3,19},{4,20},{5,21},{6,22},{7,23},{8,9},{9,8... | collective-permute-start | bytes 1978376 | tf_op jit(solution)/shard_map/ppermute | solution.py:54
  25.1 5.4 %collective-permute-start.5 = (f16[41,16,128]{2,1,0:T(8,128)(2,1)S(1)}, f16[41,16,128]{2,1,0:T(8,128)(2,1)S(1)}, u32[]{:S(2)}, u32[]{:S(2)}) collective-permute-start(f16[41,16,128]{2,1,0:T(8,128)(2,1)S(1)} %select_convert_fusion.6), channel_id=1, source_target_pairs={{0,16},{1,17},{2,18},{3,19},{4,20},{5,21},{6,22},{7,23},{8,24},{9,... | collective-permute-start | bytes 503816 | tf_op jit(solution)/shard_map/ppermute | solution.py:54
  26.9 7.2 %collective-permute-start.4 = (f16[81,16,128]{2,1,0:T(8,128)(2,1)S(1)}, f16[81,16,128]{2,1,0:T(8,128)(2,1)S(1)}, u32[]{:S(2)}, u32[]{:S(2)}) collective-permute-start(f16[81,16,128]{2,1,0:T(8,128)(2,1)S(1)} %select_convert_fusion.3), channel_id=1, source_target_pairs={{0,1},{1,0},{2,3},{3,2},{4,5},{5,4},{6,7},{7,6},{8,10},{9,11},{10,... | collective-permute-start | bytes 995336 | tf_op jit(solution)/shard_map/ppermute | solution.py:54
  34.2 4.6 %collective-permute-start.7 = (f16[21,16,128]{2,1,0:T(8,128)(2,1)S(1)}, f16[21,16,128]{2,1,0:T(8,128)(2,1)S(1)}, u32[]{:S(2)}, u32[]{:S(2)}) collective-permute-start(f16[21,16,128]{2,1,0:T(8,128)(2,1)S(1)} %select_convert_fusion.8), channel_id=1, source_target_pairs={{0,1},{1,0},{2,3},{3,2},{4,5},{5,4},{6,7},{7,6},{8,9},{9,8},{10,11... | collective-permute-start | bytes 258056 | tf_op jit(solution)/shard_map/ppermute | solution.py:54
  35.9 5.4 %collective-permute-start.6 = (f16[41,16,128]{2,1,0:T(8,128)(2,1)S(1)}, f16[41,16,128]{2,1,0:T(8,128)(2,1)S(1)}, u32[]{:S(2)}, u32[]{:S(2)}) collective-permute-start(f16[41,16,128]{2,1,0:T(8,128)(2,1)S(1)} %select_convert_fusion.5), channel_id=1, source_target_pairs={{0,2},{1,3},{2,0},{3,1},{4,6},{5,7},{6,4},{7,5},{8,24},{9,25},{10,... | collective-permute-start | bytes 503816 | tf_op jit(solution)/shard_map/ppermute | solution.py:54
  41.7 10.8 %collective-permute-start.8 = (f16[61,16,128]{2,1,0:T(8,128)(2,1)S(1)}, f16[61,16,128]{2,1,0:T(8,128)(2,1)S(1)}, u32[]{:S(2)}, u32[]{:S(2)}) collective-permute-start(f16[61,16,128]{2,1,0:T(8,128)(2,1)S(1)} %pad_maximum_fusion.2), channel_id=1, source_target_pairs={{0,4},{1,5},{2,6},{3,7},{4,0},{5,1},{6,2},{7,3},{8,12},{9,13},{10,... | collective-permute-start | bytes 749576 | tf_op jit(solution)/shard_map/ppermute | solution.py:54
  52.6 6.3 %collective-permute-start.9 = (bf16[960,128]{1,0:T(8,128)(2,1)S(1)}, bf16[960,128]{1,0:T(8,128)(2,1)S(1)}, u32[]{:S(2)}, u32[]{:S(2)}) collective-permute-start(bf16[960,128]{1,0:T(8,128)(2,1)S(1)} %bitcast.109), channel_id=1, source_target_pairs={{0,2},{1,3},{2,0},{3,1},{4,6},{5,7},{6,4},{7,5},{8,9},{9,8},{10,11... | collective-permute-start | bytes 737288 | tf_op jit(solution)/shard_map/ppermute | solution.py:54
  52.8 6.1 %collective-permute-start.12 = (bf16[960,128]{1,0:T(8,128)(2,1)S(1)}, bf16[960,128]{1,0:T(8,128)(2,1)S(1)}, u32[]{:S(2)}, u32[]{:S(2)}) collective-permute-start(bf16[960,128]{1,0:T(8,128)(2,1)S(1)} %bitcast.110), channel_id=1, source_target_pairs={{2,8},{3,9},{8,2},{9,3},{22,28},{23,29},{28,22},{29,23}} | collective-permute-start | bytes 737288 | tf_op jit(solution)/shard_map/ppermute | solution.py:325
  53.5 6.1 %collective-permute-start.11 = (bf16[960,128]{1,0:T(8,128)(2,1)S(1)}, bf16[960,128]{1,0:T(8,128)(2,1)S(1)}, u32[]{:S(2)}, u32[]{:S(2)}) collective-permute-start(bf16[960,128]{1,0:T(8,128)(2,1)S(1)} %bitcast.111), channel_id=1, source_target_pairs={{0,16},{1,17},{10,26},{11,27},{20,4},{21,5},{30,14},{31,15},{2,24}... | collective-permute-start | bytes 737288 | tf_op jit(solution)/shard_map/ppermute | solution.py:324
  59.7 4.1 %collective-permute-start.13 = (bf16[960,128]{1,0:T(8,128)(2,1)S(1)}, bf16[960,128]{1,0:T(8,128)(2,1)S(1)}, u32[]{:S(2)}, u32[]{:S(2)}) collective-permute-start(bf16[960,128]{1,0:T(8,128)(2,1)S(1)} %select_select_fusion), channel_id=1, source_target_pairs={{0,8},{1,9},{2,10},{3,11},{4,12},{5,13},{6,14},{7,15},{8,0},{9,1},... | collective-permute-start | bytes 737288 | tf_op jit(solution)/shard_map/ppermute | solution.py:54
  62.7 9.1 %collective-permute-start.10 = (bf16[1920,128]{1,0:T(8,128)(2,1)S(1)}, bf16[1920,128]{1,0:T(8,128)(2,1)S(1)}, u32[]{:S(2)}, u32[]{:S(2)}) collective-permute-start(bf16[1920,128]{1,0:T(8,128)(2,1)S(1)} %pad_maximum_fusion), channel_id=1, source_target_pairs={{0,1},{1,0},{2,3},{3,2},{4,5},{5,4},{6,7},{7,6},{8,10},{9,11},{10,... | collective-permute-start | bytes 1474568 | tf_op jit(solution)/shard_map/ppermute | solution.py:54
  72.9 9.7 %collective-permute-start.16 = (f32[32,896]{1,0:T(8,128)S(1)}, f32[32,896]{1,0:T(8,128)S(1)}, u32[]{:S(2)}, u32[]{:S(2)}) collective-permute-start(f32[32,896]{1,0:T(8,128)S(1)} %get-tuple-element.74), channel_id=1, source_target_pairs={{0,8},{1,9},{2,10},{3,11},{4,12},{5,13},{6,14},{7,15},{8,0},{9,1},... | collective-permute-start | bytes 344072 | tf_op jit(solution)/shard_map/ppermute | solution.py:54
  73.4 9.2 %collective-permute-start.15 = (f32[32,896]{1,0:T(8,128)S(1)}, f32[32,896]{1,0:T(8,128)S(1)}, u32[]{:S(2)}, u32[]{:S(2)}) collective-permute-start(f32[32,896]{1,0:T(8,128)S(1)} %get-tuple-element.75), channel_id=1, source_target_pairs={{0,16},{1,17},{2,18},{3,19},{4,20},{5,21},{6,22},{7,23},{8,24},{9,... | collective-permute-start | bytes 344072 | tf_op jit(solution)/shard_map/ppermute | solution.py:54
  76.2 6.4 %collective-permute-start.14 = (f32[32,896]{1,0:T(8,128)S(1)}, f32[32,896]{1,0:T(8,128)S(1)}, u32[]{:S(2)}, u32[]{:S(2)}) collective-permute-start(f32[32,896]{1,0:T(8,128)S(1)} %get-tuple-element.76), channel_id=1, source_target_pairs={{0,24},{1,25},{2,26},{3,27},{4,28},{5,29},{6,30},{7,31},{8,16},{9,... | collective-permute-start | bytes 344072 | tf_op jit(solution)/shard_map/ppermute | solution.py:54

commit v3 on v2

v3 whole, which is shorter than its diff:
```python
import functools

import jax
import jax.numpy as jnp
from jax import lax
from jax.experimental import pallas as pl
from jax.experimental.pallas import tpu as pltpu
from jax.sharding import PartitionSpec as P

AXES = ("row", "col")
TILE = 16
SLOTS = 3
VMEM_LIMIT = 11 * 2**20


def contract_first(lhs, rhs):
    return lax.dot_general(lhs, rhs, (((0,), (0,)), ((), ())), preferred_element_type=jnp.float32)


def contract_second(lhs, rhs):
    return lax.dot_general(lhs, rhs, (((1,), (1,)), ((), ())), preferred_element_type=jnp.float32)


def shards(ao_ints, vir_coef, naf_vectors):
    n_row = lax.axis_size("row")
    n_col = lax.axis_size("col")
    virtuals = vir_coef.shape[1]
    aux_total = ao_ints.shape[1]
    row_width = aux_total // n_row
    col_width = aux_total // n_col
    row_index = lax.axis_index("row")
    col_index = lax.axis_index("col")
    owned_rows = lax.psum_scatter(
        contract_first(ao_ints, vir_coef), ("row", "col"), scatter_dimension=0, tiled=True
    ).astype(jnp.bfloat16)
    gathered = lax.all_gather(owned_rows, ("row", "col"), axis=0, tiled=True)
    panel_rows = lax.dynamic_slice_in_dim(gathered, row_index * row_width, row_width, 0)
    panel_cols = lax.dynamic_slice_in_dim(gathered, col_index * col_width, col_width, 0)
    tile_sum = contract_second(panel_rows, panel_cols)
    projection = contract_first(panel_rows, naf_vectors)
    naf_ints = lax.psum_scatter(projection, "row", scatter_dimension=0, tiled=True)
    return (tile_sum * (1.0 / virtuals), naf_ints)


X, Y, Z0, Z1 = (2, 0), (0, 1), (0, 2), (0, 4)
ORDERS = (((Y, Z0, X), (X, Y, Z0)), ((Z0, X, Y), (Z0, X, Y)))


def flipped(value, on_core0, on_core1):
    pairs = []
    for r in range(4):
        over_row, over_col = on_core1 if r % 2 else on_core0
        pairs += [(r * 8 + c, (r ^ over_row) * 8 + (c ^ over_col)) for c in range(8)]
    return lax.ppermute(value, AXES, pairs)


def half_blocks(sizes, bits, vir, ao):
    x, core = pl.program_id(0), bits[0]
    acc = contract_first(ao[...], vir[...])
    half = acc.shape[0] // 2
    blocks = []
    for y in range(2):
        start = y * half
        for piece, rows in enumerate(sizes):
            for z0 in range(2):
                value = acc[start : start + rows].reshape(rows // TILE, TILE, acc.shape[1])
                blocks.append((piece, place_in(piece, core, x, y, z0) * (rows // TILE), value))
                start += rows
    return blocks, jnp.max(jnp.max(jnp.abs(acc), axis=0, keepdims=True), axis=1, keepdims=True)


def place_in(piece, core, x, y, z0):
    bits = {X: x, Y: y, Z0: z0}
    on_core0, on_core1 = (sum(bits[d] * 2 ** (2 - n) for n, d in enumerate(order)) for order in ORDERS[piece])
    return jnp.where(core == 0, on_core0, on_core1)


def half_first_kernel(sizes, bits, vir, ao, *refs):
    *pieces, bound = refs
    blocks, largest = half_blocks(sizes, bits, vir, ao)

    @pl.when(pl.program_id(0) == 0)
    def _():
        bound[...] = jnp.broadcast_to(largest, bound.shape)
        for piece, at, value in blocks:
            pieces[piece][pl.ds(at, value.shape[0])] = value

    @pl.when(pl.program_id(0) == 1)
    def _():
        exponent = exponent_of(jnp.maximum(bound[...], largest))
        scale = jnp.exp2(14.0 - exponent)[None, :1]
        for piece, at, value in blocks:
            out, tiles = pieces[piece], value.shape[0]
            out[pl.ds(at, tiles)] = value * scale
            before = at - place_in(piece, bits[0], 1, 0, 0) * tiles
            earlier = out[pl.ds(before, tiles)]
            out[pl.ds(before, tiles)] = earlier * scale
        for out in pieces:
            out[out.shape[0] - 1] = jnp.concatenate([exponent, exponent], axis=0)


def half_rest_kernel(sizes, bits, vir, ao, *refs):
    *pieces, bound = refs
    blocks, largest = half_blocks(sizes, bits, vir, ao)
    for piece, at, value in blocks:
        pieces[piece][pl.ds(at, value.shape[0])] = value

    @pl.when(pl.program_id(0) == 0)
    def _():
        bound[...] = jnp.broadcast_to(largest, bound.shape)
        for out in pieces:
            out[out.shape[0] - 1] = jnp.zeros(out.shape[1:], jnp.float32)

    @pl.when(pl.program_id(0) == 1)
    def _():
        bound[...] = exponent_of(jnp.maximum(bound[...], largest))


def half_pieces(ao_ints, vir_coef, core, sizes):
    naos, aux = ao_ints.shape
    virtuals = vir_coef.shape[1]
    panel = aux // 4
    shapes = [pltpu.VMEM((8 * s // TILE + 1, TILE, virtuals), jnp.float32) for s in sizes]
    bound = pltpu.VMEM((8, virtuals), jnp.float32)
    in_vmem = pl.BlockSpec(memory_space=pltpu.VMEM)
    cost = pl.CostEstimate(flops=naos * aux * virtuals, bytes_accessed=naos * aux + 2 * aux * virtuals, transcendentals=0)
    limit = pltpu.CompilerParams(vmem_limit_bytes=5 * 2**20)
    source = pltpu.with_memory_space_constraint(ao_ints, pltpu.HBM)
    away = pl.pallas_call(
        functools.partial(half_first_kernel, sizes),
        grid_spec=pltpu.PrefetchScalarGridSpec(
            num_scalar_prefetch=1,
            grid=(2,),
            in_specs=[
                pl.BlockSpec((naos, virtuals), lambda i, b: (0, 0)),
                pl.BlockSpec((naos, panel), lambda i, b: (0, 2 * i + b[0])),
            ],
            out_specs=[in_vmem] * len(shapes),
            scratch_shapes=[bound],
        ),
        out_shape=shapes,
        compiler_params=limit,
        cost_estimate=cost,
    )((1 - core).reshape(1).astype(jnp.int32), pltpu.with_memory_space_constraint(vir_coef, pltpu.HBM), source)
    def rest():
        return pl.pallas_call(
            functools.partial(half_rest_kernel, sizes),
            grid_spec=pltpu.PrefetchScalarGridSpec(
                num_scalar_prefetch=1,
                grid=(2,),
                in_specs=[
                    pl.BlockSpec((naos, virtuals), lambda i, b: (0, 0)),
                    pl.BlockSpec((naos, panel), lambda i, b: (0, 2 * i + b[0])),
                ],
                out_specs=[in_vmem] * (len(shapes) + 1),
            ),
            out_shape=shapes + [bound],
            compiler_params=limit,
            cost_estimate=cost,
        )(core.reshape(1).astype(jnp.int32), pltpu.with_memory_space_constraint(vir_coef, pltpu.HBM), source)

    return away, rest


def exponent_of(bound):
    return jnp.ceil(jnp.log2(jnp.maximum(bound, 1e-30))) + 1.0


def packed(value, exponent):
    head = lax.broadcasted_iota(jnp.int32, value.shape, 0) == value.shape[0] - 1
    return jnp.where(head, exponent, value * jnp.exp2(14.0 - exponent)).astype(jnp.float16)


def exponent_in(message):
    return message[-1, :1].astype(jnp.float32)


def risen(level, messages):
    for message in messages:
        level = jnp.maximum(level, exponent_in(message))
    return level + 1.0


def joined(kept, message, start, tiles):
    mine = lax.dynamic_slice_in_dim(kept, start, tiles + 1, 0)
    theirs = lax.dynamic_slice_in_dim(message, start, tiles + 1, 0).astype(jnp.float32)
    return mine + theirs * jnp.exp2(exponent_in(message) - 14.0)


def row_start(place, rows, piece, sizes):
    half = 2 * sum(sizes)
    return pl.multiple_of(place // 2 * half + 2 * sum(sizes[:piece]) + place % 2 * rows, TILE)


def blocks_of(sizes, places, array, first, count):
    blocks, at = [], 0
    for n in range(count):
        for piece, rows in enumerate(sizes):
            blocks.append((array, at, rows, row_start(places[first + n], rows, piece, sizes)))
            at += rows
    return blocks


def steps_of(sizes):
    cuts = []
    for rows in sizes:
        count = max(1, round(3 * rows / sum(sizes)))
        edges = [rows * n // count // TILE * TILE for n in range(count)] + [rows]
        cuts.append(tuple(zip(edges[:-1], edges[1:])))
    return cuts


def step_rows(sizes):
    return max(b - a for cuts in steps_of(sizes) for a, b in cuts)


def gram_steps(sizes, scale, blocks, cols, out, buffers, sems):
    copies = []
    cuts = steps_of(sizes)
    for ref, at, height, start in blocks:
        for a, b in cuts[sizes.index(height)]:
            n = len(copies)
            if n >= SLOTS:
                copies[n - SLOTS].wait()
            slot = n % SLOTS
            buffers[slot, : b - a] = contract_second(ref[at + a : at + b], cols[...]) * scale
            where = pl.ds(pl.multiple_of(start + a, TILE), b - a)
            copies.append(pltpu.make_async_copy(buffers.at[slot, pl.ds(0, b - a)], out.at[where, :], sems.at[slot]))
            copies[n].start()
    for copy in copies[-SLOTS:]:
        copy.wait()


def gram_first_kernel(sizes, scale, places, own, near, cols, out, buffers, sems):
    blocks = blocks_of(sizes, places, own, 0, 1) + blocks_of(sizes, places, near, 1, 1)
    gram_steps(sizes, scale, blocks, cols, out, buffers, sems)


def gram_rest_kernel(sizes, scale, places, far, cols, begun, out, buffers, sems):
    gram_steps(sizes, scale, blocks_of(sizes, places, far, 2, 2), cols, out, buffers, sems)


def gram_first(sizes, places, own, near, cols):
    in_vmem = pl.BlockSpec(memory_space=pltpu.VMEM)
    block, virtuals = own.shape
    return pl.pallas_call(
        functools.partial(gram_first_kernel, sizes, 1.0 / virtuals),
        grid_spec=pltpu.PrefetchScalarGridSpec(
            num_scalar_prefetch=1,
            grid=(),
            in_specs=[in_vmem] * 3,
            out_specs=pl.BlockSpec(memory_space=pl.ANY),
            scratch_shapes=[pltpu.VMEM((SLOTS, step_rows(sizes), 2 * block), jnp.float32), pltpu.SemaphoreType.DMA((SLOTS,))],
        ),
        out_shape=jax.ShapeDtypeStruct((4 * block, 2 * block), jnp.float32),
        compiler_params=pltpu.CompilerParams(vmem_limit_bytes=VMEM_LIMIT),
        cost_estimate=pl.CostEstimate(flops=8 * block * block * virtuals, bytes_accessed=16 * block * block, transcendentals=0),
    )(places, own, near, cols)


def gram_rest(sizes, places, far, cols, begun):
    in_vmem = pl.BlockSpec(memory_space=pltpu.VMEM)
    in_hbm = pl.BlockSpec(memory_space=pl.ANY)
    block, virtuals = far.shape[0] // 2, far.shape[1]
    return pl.pallas_call(
        functools.partial(gram_rest_kernel, sizes, 1.0 / virtuals),
        grid_spec=pltpu.PrefetchScalarGridSpec(
            num_scalar_prefetch=1,
            grid=(),
            in_specs=[in_vmem, in_vmem, in_hbm],
            out_specs=in_hbm,
            scratch_shapes=[pltpu.VMEM((SLOTS, step_rows(sizes), 2 * block), jnp.float32), pltpu.SemaphoreType.DMA((SLOTS,))],
        ),
        out_shape=jax.ShapeDtypeStruct((4 * block, 2 * block), jnp.float32),
        input_output_aliases={3: 0},
        compiler_params=pltpu.CompilerParams(vmem_limit_bytes=VMEM_LIMIT),
        cost_estimate=pl.CostEstimate(flops=8 * block * block * virtuals, bytes_accessed=16 * block * block, transcendentals=0),
    )(places, far, cols, begun)


def naf_kernel(sizes, places, own, near, far, naf, out, panel):
    blocks = blocks_of(sizes, places, own, 0, 1) + blocks_of(sizes, places, near, 1, 1)
    for ref, at, rows, row in blocks + blocks_of(sizes, places, far, 2, 2):
        panel[pl.ds(row, rows), :] = ref[at : at + rows]
    out[...] = contract_first(panel[...], naf[...])


def project(sizes, places, own, near, far, naf_vectors):
    virtuals = own.shape[1]
    rows, nnaf = naf_vectors.shape
    in_vmem = pl.BlockSpec(memory_space=pltpu.VMEM)
    return pl.pallas_call(
        functools.partial(naf_kernel, sizes),
        grid_spec=pltpu.PrefetchScalarGridSpec(
            num_scalar_prefetch=1,
            grid=(),
            in_specs=[in_vmem] * 4,
            out_specs=in_vmem,
            scratch_shapes=[pltpu.VMEM((rows, virtuals), jnp.bfloat16)],
        ),
        out_shape=pltpu.VMEM((virtuals, nnaf), jnp.float32),
        compiler_params=pltpu.CompilerParams(vmem_limit_bytes=10 * 2**20),
        cost_estimate=pl.CostEstimate(flops=2 * rows * nnaf * virtuals, bytes_accessed=2 * rows * nnaf, transcendentals=0),
    )(places, own, near, far, naf_vectors)


def shards_4x8(ao_ints, vir_coef, naf_vectors):
    virtuals = vir_coef.shape[1]
    row_index = lax.axis_index("row")
    col_index = lax.axis_index("col")
    core, x = row_index % 2, row_index // 2
    y, z0, z1 = col_index % 2, col_index // 2 % 2, col_index // 4
    place = {X: x, Y: y, Z0: z0}
    half = ao_ints.shape[1] // 16
    sizes = (592 * half // 960 // TILE * TILE,)
    sizes += (half - sizes[0],)

    away, kept_pieces = half_pieces(ao_ints, vir_coef, core, sizes)
    arrived = [flipped(p.astype(jnp.float16), (1, 0), (1, 0)) for p in away[::-1]][::-1]
    *kept, exponent = kept_pieces()
    exponent = exponent[:1]

    level = risen(exponent, arrived)
    tiles = [8 * s // TILE for s in sizes]
    for step in range(3):
        sent, left = [], []
        for piece, orders in enumerate(ORDERS):
            tiles[piece] //= 2
            own = jnp.where(core == 0, place[orders[0][step]], place[orders[1][step]])
            other = joined(kept[piece], arrived[piece], (1 - own) * tiles[piece], tiles[piece])
            out = packed(other, level)
            if piece == 0:
                kept[1], arrived[1], out = lax.optimization_barrier((kept[1], arrived[1], out))
            sent.append(flipped(out, orders[0][step], orders[1][step]))
            k, m, _ = lax.optimization_barrier((kept[piece], arrived[piece], out))
            left.append(joined(k, m, own * tiles[piece], tiles[piece]))
        kept, arrived = left, sent
        level = risen(level, arrived)

    last = [packed(joined(k, m, 0, n), level) for k, m, n in zip(kept, arrived, tiles)]
    mine = jnp.concatenate([last[0][:-1], last[1]], axis=0)
    theirs = flipped(mine, Z1, Z1)
    near_place = jnp.where(core == 0, 2 * y + 1 - z0, 2 * (1 - y) + z0)
    far_place = jnp.where(core == 0, 2 * (1 - y) + z0, 2 * y + 1 - z0)
    places = jnp.stack([2 * y + z0, near_place, far_place, 2 * (1 - y) + 1 - z0]).astype(jnp.int32)
    terms = [m[:-1].astype(jnp.float32) * jnp.exp2(exponent_in(m) - 14.0) for m in (mine, theirs)]
    own = (terms[0] + terms[1]).astype(jnp.bfloat16).reshape(-1, virtuals)
    block = sum(sizes)

    def place_of(x, core, z1, z0, y):
        return (x * 2 + core) * 8 + z1 * 4 + z0 * 2 + y

    corners = [(a, b, c) for a in range(2) for b in range(2) for c in range(2)]
    over_x = [(place_of(a, b, a, b, c), place_of(1 - a, b, a, b, c)) for a, b, c in corners]
    over_x += [(place_of(a, b, a, 1 - b, c), place_of(1 - a, 1 - b, a, b, c)) for a, b, c in corners]
    over_z = [(place_of(a, b, a, 1 - b, c), place_of(a, 1 - b, a, b, c)) for a, b, c in corners]
    near = flipped(own, Z0, Y)
    from_x = lax.ppermute(own, AXES, over_x)
    from_z = lax.ppermute(own, AXES, over_z)
    pair = jnp.concatenate([own, near], axis=0)
    far = flipped(pair, Y, Z0)
    from_x, from_z, _ = lax.optimization_barrier((from_x, from_z, pair))

    part = jnp.where(x == z1, jnp.where(core == z0, own, from_z), from_x)
    other_part = flipped(part, (1, 0), (1, 0))
    halves = jnp.where(core == 0, part, other_part), jnp.where(core == 0, other_part, part)
    cuts = (0, sizes[0]), (sizes[0], block)
    columns = jnp.concatenate([half[a:b] for a, b in cuts for half in halves], axis=0)

    gram = gram_first(sizes, places, own, near, columns)
    far, gram = lax.optimization_barrier((far, gram))
    partial = project(sizes, places, own, near, far, naf_vectors)
    partial = partial.reshape(4, virtuals // 4, -1)
    share = lambda flip: lax.dynamic_index_in_dim(partial, row_index ^ flip, 0, keepdims=False)
    parts = [flipped(share(flip), (flip, 0), (flip, 0)) for flip in (3, 2, 1)]
    gram = gram_rest(sizes, places, far, columns, gram)
    parts, gram = lax.optimization_barrier((parts, gram))
    naf_ints = share(0) + parts[0] + parts[1] + parts[2]
    return gram, naf_ints


def solution(mesh):
    in_specs = (P(("row", "col"), None), P(("row", "col"), None), P("row", "col"))
    out_specs = (P("row", "col"), P("row", "col"))
    plan = shards_4x8 if (mesh.shape["row"], mesh.shape["col"]) == (4, 8) else shards
    return jax.shard_map(plan, mesh=mesh, in_specs=in_specs, out_specs=out_specs, check_vma=False)
```

time: 83.8 us -> 81.3 us (0.970)
  waiting for transfers between devices: 27.7 us -> 31.6 us
  Pallas kernels: 23.8 us -> 21.5 us
  starting transfers between devices: 24.6 us -> 22.3 us
  other arithmetic: 5.39 us -> 4.29 us
    ppermute x15, waiting for transfers between devices: 27 us -> 30.9 us  [flipped(): return lax.ppermute(value, AXES, pairs)]
    ppermute x15, starting transfers between devices: 21.3 us -> 19 us  [flipped(): return lax.ppermute(value, AXES, pairs)]
    convert_element_type x10 -> x8, other arithmetic: 3.6 us -> 1.32 us  [packed(): jnp.where(head, exponent, value * jnp.exp2(14.0 - exponent))]
    pallas_call x4 -> x3, Pallas kernels: 9.67 us -> 8.39 us  [the longest x1 3.39 us: half_pieces(): pl.pallas_call(functools.partial(half_first_kernel, sizes), grid_spec=plt...]
    convert_element_type x0 -> x2, other arithmetic: none -> 1.13 us  [shards_4x8(): p.astype(jnp.float16)]
    pallas_call x1, Pallas kernels: 7.79 us -> 6.76 us  [gram_first(): pl.pallas_call(functools.partial(gram_first_kernel, sizes, 1.0 / virtuals...]
  transfers between devices with their start and end apart: 17 -> 17, of which waited for: 10 -> 9; matrix products, arithmetic and copies ran while one was open for 3% -> 2% of each run, Pallas kernels for 24% -> 20%
where the time goes in v3:
time: 81.3 us; the launch traced here: 80.7 us
  waiting for transfers between devices  31.6 us (39%)
  starting transfers between devices  22.3 us (27%)
  Pallas kernels  21.5 us (26%)
  other arithmetic  4.29 us (5%)
  between operations  1.02 us (1%)
    ppermute x15, waiting for transfers between devices, flipped(): return lax.ppermute(value, AXES, pairs)  30.9 us
    ppermute x15, starting transfers between devices, flipped(): return lax.ppermute(value, AXES, pairs)  19 us
    pallas_call x1, Pallas kernels, gram_first(): pl.pallas_call(functools.partial(gram_first_kernel, sizes, 1.0 / virtuals...  6.76 us
    pallas_call x1, Pallas kernels, gram_rest(): pl.pallas_call(functools.partial(gram_rest_kernel, sizes, 1.0 / virtuals)...  6.3 us
    pallas_call x1, Pallas kernels, half_pieces(): pl.pallas_call(functools.partial(half_first_kernel, sizes), grid_spec=plt...  3.39 us
    pallas_call x1, Pallas kernels, rest(): pl.pallas_call(functools.partial(half_rest_kernel, sizes), grid_spec=pltp...  3.11 us
    ppermute x1, starting transfers between devices, shards_4x8(): from_x = lax.ppermute(own, AXES, over_x)  2.62 us
    pallas_call x1, Pallas kernels, project(): pl.pallas_call(functools.partial(naf_kernel, sizes), grid_spec=pltpu.Pref...  1.89 us
  transfers between devices with their start and end apart: 17, of which 9 were waited for; matrix products, arithmetic and copies ran while one was open for 2% of the time, Pallas kernels for 20%

profile of v3, /device:TPU:0, one launch (start us, length us, event | category | flops | bytes accessed | tf_op | source)
XLA Modules:
  0.0 80.7 jit_solution(6329655001626985778)
XLA Ops:
  0.6 3.4 %shard_map.51 = (f32[297,16,128]{2,1,0:T(8,128)S(1)}, f32[185,16,128]{2,1,0:T(8,128)S(1)}) custom-call(s32[1]{0:T(128)} %bitcast.5.bits, bf16[160,128]{1,0:T(8,128)(2,1)} %vir.3, bf16[160,15360]{1,0:T(8,128)(2,1)} %ao.3), custom_call_target="tpu_custom_call" | custom-call | flops 314572800 | bytes 6389760 | tf_op jit(solution)/shard_map/pallas_call | solution.py:129
  4.7 1.0 %convert_element_type.287 = f16[185,16,128]{2,1,0:T(8,128)(2,1)} convert(f32[185,16,128]{2,1,0:T(8,128)S(1)} %get-tuple-element.38) | non-fusion elementwise | flops 378880 | bytes 2273280 | tf_op jit(solution)/shard_map/convert_element_type | solution.py:319
  5.8 3.1 %shard_map.50 = (f32[297,16,128]{2,1,0:T(8,128)S(1)}, f32[185,16,128]{2,1,0:T(8,128)S(1)}, f32[8,128]{1,0:T(8,128)S(1)}) custom-call(s32[1]{0:T(128)} %bitcast.4.bits, bf16[160,128]{1,0:T(8,128)(2,1)} %vir.3, bf16[160,15360]{1,0:T(8,128)(2,1)} %ao.3), custom_call_target="tpu_custom_call" | custom-call | flops 314572800 | bytes 6389760 | tf_op jit(solution)/shard_map/pallas_call | solution.py:146
  9.6 3.1 %collective-permute-start.3 = (f16[93,16,128]{2,1,0:T(8,128)(2,1)S(1)}, f16[93,16,128]{2,1,0:T(8,128)(2,1)S(1)}, u32[]{:S(2)}, u32[]{:S(2)}) collective-permute-start(f16[93,16,128]{2,1,0:T(8,128)(2,1)S(1)} %select_convert_fusion.1), channel_id=1, source_target_pairs={{0,2},{1,3},{2,0},{3,1},{4,6},{5,7},{6,4},{7,5},{8,10},{9,11},{10,... | collective-permute-start | bytes 1142792 | tf_op jit(solution)/shard_map/ppermute | solution.py:54
  12.6 1.5 %collective-permute-start.2 = (f16[149,16,128]{2,1,0:T(8,128)(2,1)S(1)}, f16[149,16,128]{2,1,0:T(8,128)(2,1)S(1)}, u32[]{:S(2)}, u32[]{:S(2)}) collective-permute-start(f16[149,16,128]{2,1,0:T(8,128)(2,1)S(1)} %select_convert_fusion), channel_id=1, source_target_pairs={{0,1},{1,0},{2,3},{3,2},{4,5},{5,4},{6,7},{7,6},{8,24},{9,25},{10,... | collective-permute-start | bytes 1830920 | tf_op jit(solution)/shard_map/ppermute | solution.py:54
  14.5 8.2 %collective-permute-done.2 = f16[149,16,128]{2,1,0:T(8,128)(2,1)S(1)} collective-permute-done((f16[149,16,128]{2,1,0:T(8,128)(2,1)S(1)}, f16[149,16,128]{2,1,0:T(8,128)(2,1)S(1)}, u32[]{:S(2)}, u32[]{:S(2)}) %collective-permute-start.2) | collective-permute-done | bytes 610336 | tf_op jit(solution)/shard_map/ppermute | solution.py:54
  23.1 1.6 %collective-permute-start.5 = (f16[47,16,128]{2,1,0:T(8,128)(2,1)S(1)}, f16[47,16,128]{2,1,0:T(8,128)(2,1)S(1)}, u32[]{:S(2)}, u32[]{:S(2)}) collective-permute-start(f16[47,16,128]{2,1,0:T(8,128)(2,1)S(1)} %select_convert_fusion.3), channel_id=1, source_target_pairs={{0,16},{1,17},{2,18},{3,19},{4,20},{5,21},{6,22},{7,23},{8,24},{9,... | collective-permute-start | bytes 577544 | tf_op jit(solution)/shard_map/ppermute | solution.py:54
  25.5 6.0 %collective-permute-done.4 = f16[75,16,128]{2,1,0:T(8,128)(2,1)S(1)} collective-permute-done((f16[75,16,128]{2,1,0:T(8,128)(2,1)S(1)}, f16[75,16,128]{2,1,0:T(8,128)(2,1)S(1)}, u32[]{:S(2)}, u32[]{:S(2)}) %collective-permute-start.4) | collective-permute-done | bytes 307232 | tf_op jit(solution)/shard_map/ppermute | solution.py:54
  31.8 1.6 %collective-permute-start.7 = (f16[24,16,128]{2,1,0:T(8,128)(2,1)S(1)}, f16[24,16,128]{2,1,0:T(8,128)(2,1)S(1)}, u32[]{:S(2)}, u32[]{:S(2)}) collective-permute-start(f16[24,16,128]{2,1,0:T(8,128)(2,1)S(1)} %select_convert_fusion.6), channel_id=1, source_target_pairs={{0,1},{1,0},{2,3},{3,2},{4,5},{5,4},{6,7},{7,6},{8,9},{9,8},{10,11... | collective-permute-start | bytes 294920 | tf_op jit(solution)/shard_map/ppermute | solution.py:54
  34.0 2.5 %collective-permute-done.7 = f16[24,16,128]{2,1,0:T(8,128)(2,1)S(1)} collective-permute-done((f16[24,16,128]{2,1,0:T(8,128)(2,1)S(1)}, f16[24,16,128]{2,1,0:T(8,128)(2,1)S(1)}, u32[]{:S(2)}, u32[]{:S(2)}) %collective-permute-start.7) | collective-permute-done | bytes 98336 | tf_op jit(solution)/shard_map/ppermute | solution.py:54
  36.5 2.1 %collective-permute-done.6 = f16[38,16,128]{2,1,0:T(8,128)(2,1)S(1)} collective-permute-done((f16[38,16,128]{2,1,0:T(8,128)(2,1)S(1)}, f16[38,16,128]{2,1,0:T(8,128)(2,1)S(1)}, u32[]{:S(2)}, u32[]{:S(2)}) %collective-permute-start.6) | collective-permute-done | bytes 155680 | tf_op jit(solution)/shard_map/ppermute | solution.py:54
  39.0 2.7 %collective-permute-start.8 = (f16[61,16,128]{2,1,0:T(8,128)(2,1)S(1)}, f16[61,16,128]{2,1,0:T(8,128)(2,1)S(1)}, u32[]{:S(2)}, u32[]{:S(2)}) collective-permute-start(f16[61,16,128]{2,1,0:T(8,128)(2,1)S(1)} %pad_maximum_fusion.2), channel_id=1, source_target_pairs={{0,4},{1,5},{2,6},{3,7},{4,0},{5,1},{6,2},{7,3},{8,12},{9,13},{10,... | collective-permute-start | bytes 749576 | tf_op jit(solution)/shard_map/ppermute | solution.py:54
  41.6 7.9 %collective-permute-done.8 = f16[61,16,128]{2,1,0:T(8,128)(2,1)S(1)} collective-permute-done((f16[61,16,128]{2,1,0:T(8,128)(2,1)S(1)}, f16[61,16,128]{2,1,0:T(8,128)(2,1)S(1)}, u32[]{:S(2)}, u32[]{:S(2)}) %collective-permute-start.8) | collective-permute-done | bytes 249888 | tf_op jit(solution)/shard_map/ppermute | solution.py:54
  49.9 0.7 collective-permute-start.12
  50.6 2.6 %collective-permute-start.11 = (bf16[960,128]{1,0:T(8,128)(2,1)S(1)}, bf16[960,128]{1,0:T(8,128)(2,1)S(1)}, u32[]{:S(2)}, u32[]{:S(2)}) collective-permute-start(bf16[960,128]{1,0:T(8,128)(2,1)S(1)} %bitcast.125), channel_id=1, source_target_pairs={{0,16},{1,17},{10,26},{11,27},{20,4},{21,5},{30,14},{31,15},{2,24}... | collective-permute-start | bytes 737288 | tf_op jit(solution)/shard_map/ppermute | solution.py:358
  53.2 2.7 %collective-permute-done.9.near = bf16[960,128]{1,0:T(8,128)(2,1)S(1)} collective-permute-done((bf16[960,128]{1,0:T(8,128)(2,1)S(1)}, bf16[960,128]{1,0:T(8,128)(2,1)S(1)}, u32[]{:S(2)}, u32[]{:S(2)}) %collective-permute-start.9) | collective-permute-done | bytes 245792 | tf_op jit(solution)/shard_map/ppermute | solution.py:54
  56.0 0.7 collective-permute-done.11
  56.8 2.9 %collective-permute-start.13 = (bf16[960,128]{1,0:T(8,128)(2,1)S(1)}, bf16[960,128]{1,0:T(8,128)(2,1)S(1)}, u32[]{:S(2)}, u32[]{:S(2)}) collective-permute-start(bf16[960,128]{1,0:T(8,128)(2,1)S(1)} %select_select_fusion), channel_id=1, source_target_pairs={{0,8},{1,9},{2,10},{3,11},{4,12},{5,13},{6,14},{7,15},{8,0},{9,1},... | collective-permute-start | bytes 737288 | tf_op jit(solution)/shard_map/ppermute | solution.py:54
  61.0 6.8 %shard_map.52.begun = f32[3840,1920]{1,0:T(8,128)} custom-call(s32[4]{0:T(128)S(1)} %pad_add_fusion.places, bf16[960,128]{1,0:T(8,128)(2,1)S(1)} %bitcast.127, bf16[960,128]{1,0:T(8,128)(2,1)S(1)} %collective-permute-done.9.near, bf16[1920,128]{1,0:T(8,128)(2,1)S(1)} %pad_maximum_fusion.1.cols), custom_call_target="tpu_custom_call" | custom-call | flops 943718400 | bytes 14745600 | tf_op jit(solution)/shard_map/pallas_call | solution.py:246
  67.8 0.8 collective-permute-done.10.far
  68.6 1.9 %shard_map.53 = f32[128,896]{1,0:T(8,128)S(1)} custom-call(s32[4]{0:T(128)S(1)} %pad_add_fusion.places, bf16[960,128]{1,0:T(8,128)(2,1)S(1)} %bitcast.128, bf16[960,128]{1,0:T(8,128)(2,1)S(1)} %collective-permute-done.9.near, bf16[1920,128]{1,0:T(8,128)(2,1)S(1)} %collective-permute-done.10.far, bf16[3840,896]{1,0:T(8,128)(2,1)S(1)} %bitcast.122), custom_call_target="tpu_custom_call" | custom-call | flops 880803840 | bytes 6881280 | tf_op jit(solution)/shard_map/pallas_call | solution.py:292
  70.6 3.0 %collective-permute-start.15 = (f32[32,896]{1,0:T(8,128)S(1)}, f32[32,896]{1,0:T(8,128)S(1)}, u32[]{:S(2)}, u32[]{:S(2)}) collective-permute-start(f32[32,896]{1,0:T(8,128)S(1)} %get-tuple-element.81), channel_id=1, source_target_pairs={{0,16},{1,17},{2,18},{3,19},{4,20},{5,21},{6,22},{7,23},{8,24},{9,... | collective-permute-start | bytes 344072 | tf_op jit(solution)/shard_map/ppermute | solution.py:54
  73.7 6.3 %shard_map.54 = f32[3840,1920]{1,0:T(8,128)} custom-call(s32[4]{0:T(128)S(1)} %pad_add_fusion.places, bf16[1920,128]{1,0:T(8,128)(2,1)S(1)} %collective-permute-done.10.far, bf16[1920,128]{1,0:T(8,128)(2,1)S(1)} %pad_maximum_fusion.1.cols, f32[3840,1920]{1,0:T(8,128)} %shard_map.52.begun), custom_call_target="tpu_custom_call", output_to_operand_aliasing={{}: (3, {})} | custom-call | flops 943718400 | bytes 14745600 | tf_op jit(solution)/shard_map/pallas_call | solution.py:265
  80.0 0.7 fusion.6
  (74 shorter events, 5.9 us)
Async XLA Ops:
  4.2 4.7 %collective-permute-start = (f16[297,16,128]{2,1,0:T(8,128)(2,1)S(1)}, f16[297,16,128]{2,1,0:T(8,128)(2,1)S(1)}, u32[]{:S(2)}, u32[]{:S(2)}) collective-permute-start(f16[297,16,128]{2,1,0:T(8,128)(2,1)S(1)} %convert_element_type.284), channel_id=1, source_target_pairs={{0,8},{1,9},{2,10},{3,11},{4,12},{5,13},{6,14},{7,15},{8,0},{9,1},... | collective-permute-start | bytes 3649544 | tf_op jit(solution)/shard_map/ppermute | solution.py:54
  5.7 3.3 %collective-permute-start.1 = (f16[185,16,128]{2,1,0:T(8,128)(2,1)}, f16[185,16,128]{2,1,0:T(8,128)(2,1)S(1)}, u32[]{:S(2)}, u32[]{:S(2)}) collective-permute-start(f16[185,16,128]{2,1,0:T(8,128)(2,1)} %convert_element_type.287), channel_id=1, source_target_pairs={{0,8},{1,9},{2,10},{3,11},{4,12},{5,13},{6,14},{7,15},{8,0},{9,1},... | collective-permute-start | bytes 2273288 | tf_op jit(solution)/shard_map/ppermute | solution.py:54
  9.6 13.2 %collective-permute-start.3 = (f16[93,16,128]{2,1,0:T(8,128)(2,1)S(1)}, f16[93,16,128]{2,1,0:T(8,128)(2,1)S(1)}, u32[]{:S(2)}, u32[]{:S(2)}) collective-permute-start(f16[93,16,128]{2,1,0:T(8,128)(2,1)S(1)} %select_convert_fusion.1), channel_id=1, source_target_pairs={{0,2},{1,3},{2,0},{3,1},{4,6},{5,7},{6,4},{7,5},{8,10},{9,11},{10,... | collective-permute-start | bytes 1142792 | tf_op jit(solution)/shard_map/ppermute | solution.py:54
  12.6 10.1 %collective-permute-start.2 = (f16[149,16,128]{2,1,0:T(8,128)(2,1)S(1)}, f16[149,16,128]{2,1,0:T(8,128)(2,1)S(1)}, u32[]{:S(2)}, u32[]{:S(2)}) collective-permute-start(f16[149,16,128]{2,1,0:T(8,128)(2,1)S(1)} %select_convert_fusion), channel_id=1, source_target_pairs={{0,1},{1,0},{2,3},{3,2},{4,5},{5,4},{6,7},{7,6},{8,24},{9,25},{10,... | collective-permute-start | bytes 1830920 | tf_op jit(solution)/shard_map/ppermute | solution.py:54
  23.1 8.4 %collective-permute-start.5 = (f16[47,16,128]{2,1,0:T(8,128)(2,1)S(1)}, f16[47,16,128]{2,1,0:T(8,128)(2,1)S(1)}, u32[]{:S(2)}, u32[]{:S(2)}) collective-permute-start(f16[47,16,128]{2,1,0:T(8,128)(2,1)S(1)} %select_convert_fusion.3), channel_id=1, source_target_pairs={{0,16},{1,17},{2,18},{3,19},{4,20},{5,21},{6,22},{7,23},{8,24},{9,... | collective-permute-start | bytes 577544 | tf_op jit(solution)/shard_map/ppermute | solution.py:54
  24.7 6.9 %collective-permute-start.4 = (f16[75,16,128]{2,1,0:T(8,128)(2,1)S(1)}, f16[75,16,128]{2,1,0:T(8,128)(2,1)S(1)}, u32[]{:S(2)}, u32[]{:S(2)}) collective-permute-start(f16[75,16,128]{2,1,0:T(8,128)(2,1)S(1)} %select_convert_fusion.2), channel_id=1, source_target_pairs={{0,2},{1,3},{2,0},{3,1},{4,6},{5,7},{6,4},{7,5},{8,9},{9,8},{10,11... | collective-permute-start | bytes 921608 | tf_op jit(solution)/shard_map/ppermute | solution.py:54
  31.8 4.7 %collective-permute-start.7 = (f16[24,16,128]{2,1,0:T(8,128)(2,1)S(1)}, f16[24,16,128]{2,1,0:T(8,128)(2,1)S(1)}, u32[]{:S(2)}, u32[]{:S(2)}) collective-permute-start(f16[24,16,128]{2,1,0:T(8,128)(2,1)S(1)} %select_convert_fusion.6), channel_id=1, source_target_pairs={{0,1},{1,0},{2,3},{3,2},{4,5},{5,4},{6,7},{7,6},{8,9},{9,8},{10,11... | collective-permute-start | bytes 294920 | tf_op jit(solution)/shard_map/ppermute | solution.py:54
  33.4 5.2 %collective-permute-start.6 = (f16[38,16,128]{2,1,0:T(8,128)(2,1)S(1)}, f16[38,16,128]{2,1,0:T(8,128)(2,1)S(1)}, u32[]{:S(2)}, u32[]{:S(2)}) collective-permute-start(f16[38,16,128]{2,1,0:T(8,128)(2,1)S(1)} %select_convert_fusion.4), channel_id=1, source_target_pairs={{0,16},{1,17},{2,18},{3,19},{4,20},{5,21},{6,22},{7,23},{8,10},{9,... | collective-permute-start | bytes 466952 | tf_op jit(solution)/shard_map/ppermute | solution.py:54
  39.0 10.6 %collective-permute-start.8 = (f16[61,16,128]{2,1,0:T(8,128)(2,1)S(1)}, f16[61,16,128]{2,1,0:T(8,128)(2,1)S(1)}, u32[]{:S(2)}, u32[]{:S(2)}) collective-permute-start(f16[61,16,128]{2,1,0:T(8,128)(2,1)S(1)} %pad_maximum_fusion.2), channel_id=1, source_target_pairs={{0,4},{1,5},{2,6},{3,7},{4,0},{5,1},{6,2},{7,3},{8,12},{9,13},{10,... | collective-permute-start | bytes 749576 | tf_op jit(solution)/shard_map/ppermute | solution.py:54
  49.7 6.3 %collective-permute-start.9 = (bf16[960,128]{1,0:T(8,128)(2,1)S(1)}, bf16[960,128]{1,0:T(8,128)(2,1)S(1)}, u32[]{:S(2)}, u32[]{:S(2)}) collective-permute-start(bf16[960,128]{1,0:T(8,128)(2,1)S(1)} %bitcast.123), channel_id=1, source_target_pairs={{0,2},{1,3},{2,0},{3,1},{4,6},{5,7},{6,4},{7,5},{8,9},{9,8},{10,11... | collective-permute-start | bytes 737288 | tf_op jit(solution)/shard_map/ppermute | solution.py:54
  49.9 6.1 %collective-permute-start.12 = (bf16[960,128]{1,0:T(8,128)(2,1)S(1)}, bf16[960,128]{1,0:T(8,128)(2,1)S(1)}, u32[]{:S(2)}, u32[]{:S(2)}) collective-permute-start(bf16[960,128]{1,0:T(8,128)(2,1)S(1)} %bitcast.124), channel_id=1, source_target_pairs={{2,8},{3,9},{8,2},{9,3},{22,28},{23,29},{28,22},{29,23}} | collective-permute-start | bytes 737288 | tf_op jit(solution)/shard_map/ppermute | solution.py:359
  50.6 6.1 %collective-permute-start.11 = (bf16[960,128]{1,0:T(8,128)(2,1)S(1)}, bf16[960,128]{1,0:T(8,128)(2,1)S(1)}, u32[]{:S(2)}, u32[]{:S(2)}) collective-permute-start(bf16[960,128]{1,0:T(8,128)(2,1)S(1)} %bitcast.125), channel_id=1, source_target_pairs={{0,16},{1,17},{10,26},{11,27},{20,4},{21,5},{30,14},{31,15},{2,24}... | collective-permute-start | bytes 737288 | tf_op jit(solution)/shard_map/ppermute | solution.py:358
  56.8 4.1 %collective-permute-start.13 = (bf16[960,128]{1,0:T(8,128)(2,1)S(1)}, bf16[960,128]{1,0:T(8,128)(2,1)S(1)}, u32[]{:S(2)}, u32[]{:S(2)}) collective-permute-start(bf16[960,128]{1,0:T(8,128)(2,1)S(1)} %select_select_fusion), channel_id=1, source_target_pairs={{0,8},{1,9},{2,10},{3,11},{4,12},{5,13},{6,14},{7,15},{8,0},{9,1},... | collective-permute-start | bytes 737288 | tf_op jit(solution)/shard_map/ppermute | solution.py:54
  59.7 8.8 %collective-permute-start.10 = (bf16[1920,128]{1,0:T(8,128)(2,1)S(1)}, bf16[1920,128]{1,0:T(8,128)(2,1)S(1)}, u32[]{:S(2)}, u32[]{:S(2)}) collective-permute-start(bf16[1920,128]{1,0:T(8,128)(2,1)S(1)} %pad_maximum_fusion), channel_id=1, source_target_pairs={{0,1},{1,0},{2,3},{3,2},{4,5},{5,4},{6,7},{7,6},{8,10},{9,11},{10,... | collective-permute-start | bytes 1474568 | tf_op jit(solution)/shard_map/ppermute | solution.py:54
  60.9 7.6 %slice-start = ((s8[6881280]{0:T(1024)(128)(4,1)}), s8[4194304]{0:T(1024)(128)(4,1)S(1)}, s32[]{:S(2)}) async-start(s8[6881280]{0:T(1024)(128)(4,1)} %bitcast.121), calls=%async_computation | async-start | bytes 8388608
  61.0 7.6 %slice-start.1 = ((s8[6881280]{0:T(1024)(128)(4,1)}), s8[2686976]{0:T(1024)(128)(4,1)S(1)}, s32[]{:S(2)}) async-start(s8[6881280]{0:T(1024)(128)(4,1)} %bitcast.121), calls=%async_computation.1 | async-start | bytes 5373952
  70.5 9.5 %collective-permute-start.16 = (f32[32,896]{1,0:T(8,128)S(1)}, f32[32,896]{1,0:T(8,128)S(1)}, u32[]{:S(2)}, u32[]{:S(2)}) collective-permute-start(f32[32,896]{1,0:T(8,128)S(1)} %get-tuple-element.80), channel_id=1, source_target_pairs={{0,8},{1,9},{2,10},{3,11},{4,12},{5,13},{6,14},{7,15},{8,0},{9,1},... | collective-permute-start | bytes 344072 | tf_op jit(solution)/shard_map/ppermute | solution.py:54
  70.6 9.4 %collective-permute-start.15 = (f32[32,896]{1,0:T(8,128)S(1)}, f32[32,896]{1,0:T(8,128)S(1)}, u32[]{:S(2)}, u32[]{:S(2)}) collective-permute-start(f32[32,896]{1,0:T(8,128)S(1)} %get-tuple-element.81), channel_id=1, source_target_pairs={{0,16},{1,17},{2,18},{3,19},{4,20},{5,21},{6,22},{7,23},{8,24},{9,... | collective-permute-start | bytes 344072 | tf_op jit(solution)/shard_map/ppermute | solution.py:54
  73.6 6.4 %collective-permute-start.14 = (f32[32,896]{1,0:T(8,128)S(1)}, f32[32,896]{1,0:T(8,128)S(1)}, u32[]{:S(2)}, u32[]{:S(2)}) collective-permute-start(f32[32,896]{1,0:T(8,128)S(1)} %get-tuple-element.82), channel_id=1, source_target_pairs={{0,24},{1,25},{2,26},{3,27},{4,28},{5,29},{6,30},{7,31},{8,16},{9,... | collective-permute-start | bytes 344072 | tf_op jit(solution)/shard_map/ppermute | solution.py:54

commit v4 on v3

--- a/solution.py
+++ b/solution.py
@@ -231,61 +231,62 @@
         copy.wait()
 
 
-def gram_first_kernel(sizes, scale, places, own, near, cols, out, buffers, sems):
-    blocks = blocks_of(sizes, places, own, 0, 1) + blocks_of(sizes, places, near, 1, 1)
+def gram_first_kernel(sizes, scale, places, pair, cols, out, buffers, sems):
+    blocks = blocks_of(sizes, (places[0], places[2]), pair, 0, 2)
     gram_steps(sizes, scale, blocks, cols, out, buffers, sems)
 
 
-def gram_rest_kernel(sizes, scale, places, far, cols, begun, out, buffers, sems):
-    gram_steps(sizes, scale, blocks_of(sizes, places, far, 2, 2), cols, out, buffers, sems)
-
-
-def gram_first(sizes, places, own, near, cols):
+def gram_rest_kernel(sizes, scale, places, near, far, cols, begun, out, buffers, sems):
+    blocks = blocks_of(sizes, places, near, 1, 1) + blocks_of(sizes, places, far, 3, 1)
+    gram_steps(sizes, scale, blocks, cols, out, buffers, sems)
+
+
+def gram_first(sizes, places, pair, cols):
     in_vmem = pl.BlockSpec(memory_space=pltpu.VMEM)
-    block, virtuals = own.shape
+    block, virtuals = pair.shape[0] // 2, pair.shape[1]
     return pl.pallas_call(
         functools.partial(gram_first_kernel, sizes, 1.0 / virtuals),
         grid_spec=pltpu.PrefetchScalarGridSpec(
             num_scalar_prefetch=1,
             grid=(),
-            in_specs=[in_vmem] * 3,
+            in_specs=[in_vmem] * 2,
             out_specs=pl.BlockSpec(memory_space=pl.ANY),
             scratch_shapes=[pltpu.VMEM((SLOTS, step_rows(sizes), 2 * block), jnp.float32), pltpu.SemaphoreType.DMA((SLOTS,))],
         ),
         out_shape=jax.ShapeDtypeStruct((4 * block, 2 * block), jnp.float32),
         compiler_params=pltpu.CompilerParams(vmem_limit_bytes=VMEM_LIMIT),
         cost_estimate=pl.CostEstimate(flops=8 * block * block * virtuals, bytes_accessed=16 * block * block, transcendentals=0),
-    )(places, own, near, cols)
-
-
-def gram_rest(sizes, places, far, cols, begun):
+    )(places, pair, cols)
+
+
+def gram_rest(sizes, places, near, far, cols, begun):
     in_vmem = pl.BlockSpec(memory_space=pltpu.VMEM)
     in_hbm = pl.BlockSpec(memory_space=pl.ANY)
-    block, virtuals = far.shape[0] // 2, far.shape[1]
+    block, virtuals = far.shape
     return pl.pallas_call(
         functools.partial(gram_rest_kernel, sizes, 1.0 / virtuals),
         grid_spec=pltpu.PrefetchScalarGridSpec(
             num_scalar_prefetch=1,
             grid=(),
-            in_specs=[in_vmem, in_vmem, in_hbm],
+            in_specs=[in_vmem, in_vmem, in_vmem, in_hbm],
             out_specs=in_hbm,
             scratch_shapes=[pltpu.VMEM((SLOTS, step_rows(sizes), 2 * block), jnp.float32), pltpu.SemaphoreType.DMA((SLOTS,))],
         ),
         out_shape=jax.ShapeDtypeStruct((4 * block, 2 * block), jnp.float32),
-        input_output_aliases={3: 0},
+        input_output_aliases={4: 0},
         compiler_params=pltpu.CompilerParams(vmem_limit_bytes=VMEM_LIMIT),
         cost_estimate=pl.CostEstimate(flops=8 * block * block * virtuals, bytes_accessed=16 * block * block, transcendentals=0),
-    )(places, far, cols, begun)
-
-
-def naf_kernel(sizes, places, own, near, far, naf, out, panel):
-    blocks = blocks_of(sizes, places, own, 0, 1) + blocks_of(sizes, places, near, 1, 1)
-    for ref, at, rows, row in blocks + blocks_of(sizes, places, far, 2, 2):
-        panel[pl.ds(row, rows), :] = ref[at : at + rows]
+    )(places, near, far, cols, begun)
+
+
+def naf_kernel(sizes, places, own, near, side, far, naf, out, panel):
+    for n, block in enumerate((own, near, side, far)):
+        for ref, at, rows, row in blocks_of(sizes, places, block, n, 1):
+            panel[pl.ds(row, rows), :] = ref[at : at + rows]
     out[...] = contract_first(panel[...], naf[...])
 
 
-def project(sizes, places, own, near, far, naf_vectors):
+def project(sizes, places, own, near, side, far, naf_vectors):
     virtuals = own.shape[1]
     rows, nnaf = naf_vectors.shape
     in_vmem = pl.BlockSpec(memory_space=pltpu.VMEM)
@@ -294,14 +295,14 @@
         grid_spec=pltpu.PrefetchScalarGridSpec(
             num_scalar_prefetch=1,
             grid=(),
-            in_specs=[in_vmem] * 4,
+            in_specs=[in_vmem] * 5,
             out_specs=in_vmem,
             scratch_shapes=[pltpu.VMEM((rows, virtuals), jnp.bfloat16)],
         ),
         out_shape=pltpu.VMEM((virtuals, nnaf), jnp.float32),
         compiler_params=pltpu.CompilerParams(vmem_limit_bytes=10 * 2**20),
         cost_estimate=pl.CostEstimate(flops=2 * rows * nnaf * virtuals, bytes_accessed=2 * rows * nnaf, transcendentals=0),
-    )(places, own, near, far, naf_vectors)
+    )(places, own, near, side, far, naf_vectors)
 
 
 def shards_4x8(ao_ints, vir_coef, naf_vectors):
@@ -340,9 +341,7 @@
     last = [packed(joined(k, m, 0, n), level) for k, m, n in zip(kept, arrived, tiles)]
     mine = jnp.concatenate([last[0][:-1], last[1]], axis=0)
     theirs = flipped(mine, Z1, Z1)
-    near_place = jnp.where(core == 0, 2 * y + 1 - z0, 2 * (1 - y) + z0)
-    far_place = jnp.where(core == 0, 2 * (1 - y) + z0, 2 * y + 1 - z0)
-    places = jnp.stack([2 * y + z0, near_place, far_place, 2 * (1 - y) + 1 - z0]).astype(jnp.int32)
+    places = jnp.stack([2 * (i ^ y) + (j ^ z0) for i in range(2) for j in range(2)]).astype(jnp.int32)
     terms = [m[:-1].astype(jnp.float32) * jnp.exp2(exponent_in(m) - 14.0) for m in (mine, theirs)]
     own = (terms[0] + terms[1]).astype(jnp.bfloat16).reshape(-1, virtuals)
     block = sum(sizes)
@@ -353,27 +352,29 @@
     corners = [(a, b, c) for a in range(2) for b in range(2) for c in range(2)]
     over_x = [(place_of(a, b, a, b, c), place_of(1 - a, b, a, b, c)) for a, b, c in corners]
     over_x += [(place_of(a, b, a, 1 - b, c), place_of(1 - a, 1 - b, a, b, c)) for a, b, c in corners]
-    over_z = [(place_of(a, b, a, 1 - b, c), place_of(a, 1 - b, a, b, c)) for a, b, c in corners]
-    near = flipped(own, Z0, Y)
+    near = flipped(own, Z0, Z0)
     from_x = lax.ppermute(own, AXES, over_x)
-    from_z = lax.ppermute(own, AXES, over_z)
-    pair = jnp.concatenate([own, near], axis=0)
-    far = flipped(pair, Y, Z0)
-    from_x, from_z, _ = lax.optimization_barrier((from_x, from_z, pair))
-
-    part = jnp.where(x == z1, jnp.where(core == z0, own, from_z), from_x)
-    other_part = flipped(part, (1, 0), (1, 0))
-    halves = jnp.where(core == 0, part, other_part), jnp.where(core == 0, other_part, part)
+    side = flipped(own, Y, Y)
+    pair = jnp.concatenate([own, side], axis=0)
+    from_x, near, pair = lax.optimization_barrier((from_x, near, pair))
+    here = jnp.where(x == z1, own, from_x)
+    there = jnp.where(x == z1, near, from_x)
+    mine = jnp.where(z0 == 0, jnp.concatenate([here, there], axis=0), jnp.concatenate([there, here], axis=0))
+    theirs = flipped(mine, (1, 0), (1, 0))
+    far = flipped(near, Y, Y)
+    first_mine = (core == z0) == ((z0 == 0) | (x == z1))
+    second_mine = (core == z0) == ((z0 == 1) | (x == z1))
+    halves = jnp.where(first_mine, mine[:block], theirs[:block]), jnp.where(second_mine, mine[block:], theirs[block:])
     cuts = (0, sizes[0]), (sizes[0], block)
     columns = jnp.concatenate([half[a:b] for a, b in cuts for half in halves], axis=0)
 
-    gram = gram_first(sizes, places, own, near, columns)
+    gram = gram_first(sizes, places, pair, columns)
     far, gram = lax.optimization_barrier((far, gram))
-    partial = project(sizes, places, own, near, far, naf_vectors)
+    partial = project(sizes, places, own, near, pair[block:], far, naf_vectors)
     partial = partial.reshape(4, virtuals // 4, -1)
     share = lambda flip: lax.dynamic_index_in_dim(partial, row_index ^ flip, 0, keepdims=False)
     parts = [flipped(share(flip), (flip, 0), (flip, 0)) for flip in (3, 2, 1)]
-    gram = gram_rest(sizes, places, far, columns, gram)
+    gram = gram_rest(sizes, places, near, far, columns, gram)
     parts, gram = lax.optimization_barrier((parts, gram))
     naf_ints = share(0) + parts[0] + parts[1] + parts[2]
     return gram, naf_ints

time: 81.3 us -> 80.2 us (0.986)
  starting transfers between devices: 22.3 us -> 19.8 us
  waiting for transfers between devices: 31.6 us -> 33.1 us
    ppermute x1, waiting for transfers between devices: 0.71 us -> 2.7 us  [shards_4x8(): from_x = lax.ppermute(own, AXES, over_x)]
    ppermute x15 -> x16, starting transfers between devices: 19 us -> 17.2 us  [flipped(): return lax.ppermute(value, AXES, pairs)]
    ppermute x15 -> x16, waiting for transfers between devices: 30.9 us -> 30.4 us  [flipped(): return lax.ppermute(value, AXES, pairs)]
where the time goes in v4:
time: 80.2 us; the launch traced here: 80 us
  waiting for transfers between devices  33.1 us (41%)
  Pallas kernels  21.4 us (27%)
  starting transfers between devices  19.8 us (25%)
  other arithmetic  4.46 us (6%)
  between operations  1.09 us (1%)
    ppermute x16, waiting for transfers between devices, flipped(): return lax.ppermute(value, AXES, pairs)  30.4 us
    ppermute x16, starting transfers between devices, flipped(): return lax.ppermute(value, AXES, pairs)  17.2 us
    pallas_call x1, Pallas kernels, gram_first(): pl.pallas_call(functools.partial(gram_first_kernel, sizes, 1.0 / virtuals...  6.76 us
    pallas_call x1, Pallas kernels, gram_rest(): pl.pallas_call(functools.partial(gram_rest_kernel, sizes, 1.0 / virtuals)...  6.3 us
    pallas_call x1, Pallas kernels, half_pieces(): pl.pallas_call(functools.partial(half_first_kernel, sizes), grid_spec=plt...  3.39 us
    pallas_call x1, Pallas kernels, rest(): pl.pallas_call(functools.partial(half_rest_kernel, sizes), grid_spec=pltp...  3.11 us
    ppermute x1, waiting for transfers between devices, shards_4x8(): from_x = lax.ppermute(own, AXES, over_x)  2.7 us
    ppermute x1, starting transfers between devices, shards_4x8(): from_x = lax.ppermute(own, AXES, over_x)  2.6 us
  transfers between devices with their start and end apart: 17, of which 9 were waited for; matrix products, arithmetic and copies ran while one was open for 2% of the time, Pallas kernels for 20%

profile of v4, /device:TPU:0, one launch (start us, length us, event | category | flops | bytes accessed | tf_op | source)
XLA Modules:
  0.0 80.0 jit_solution(1636356274696248961)
XLA Ops:
  0.6 3.4 %shard_map.51 = (f32[297,16,128]{2,1,0:T(8,128)S(1)}, f32[185,16,128]{2,1,0:T(8,128)S(1)}) custom-call(s32[1]{0:T(128)} %bitcast.5.bits, bf16[160,128]{1,0:T(8,128)(2,1)} %vir.3, bf16[160,15360]{1,0:T(8,128)(2,1)} %ao.3), custom_call_target="tpu_custom_call" | custom-call | flops 314572800 | bytes 6389760 | tf_op jit(solution)/shard_map/pallas_call | solution.py:129
  4.7 1.0 %convert_element_type.287 = f16[185,16,128]{2,1,0:T(8,128)(2,1)} convert(f32[185,16,128]{2,1,0:T(8,128)S(1)} %get-tuple-element.39) | non-fusion elementwise | flops 378880 | bytes 2273280 | tf_op jit(solution)/shard_map/convert_element_type | solution.py:320
  5.8 3.1 %shard_map.50 = (f32[297,16,128]{2,1,0:T(8,128)S(1)}, f32[185,16,128]{2,1,0:T(8,128)S(1)}, f32[8,128]{1,0:T(8,128)S(1)}) custom-call(s32[1]{0:T(128)} %bitcast.4.bits, bf16[160,128]{1,0:T(8,128)(2,1)} %vir.3, bf16[160,15360]{1,0:T(8,128)(2,1)} %ao.3), custom_call_target="tpu_custom_call" | custom-call | flops 314572800 | bytes 6389760 | tf_op jit(solution)/shard_map/pallas_call | solution.py:146
  9.6 3.1 %collective-permute-start.3 = (f16[93,16,128]{2,1,0:T(8,128)(2,1)S(1)}, f16[93,16,128]{2,1,0:T(8,128)(2,1)S(1)}, u32[]{:S(2)}, u32[]{:S(2)}) collective-permute-start(f16[93,16,128]{2,1,0:T(8,128)(2,1)S(1)} %select_convert_fusion.1), channel_id=1, source_target_pairs={{0,2},{1,3},{2,0},{3,1},{4,6},{5,7},{6,4},{7,5},{8,10},{9,11},{10,... | collective-permute-start | bytes 1142792 | tf_op jit(solution)/shard_map/ppermute | solution.py:54
  12.6 1.5 %collective-permute-start.2 = (f16[149,16,128]{2,1,0:T(8,128)(2,1)S(1)}, f16[149,16,128]{2,1,0:T(8,128)(2,1)S(1)}, u32[]{:S(2)}, u32[]{:S(2)}) collective-permute-start(f16[149,16,128]{2,1,0:T(8,128)(2,1)S(1)} %select_convert_fusion), channel_id=1, source_target_pairs={{0,1},{1,0},{2,3},{3,2},{4,5},{5,4},{6,7},{7,6},{8,24},{9,25},{10,... | collective-permute-start | bytes 1830920 | tf_op jit(solution)/shard_map/ppermute | solution.py:54
  14.5 8.2 %collective-permute-done.2 = f16[149,16,128]{2,1,0:T(8,128)(2,1)S(1)} collective-permute-done((f16[149,16,128]{2,1,0:T(8,128)(2,1)S(1)}, f16[149,16,128]{2,1,0:T(8,128)(2,1)S(1)}, u32[]{:S(2)}, u32[]{:S(2)}) %collective-permute-start.2) | collective-permute-done | bytes 610336 | tf_op jit(solution)/shard_map/ppermute | solution.py:54
  23.1 1.6 %collective-permute-start.5 = (f16[47,16,128]{2,1,0:T(8,128)(2,1)S(1)}, f16[47,16,128]{2,1,0:T(8,128)(2,1)S(1)}, u32[]{:S(2)}, u32[]{:S(2)}) collective-permute-start(f16[47,16,128]{2,1,0:T(8,128)(2,1)S(1)} %select_convert_fusion.3), channel_id=1, source_target_pairs={{0,16},{1,17},{2,18},{3,19},{4,20},{5,21},{6,22},{7,23},{8,24},{9,... | collective-permute-start | bytes 577544 | tf_op jit(solution)/shard_map/ppermute | solution.py:54
  24.7 0.7 collective-permute-start.4
  25.5 6.0 %collective-permute-done.4 = f16[75,16,128]{2,1,0:T(8,128)(2,1)S(1)} collective-permute-done((f16[75,16,128]{2,1,0:T(8,128)(2,1)S(1)}, f16[75,16,128]{2,1,0:T(8,128)(2,1)S(1)}, u32[]{:S(2)}, u32[]{:S(2)}) %collective-permute-start.4) | collective-permute-done | bytes 307232 | tf_op jit(solution)/shard_map/ppermute | solution.py:54
  31.8 1.6 %collective-permute-start.7 = (f16[24,16,128]{2,1,0:T(8,128)(2,1)S(1)}, f16[24,16,128]{2,1,0:T(8,128)(2,1)S(1)}, u32[]{:S(2)}, u32[]{:S(2)}) collective-permute-start(f16[24,16,128]{2,1,0:T(8,128)(2,1)S(1)} %select_convert_fusion.6), channel_id=1, source_target_pairs={{0,1},{1,0},{2,3},{3,2},{4,5},{5,4},{6,7},{7,6},{8,9},{9,8},{10,11... | collective-permute-start | bytes 294920 | tf_op jit(solution)/shard_map/ppermute | solution.py:54
  34.0 2.5 %collective-permute-done.7 = f16[24,16,128]{2,1,0:T(8,128)(2,1)S(1)} collective-permute-done((f16[24,16,128]{2,1,0:T(8,128)(2,1)S(1)}, f16[24,16,128]{2,1,0:T(8,128)(2,1)S(1)}, u32[]{:S(2)}, u32[]{:S(2)}) %collective-permute-start.7) | collective-permute-done | bytes 98336 | tf_op jit(solution)/shard_map/ppermute | solution.py:54
  36.5 2.1 %collective-permute-done.6 = f16[38,16,128]{2,1,0:T(8,128)(2,1)S(1)} collective-permute-done((f16[38,16,128]{2,1,0:T(8,128)(2,1)S(1)}, f16[38,16,128]{2,1,0:T(8,128)(2,1)S(1)}, u32[]{:S(2)}, u32[]{:S(2)}) %collective-permute-start.6) | collective-permute-done | bytes 155680 | tf_op jit(solution)/shard_map/ppermute | solution.py:54
  39.0 2.7 %collective-permute-start.8 = (f16[61,16,128]{2,1,0:T(8,128)(2,1)S(1)}, f16[61,16,128]{2,1,0:T(8,128)(2,1)S(1)}, u32[]{:S(2)}, u32[]{:S(2)}) collective-permute-start(f16[61,16,128]{2,1,0:T(8,128)(2,1)S(1)} %pad_maximum_fusion.2), channel_id=1, source_target_pairs={{0,4},{1,5},{2,6},{3,7},{4,0},{5,1},{6,2},{7,3},{8,12},{9,13},{10,... | collective-permute-start | bytes 749576 | tf_op jit(solution)/shard_map/ppermute | solution.py:54
  41.6 7.9 %collective-permute-done.8 = f16[61,16,128]{2,1,0:T(8,128)(2,1)S(1)} collective-permute-done((f16[61,16,128]{2,1,0:T(8,128)(2,1)S(1)}, f16[61,16,128]{2,1,0:T(8,128)(2,1)S(1)}, u32[]{:S(2)}, u32[]{:S(2)}) %collective-permute-start.8) | collective-permute-done | bytes 249888 | tf_op jit(solution)/shard_map/ppermute | solution.py:54
  49.7 0.6 collective-permute-start.11
  50.4 2.6 %collective-permute-start.9 = (bf16[960,128]{1,0:T(8,128)(2,1)S(1)}, bf16[960,128]{1,0:T(8,128)(2,1)S(1)}, u32[]{:S(2)}, u32[]{:S(2)}) collective-permute-start(bf16[960,128]{1,0:T(8,128)(2,1)S(1)} %bitcast.125), channel_id=1, source_target_pairs={{0,16},{1,17},{10,26},{11,27},{20,4},{21,5},{30,14},{31,15},{2,24}... | collective-permute-start | bytes 737288 | tf_op jit(solution)/shard_map/ppermute | solution.py:356
  53.0 2.9 %collective-permute-done.11 = bf16[960,128]{1,0:T(8,128)(2,1)S(1)} collective-permute-done((bf16[960,128]{1,0:T(8,128)(2,1)S(1)}, bf16[960,128]{1,0:T(8,128)(2,1)S(1)}, u32[]{:S(2)}, u32[]{:S(2)}) %collective-permute-start.11) | collective-permute-done | bytes 245792 | tf_op jit(solution)/shard_map/ppermute | solution.py:54
  56.5 2.7 %collective-permute-done.9 = bf16[960,128]{1,0:T(8,128)(2,1)S(1)} collective-permute-done((bf16[960,128]{1,0:T(8,128)(2,1)S(1)}, bf16[960,128]{1,0:T(8,128)(2,1)S(1)}, u32[]{:S(2)}, u32[]{:S(2)}) %collective-permute-start.9) | collective-permute-done | bytes 245792 | tf_op jit(solution)/shard_map/ppermute | solution.py:356
  59.6 1.5 %collective-permute-start.12 = (bf16[960,128]{1,0:T(8,128)(2,1)S(1)}, bf16[960,128]{1,0:T(8,128)(2,1)S(1)}, u32[]{:S(2)}, u32[]{:S(2)}) collective-permute-start(bf16[960,128]{1,0:T(8,128)(2,1)S(1)} %collective-permute-done.10.near), channel_id=1, source_target_pairs={{0,1},{1,0},{2,3},{3,2},{4,5},{5,4},{6,7},{7,6},{8,9},{9,8},{10,11... | collective-permute-start | bytes 737288 | tf_op jit(solution)/shard_map/ppermute | solution.py:54
  61.5 6.8 %shard_map.52.begun = f32[3840,1920]{1,0:T(8,128)} custom-call(s32[4]{0:T(128)S(1)} %pad_add_fusion.places, bf16[1920,128]{1,0:T(8,128)(2,1)S(1)} %pad_maximum_fusion.pair, bf16[1920,128]{1,0:T(8,128)(2,1)S(1)} %pad_maximum_fusion.1.cols), custom_call_target="tpu_custom_call" | custom-call | flops 943718400 | bytes 14745600 | tf_op jit(solution)/shard_map/pallas_call | solution.py:247
  68.3 1.9 %shard_map.53 = f32[128,896]{1,0:T(8,128)S(1)} custom-call(s32[4]{0:T(128)S(1)} %pad_add_fusion.places, bf16[960,128]{1,0:T(8,128)(2,1)S(1)} %bitcast.127, bf16[960,128]{1,0:T(8,128)(2,1)S(1)} %collective-permute-done.10.near, bf16[960,128]{1,0:T(8,128)(2,1)S(1)} %slice.124.side, bf16[960,128]{1,0:T(8,128)(2,1)S(1)} %collective-permute-done.12.far, ...), custom_call_target="tpu_custom_call" | custom-call | flops 880803840 | bytes 6881280 | tf_op jit(solution)/shard_map/pallas_call | solution.py:293
  70.4 2.5 %collective-permute-start.15 = (f32[32,896]{1,0:T(8,128)S(1)}, f32[32,896]{1,0:T(8,128)S(1)}, u32[]{:S(2)}, u32[]{:S(2)}) collective-permute-start(f32[32,896]{1,0:T(8,128)S(1)} %get-tuple-element.83), channel_id=1, source_target_pairs={{0,16},{1,17},{2,18},{3,19},{4,20},{5,21},{6,22},{7,23},{8,24},{9,... | collective-permute-start | bytes 344072 | tf_op jit(solution)/shard_map/ppermute | solution.py:54
  73.0 6.3 %shard_map.54 = f32[3840,1920]{1,0:T(8,128)} custom-call(s32[4]{0:T(128)S(1)} %pad_add_fusion.places, bf16[960,128]{1,0:T(8,128)(2,1)S(1)} %collective-permute-done.10.near, bf16[960,128]{1,0:T(8,128)(2,1)S(1)} %collective-permute-done.12.far, bf16[1920,128]{1,0:T(8,128)(2,1)S(1)} %pad_maximum_fusion.1.cols, ...), custom_call_target="tpu_custom_call", output_to_operand_aliasing={{}: (4, {})} | custom-call | flops 943718400 | bytes 14745600 | tf_op jit(solution)/shard_map/pallas_call | solution.py:266
  79.3 0.7 fusion.6
  (76 shorter events, 5.1 us)
Async XLA Ops:
  4.2 4.7 %collective-permute-start = (f16[297,16,128]{2,1,0:T(8,128)(2,1)S(1)}, f16[297,16,128]{2,1,0:T(8,128)(2,1)S(1)}, u32[]{:S(2)}, u32[]{:S(2)}) collective-permute-start(f16[297,16,128]{2,1,0:T(8,128)(2,1)S(1)} %convert_element_type.284), channel_id=1, source_target_pairs={{0,8},{1,9},{2,10},{3,11},{4,12},{5,13},{6,14},{7,15},{8,0},{9,1},... | collective-permute-start | bytes 3649544 | tf_op jit(solution)/shard_map/ppermute | solution.py:54
  5.7 3.3 %collective-permute-start.1 = (f16[185,16,128]{2,1,0:T(8,128)(2,1)}, f16[185,16,128]{2,1,0:T(8,128)(2,1)S(1)}, u32[]{:S(2)}, u32[]{:S(2)}) collective-permute-start(f16[185,16,128]{2,1,0:T(8,128)(2,1)} %convert_element_type.287), channel_id=1, source_target_pairs={{0,8},{1,9},{2,10},{3,11},{4,12},{5,13},{6,14},{7,15},{8,0},{9,1},... | collective-permute-start | bytes 2273288 | tf_op jit(solution)/shard_map/ppermute | solution.py:54
  9.6 13.2 %collective-permute-start.3 = (f16[93,16,128]{2,1,0:T(8,128)(2,1)S(1)}, f16[93,16,128]{2,1,0:T(8,128)(2,1)S(1)}, u32[]{:S(2)}, u32[]{:S(2)}) collective-permute-start(f16[93,16,128]{2,1,0:T(8,128)(2,1)S(1)} %select_convert_fusion.1), channel_id=1, source_target_pairs={{0,2},{1,3},{2,0},{3,1},{4,6},{5,7},{6,4},{7,5},{8,10},{9,11},{10,... | collective-permute-start | bytes 1142792 | tf_op jit(solution)/shard_map/ppermute | solution.py:54
  12.6 10.1 %collective-permute-start.2 = (f16[149,16,128]{2,1,0:T(8,128)(2,1)S(1)}, f16[149,16,128]{2,1,0:T(8,128)(2,1)S(1)}, u32[]{:S(2)}, u32[]{:S(2)}) collective-permute-start(f16[149,16,128]{2,1,0:T(8,128)(2,1)S(1)} %select_convert_fusion), channel_id=1, source_target_pairs={{0,1},{1,0},{2,3},{3,2},{4,5},{5,4},{6,7},{7,6},{8,24},{9,25},{10,... | collective-permute-start | bytes 1830920 | tf_op jit(solution)/shard_map/ppermute | solution.py:54
  23.1 8.4 %collective-permute-start.5 = (f16[47,16,128]{2,1,0:T(8,128)(2,1)S(1)}, f16[47,16,128]{2,1,0:T(8,128)(2,1)S(1)}, u32[]{:S(2)}, u32[]{:S(2)}) collective-permute-start(f16[47,16,128]{2,1,0:T(8,128)(2,1)S(1)} %select_convert_fusion.3), channel_id=1, source_target_pairs={{0,16},{1,17},{2,18},{3,19},{4,20},{5,21},{6,22},{7,23},{8,24},{9,... | collective-permute-start | bytes 577544 | tf_op jit(solution)/shard_map/ppermute | solution.py:54
  24.7 6.9 %collective-permute-start.4 = (f16[75,16,128]{2,1,0:T(8,128)(2,1)S(1)}, f16[75,16,128]{2,1,0:T(8,128)(2,1)S(1)}, u32[]{:S(2)}, u32[]{:S(2)}) collective-permute-start(f16[75,16,128]{2,1,0:T(8,128)(2,1)S(1)} %select_convert_fusion.2), channel_id=1, source_target_pairs={{0,2},{1,3},{2,0},{3,1},{4,6},{5,7},{6,4},{7,5},{8,9},{9,8},{10,11... | collective-permute-start | bytes 921608 | tf_op jit(solution)/shard_map/ppermute | solution.py:54
  31.8 4.7 %collective-permute-start.7 = (f16[24,16,128]{2,1,0:T(8,128)(2,1)S(1)}, f16[24,16,128]{2,1,0:T(8,128)(2,1)S(1)}, u32[]{:S(2)}, u32[]{:S(2)}) collective-permute-start(f16[24,16,128]{2,1,0:T(8,128)(2,1)S(1)} %select_convert_fusion.6), channel_id=1, source_target_pairs={{0,1},{1,0},{2,3},{3,2},{4,5},{5,4},{6,7},{7,6},{8,9},{9,8},{10,11... | collective-permute-start | bytes 294920 | tf_op jit(solution)/shard_map/ppermute | solution.py:54
  33.4 5.2 %collective-permute-start.6 = (f16[38,16,128]{2,1,0:T(8,128)(2,1)S(1)}, f16[38,16,128]{2,1,0:T(8,128)(2,1)S(1)}, u32[]{:S(2)}, u32[]{:S(2)}) collective-permute-start(f16[38,16,128]{2,1,0:T(8,128)(2,1)S(1)} %select_convert_fusion.4), channel_id=1, source_target_pairs={{0,16},{1,17},{2,18},{3,19},{4,20},{5,21},{6,22},{7,23},{8,10},{9,... | collective-permute-start | bytes 466952 | tf_op jit(solution)/shard_map/ppermute | solution.py:54
  39.0 10.6 %collective-permute-start.8 = (f16[61,16,128]{2,1,0:T(8,128)(2,1)S(1)}, f16[61,16,128]{2,1,0:T(8,128)(2,1)S(1)}, u32[]{:S(2)}, u32[]{:S(2)}) collective-permute-start(f16[61,16,128]{2,1,0:T(8,128)(2,1)S(1)} %pad_maximum_fusion.2), channel_id=1, source_target_pairs={{0,4},{1,5},{2,6},{3,7},{4,0},{5,1},{6,2},{7,3},{8,12},{9,13},{10,... | collective-permute-start | bytes 749576 | tf_op jit(solution)/shard_map/ppermute | solution.py:54
  49.7 6.3 %collective-permute-start.11 = (bf16[960,128]{1,0:T(8,128)(2,1)S(1)}, bf16[960,128]{1,0:T(8,128)(2,1)S(1)}, u32[]{:S(2)}, u32[]{:S(2)}) collective-permute-start(bf16[960,128]{1,0:T(8,128)(2,1)S(1)} %bitcast.123), channel_id=1, source_target_pairs={{0,1},{1,0},{2,3},{3,2},{4,5},{5,4},{6,7},{7,6},{8,9},{9,8},{10,11... | collective-permute-start | bytes 737288 | tf_op jit(solution)/shard_map/ppermute | solution.py:54
  50.3 6.2 %collective-permute-start.10 = (bf16[960,128]{1,0:T(8,128)(2,1)S(1)}, bf16[960,128]{1,0:T(8,128)(2,1)S(1)}, u32[]{:S(2)}, u32[]{:S(2)}) collective-permute-start(bf16[960,128]{1,0:T(8,128)(2,1)S(1)} %bitcast.124), channel_id=1, source_target_pairs={{0,2},{1,3},{2,0},{3,1},{4,6},{5,7},{6,4},{7,5},{8,10},{9,11},{10,... | collective-permute-start | bytes 737288 | tf_op jit(solution)/shard_map/ppermute | solution.py:54
  50.4 8.7 %collective-permute-start.9 = (bf16[960,128]{1,0:T(8,128)(2,1)S(1)}, bf16[960,128]{1,0:T(8,128)(2,1)S(1)}, u32[]{:S(2)}, u32[]{:S(2)}) collective-permute-start(bf16[960,128]{1,0:T(8,128)(2,1)S(1)} %bitcast.125), channel_id=1, source_target_pairs={{0,16},{1,17},{10,26},{11,27},{20,4},{21,5},{30,14},{31,15},{2,24}... | collective-permute-start | bytes 737288 | tf_op jit(solution)/shard_map/ppermute | solution.py:356
  59.4 1.9 %collective-permute-start.13 = (bf16[1920,128]{1,0:T(8,128)(2,1)S(1)}, bf16[1920,128]{1,0:T(8,128)(2,1)S(1)}, u32[]{:S(2)}, u32[]{:S(2)}) collective-permute-start(bf16[1920,128]{1,0:T(8,128)(2,1)S(1)} %maximum_select_fusion), channel_id=1, source_target_pairs={{0,8},{1,9},{2,10},{3,11},{4,12},{5,13},{6,14},{7,15},{8,0},{9,1},... | collective-permute-start | bytes 1474568 | tf_op jit(solution)/shard_map/ppermute | solution.py:54
  59.6 8.7 %collective-permute-start.12 = (bf16[960,128]{1,0:T(8,128)(2,1)S(1)}, bf16[960,128]{1,0:T(8,128)(2,1)S(1)}, u32[]{:S(2)}, u32[]{:S(2)}) collective-permute-start(bf16[960,128]{1,0:T(8,128)(2,1)S(1)} %collective-permute-done.10.near), channel_id=1, source_target_pairs={{0,1},{1,0},{2,3},{3,2},{4,5},{5,4},{6,7},{7,6},{8,9},{9,8},{10,11... | collective-permute-start | bytes 737288 | tf_op jit(solution)/shard_map/ppermute | solution.py:54
  61.4 6.8 %slice-start = ((s8[6881280]{0:T(1024)(128)(4,1)}), s8[4194304]{0:T(1024)(128)(4,1)S(1)}, s32[]{:S(2)}) async-start(s8[6881280]{0:T(1024)(128)(4,1)} %bitcast.121), calls=%async_computation | async-start | bytes 8388608
  61.5 6.8 %slice-start.1 = ((s8[6881280]{0:T(1024)(128)(4,1)}), s8[2686976]{0:T(1024)(128)(4,1)S(1)}, s32[]{:S(2)}) async-start(s8[6881280]{0:T(1024)(128)(4,1)} %bitcast.121), calls=%async_computation.1 | async-start | bytes 5373952
  70.2 9.0 %collective-permute-start.16 = (f32[32,896]{1,0:T(8,128)S(1)}, f32[32,896]{1,0:T(8,128)S(1)}, u32[]{:S(2)}, u32[]{:S(2)}) collective-permute-start(f32[32,896]{1,0:T(8,128)S(1)} %get-tuple-element.82), channel_id=1, source_target_pairs={{0,8},{1,9},{2,10},{3,11},{4,12},{5,13},{6,14},{7,15},{8,0},{9,1},... | collective-permute-start | bytes 344072 | tf_op jit(solution)/shard_map/ppermute | solution.py:54
  70.4 8.9 %collective-permute-start.15 = (f32[32,896]{1,0:T(8,128)S(1)}, f32[32,896]{1,0:T(8,128)S(1)}, u32[]{:S(2)}, u32[]{:S(2)}) collective-permute-start(f32[32,896]{1,0:T(8,128)S(1)} %get-tuple-element.83), channel_id=1, source_target_pairs={{0,16},{1,17},{2,18},{3,19},{4,20},{5,21},{6,22},{7,23},{8,24},{9,... | collective-permute-start | bytes 344072 | tf_op jit(solution)/shard_map/ppermute | solution.py:54
  73.0 6.3 %collective-permute-start.14 = (f32[32,896]{1,0:T(8,128)S(1)}, f32[32,896]{1,0:T(8,128)S(1)}, u32[]{:S(2)}, u32[]{:S(2)}) collective-permute-start(f32[32,896]{1,0:T(8,128)S(1)} %get-tuple-element.84), channel_id=1, source_target_pairs={{0,24},{1,25},{2,26},{3,27},{4,28},{5,29},{6,30},{7,31},{8,16},{9,... | collective-permute-start | bytes 344072 | tf_op jit(solution)/shard_map/ppermute | solution.py:54

commit v5 on v4

--- a/solution.py
+++ b/solution.py
@@ -214,7 +214,7 @@
     return max(b - a for cuts in steps_of(sizes) for a, b in cuts)
 
 
-def gram_steps(sizes, scale, blocks, cols, out, buffers, sems):
+def gram_steps(sizes, scale, blocks, cols, out, buffers, sems, beside=()):
     copies = []
     cuts = steps_of(sizes)
     for ref, at, height, start in blocks:
@@ -227,13 +227,36 @@
             where = pl.ds(pl.multiple_of(start + a, TILE), b - a)
             copies.append(pltpu.make_async_copy(buffers.at[slot, pl.ds(0, b - a)], out.at[where, :], sems.at[slot]))
             copies[n].start()
+            if n < len(beside):
+                beside[n]()
     for copy in copies[-SLOTS:]:
         copy.wait()
 
 
-def gram_first_kernel(sizes, scale, places, pair, cols, out, buffers, sems):
+def gram_first_kernel(sizes, scale, places, pair, near, cols, naf, out, partial, ahead, buffers, rows_in, sems, naf_sems):
     blocks = blocks_of(sizes, (places[0], places[2]), pair, 0, 2)
-    gram_steps(sizes, scale, blocks, cols, out, buffers, sems)
+    terms, loads, at = [], [], 0
+    for ref, first, height, row in blocks + blocks_of(sizes, places, near, 1, 1):
+        here = rows_in.at[pl.ds(at, height), :]
+        loads.append(pltpu.make_async_copy(naf.at[pl.ds(row, height), :], here, naf_sems.at[len(loads)]))
+        terms.append((ref, first, at, height))
+        at += height
+    for _, first, height, row in blocks_of(sizes, places, ahead, 3, 1):
+        here = ahead.at[pl.ds(first, height), :]
+        loads.append(pltpu.make_async_copy(naf.at[pl.ds(row, height), :], here, naf_sems.at[len(loads)]))
+    for load in loads:
+        load.start()
+
+    def add(n):
+        ref, first, at, height = terms[n]
+        loads[n].wait()
+        term = contract_first(ref[first : first + height], rows_in[at : at + height])
+        partial[...] = term if n == 0 else partial[...] + term
+
+    beside = [functools.partial(add, n) for n in range(len(terms))]
+    gram_steps(sizes, scale, blocks, cols, out, buffers, sems, beside)
+    for load in loads[len(terms) :]:
+        load.wait()
 
 
 def gram_rest_kernel(sizes, scale, places, near, far, cols, begun, out, buffers, sems):
@@ -241,22 +264,33 @@
     gram_steps(sizes, scale, blocks, cols, out, buffers, sems)
 
 
-def gram_first(sizes, places, pair, cols):
+def gram_first(sizes, places, pair, near, cols, naf_vectors):
     in_vmem = pl.BlockSpec(memory_space=pltpu.VMEM)
-    block, virtuals = pair.shape[0] // 2, pair.shape[1]
+    in_hbm = pl.BlockSpec(memory_space=pl.ANY)
+    block, virtuals = near.shape
+    nnaf = naf_vectors.shape[1]
     return pl.pallas_call(
         functools.partial(gram_first_kernel, sizes, 1.0 / virtuals),
         grid_spec=pltpu.PrefetchScalarGridSpec(
             num_scalar_prefetch=1,
             grid=(),
-            in_specs=[in_vmem] * 2,
-            out_specs=pl.BlockSpec(memory_space=pl.ANY),
-            scratch_shapes=[pltpu.VMEM((SLOTS, step_rows(sizes), 2 * block), jnp.float32), pltpu.SemaphoreType.DMA((SLOTS,))],
+            in_specs=[in_vmem] * 3 + [in_hbm],
+            out_specs=[in_hbm, in_vmem, in_vmem],
+            scratch_shapes=[
+                pltpu.VMEM((SLOTS, step_rows(sizes), 2 * block), jnp.float32),
+                pltpu.VMEM((3 * block, nnaf), jnp.bfloat16),
+                pltpu.SemaphoreType.DMA((SLOTS,)),
+                pltpu.SemaphoreType.DMA((8,)),
+            ],
         ),
-        out_shape=jax.ShapeDtypeStruct((4 * block, 2 * block), jnp.float32),
-        compiler_params=pltpu.CompilerParams(vmem_limit_bytes=VMEM_LIMIT),
+        out_shape=[
+            jax.ShapeDtypeStruct((4 * block, 2 * block), jnp.float32),
+            pltpu.VMEM((virtuals, nnaf), jnp.float32),
+            pltpu.VMEM((block, nnaf), jnp.bfloat16),
+        ],
+        compiler_params=pltpu.CompilerParams(vmem_limit_bytes=18 * 2**20),
         cost_estimate=pl.CostEstimate(flops=8 * block * block * virtuals, bytes_accessed=16 * block * block, transcendentals=0),
-    )(places, pair, cols)
+    )(places, pair, near, cols, pltpu.with_memory_space_constraint(naf_vectors, pltpu.HBM))
 
 
 def gram_rest(sizes, places, near, far, cols, begun):
@@ -279,30 +313,20 @@
     )(places, near, far, cols, begun)
 
 
-def naf_kernel(sizes, places, own, near, side, far, naf, out, panel):
-    for n, block in enumerate((own, near, side, far)):
-        for ref, at, rows, row in blocks_of(sizes, places, block, n, 1):
-            panel[pl.ds(row, rows), :] = ref[at : at + rows]
-    out[...] = contract_first(panel[...], naf[...])
-
-
-def project(sizes, places, own, near, side, far, naf_vectors):
-    virtuals = own.shape[1]
-    rows, nnaf = naf_vectors.shape
+def naf_kernel(far, ahead, before, out):
+    out[...] = before[...] + contract_first(far[...], ahead[...])
+
+
+def project(far, ahead, before):
     in_vmem = pl.BlockSpec(memory_space=pltpu.VMEM)
     return pl.pallas_call(
-        functools.partial(naf_kernel, sizes),
-        grid_spec=pltpu.PrefetchScalarGridSpec(
-            num_scalar_prefetch=1,
-            grid=(),
-            in_specs=[in_vmem] * 5,
-            out_specs=in_vmem,
-            scratch_shapes=[pltpu.VMEM((rows, virtuals), jnp.bfloat16)],
-        ),
-        out_shape=pltpu.VMEM((virtuals, nnaf), jnp.float32),
-        compiler_params=pltpu.CompilerParams(vmem_limit_bytes=10 * 2**20),
-        cost_estimate=pl.CostEstimate(flops=2 * rows * nnaf * virtuals, bytes_accessed=2 * rows * nnaf, transcendentals=0),
-    )(places, own, near, side, far, naf_vectors)
+        naf_kernel,
+        in_specs=[in_vmem] * 3,
+        out_specs=in_vmem,
+        out_shape=pltpu.VMEM(before.shape, jnp.float32),
+        compiler_params=pltpu.CompilerParams(vmem_limit_bytes=5 * 2**20),
+        cost_estimate=pl.CostEstimate(flops=2 * far.shape[0] * before.size, bytes_accessed=0, transcendentals=0),
+    )(far, ahead, before)
 
 
 def shards_4x8(ao_ints, vir_coef, naf_vectors):
@@ -368,9 +392,9 @@
     cuts = (0, sizes[0]), (sizes[0], block)
     columns = jnp.concatenate([half[a:b] for a, b in cuts for half in halves], axis=0)
 
-    gram = gram_first(sizes, places, pair, columns)
+    gram, partial, ahead = gram_first(sizes, places, pair, near, columns, naf_vectors)
     far, gram = lax.optimization_barrier((far, gram))
-    partial = project(sizes, places, own, near, pair[block:], far, naf_vectors)
+    partial = project(far, ahead, partial)
     partial = partial.reshape(4, virtuals // 4, -1)
     share = lambda flip: lax.dynamic_index_in_dim(partial, row_index ^ flip, 0, keepdims=False)
     parts = [flipped(share(flip), (flip, 0), (flip, 0)) for flip in (3, 2, 1)]

time: 80.2 us -> 79.6 us (level)
    pallas_call x1, Pallas kernels: 1.88 us -> 0.48 us  [project(): pl.pallas_call(naf_kernel, in_specs=[in_vmem] * 3, out_specs=in_vmem, out...]
    pallas_call x1, Pallas kernels: 6.76 us -> 7.67 us  [gram_first(): pl.pallas_call(functools.partial(gram_first_kernel, sizes, 1.0 / virtuals...]
  transfers between devices with their start and end apart: 17 -> 17, of which waited for: 9 -> 9; matrix products, arithmetic and copies ran while one was open for 2% -> 2% of each run, Pallas kernels for 20% -> 21%
where the time goes in v5:
time: 79.6 us; the launch traced here: 79.5 us
  waiting for transfers between devices  33.1 us (42%)
  Pallas kernels  21 us (26%)
  starting transfers between devices  19.8 us (25%)
  other arithmetic  4.45 us (6%)
  between operations  1.05 us (1%)
    ppermute x16, waiting for transfers between devices, flipped(): return lax.ppermute(value, AXES, pairs)  30.4 us
    ppermute x16, starting transfers between devices, flipped(): return lax.ppermute(value, AXES, pairs)  17.2 us
    pallas_call x1, Pallas kernels, gram_first(): pl.pallas_call(functools.partial(gram_first_kernel, sizes, 1.0 / virtuals...  7.67 us
    pallas_call x1, Pallas kernels, gram_rest(): pl.pallas_call(functools.partial(gram_rest_kernel, sizes, 1.0 / virtuals)...  6.31 us
    pallas_call x1, Pallas kernels, half_pieces(): pl.pallas_call(functools.partial(half_first_kernel, sizes), grid_spec=plt...  3.39 us
    pallas_call x1, Pallas kernels, rest(): pl.pallas_call(functools.partial(half_rest_kernel, sizes), grid_spec=pltp...  3.11 us
    ppermute x1, waiting for transfers between devices, shards_4x8(): from_x = lax.ppermute(own, AXES, over_x)  2.7 us
    ppermute x1, starting transfers between devices, shards_4x8(): from_x = lax.ppermute(own, AXES, over_x)  2.6 us
  transfers between devices with their start and end apart: 17, of which 9 were waited for; matrix products, arithmetic and copies ran while one was open for 2% of the time, Pallas kernels for 21%

profile of v5, /device:TPU:0, one launch (start us, length us, event | category | flops | bytes accessed | tf_op | source)
XLA Modules:
  0.0 79.5 jit_solution(13390965975066861198)
XLA Ops:
  0.6 3.4 %shard_map.51 = (f32[297,16,128]{2,1,0:T(8,128)S(1)}, f32[185,16,128]{2,1,0:T(8,128)S(1)}) custom-call(s32[1]{0:T(128)} %bitcast.1.bits, bf16[160,128]{1,0:T(8,128)(2,1)} %vir.3, bf16[160,15360]{1,0:T(8,128)(2,1)} %ao.3), custom_call_target="tpu_custom_call" | custom-call | flops 314572800 | bytes 6389760 | tf_op jit(solution)/shard_map/pallas_call | solution.py:129
  4.7 1.0 %convert_element_type.287 = f16[185,16,128]{2,1,0:T(8,128)(2,1)} convert(f32[185,16,128]{2,1,0:T(8,128)S(1)} %get-tuple-element.42) | non-fusion elementwise | flops 378880 | bytes 2273280 | tf_op jit(solution)/shard_map/convert_element_type | solution.py:344
  5.8 3.1 %shard_map.50 = (f32[297,16,128]{2,1,0:T(8,128)S(1)}, f32[185,16,128]{2,1,0:T(8,128)S(1)}, f32[8,128]{1,0:T(8,128)S(1)}) custom-call(s32[1]{0:T(128)} %bitcast.bits, bf16[160,128]{1,0:T(8,128)(2,1)} %vir.3, bf16[160,15360]{1,0:T(8,128)(2,1)} %ao.3), custom_call_target="tpu_custom_call" | custom-call | flops 314572800 | bytes 6389760 | tf_op jit(solution)/shard_map/pallas_call | solution.py:146
  9.6 3.1 %collective-permute-start.3 = (f16[93,16,128]{2,1,0:T(8,128)(2,1)S(1)}, f16[93,16,128]{2,1,0:T(8,128)(2,1)S(1)}, u32[]{:S(2)}, u32[]{:S(2)}) collective-permute-start(f16[93,16,128]{2,1,0:T(8,128)(2,1)S(1)} %select_convert_fusion.1), channel_id=1, source_target_pairs={{0,2},{1,3},{2,0},{3,1},{4,6},{5,7},{6,4},{7,5},{8,10},{9,11},{10,... | collective-permute-start | bytes 1142792 | tf_op jit(solution)/shard_map/ppermute | solution.py:54
  12.6 1.5 %collective-permute-start.2 = (f16[149,16,128]{2,1,0:T(8,128)(2,1)S(1)}, f16[149,16,128]{2,1,0:T(8,128)(2,1)S(1)}, u32[]{:S(2)}, u32[]{:S(2)}) collective-permute-start(f16[149,16,128]{2,1,0:T(8,128)(2,1)S(1)} %select_convert_fusion), channel_id=1, source_target_pairs={{0,1},{1,0},{2,3},{3,2},{4,5},{5,4},{6,7},{7,6},{8,24},{9,25},{10,... | collective-permute-start | bytes 1830920 | tf_op jit(solution)/shard_map/ppermute | solution.py:54
  14.5 8.2 %collective-permute-done.2 = f16[149,16,128]{2,1,0:T(8,128)(2,1)S(1)} collective-permute-done((f16[149,16,128]{2,1,0:T(8,128)(2,1)S(1)}, f16[149,16,128]{2,1,0:T(8,128)(2,1)S(1)}, u32[]{:S(2)}, u32[]{:S(2)}) %collective-permute-start.2) | collective-permute-done | bytes 610336 | tf_op jit(solution)/shard_map/ppermute | solution.py:54
  23.1 1.6 %collective-permute-start.5 = (f16[47,16,128]{2,1,0:T(8,128)(2,1)S(1)}, f16[47,16,128]{2,1,0:T(8,128)(2,1)S(1)}, u32[]{:S(2)}, u32[]{:S(2)}) collective-permute-start(f16[47,16,128]{2,1,0:T(8,128)(2,1)S(1)} %select_convert_fusion.3), channel_id=1, source_target_pairs={{0,16},{1,17},{2,18},{3,19},{4,20},{5,21},{6,22},{7,23},{8,24},{9,... | collective-permute-start | bytes 577544 | tf_op jit(solution)/shard_map/ppermute | solution.py:54
  24.7 0.7 collective-permute-start.4
  25.5 6.0 %collective-permute-done.4 = f16[75,16,128]{2,1,0:T(8,128)(2,1)S(1)} collective-permute-done((f16[75,16,128]{2,1,0:T(8,128)(2,1)S(1)}, f16[75,16,128]{2,1,0:T(8,128)(2,1)S(1)}, u32[]{:S(2)}, u32[]{:S(2)}) %collective-permute-start.4) | collective-permute-done | bytes 307232 | tf_op jit(solution)/shard_map/ppermute | solution.py:54
  31.8 1.6 %collective-permute-start.7 = (f16[24,16,128]{2,1,0:T(8,128)(2,1)S(1)}, f16[24,16,128]{2,1,0:T(8,128)(2,1)S(1)}, u32[]{:S(2)}, u32[]{:S(2)}) collective-permute-start(f16[24,16,128]{2,1,0:T(8,128)(2,1)S(1)} %select_convert_fusion.6), channel_id=1, source_target_pairs={{0,1},{1,0},{2,3},{3,2},{4,5},{5,4},{6,7},{7,6},{8,9},{9,8},{10,11... | collective-permute-start | bytes 294920 | tf_op jit(solution)/shard_map/ppermute | solution.py:54
  33.4 0.5 collective-permute-start.6
  34.0 2.5 %collective-permute-done.7 = f16[24,16,128]{2,1,0:T(8,128)(2,1)S(1)} collective-permute-done((f16[24,16,128]{2,1,0:T(8,128)(2,1)S(1)}, f16[24,16,128]{2,1,0:T(8,128)(2,1)S(1)}, u32[]{:S(2)}, u32[]{:S(2)}) %collective-permute-start.7) | collective-permute-done | bytes 98336 | tf_op jit(solution)/shard_map/ppermute | solution.py:54
  36.5 2.1 %collective-permute-done.6 = f16[38,16,128]{2,1,0:T(8,128)(2,1)S(1)} collective-permute-done((f16[38,16,128]{2,1,0:T(8,128)(2,1)S(1)}, f16[38,16,128]{2,1,0:T(8,128)(2,1)S(1)}, u32[]{:S(2)}, u32[]{:S(2)}) %collective-permute-start.6) | collective-permute-done | bytes 155680 | tf_op jit(solution)/shard_map/ppermute | solution.py:54
  39.0 2.7 %collective-permute-start.8 = (f16[61,16,128]{2,1,0:T(8,128)(2,1)S(1)}, f16[61,16,128]{2,1,0:T(8,128)(2,1)S(1)}, u32[]{:S(2)}, u32[]{:S(2)}) collective-permute-start(f16[61,16,128]{2,1,0:T(8,128)(2,1)S(1)} %pad_maximum_fusion.2), channel_id=1, source_target_pairs={{0,4},{1,5},{2,6},{3,7},{4,0},{5,1},{6,2},{7,3},{8,12},{9,13},{10,... | collective-permute-start | bytes 749576 | tf_op jit(solution)/shard_map/ppermute | solution.py:54
  41.6 7.9 %collective-permute-done.8 = f16[61,16,128]{2,1,0:T(8,128)(2,1)S(1)} collective-permute-done((f16[61,16,128]{2,1,0:T(8,128)(2,1)S(1)}, f16[61,16,128]{2,1,0:T(8,128)(2,1)S(1)}, u32[]{:S(2)}, u32[]{:S(2)}) %collective-permute-start.8) | collective-permute-done | bytes 249888 | tf_op jit(solution)/shard_map/ppermute | solution.py:54
  49.7 0.6 collective-permute-start.11
  50.4 2.6 %collective-permute-start.9 = (bf16[960,128]{1,0:T(8,128)(2,1)S(1)}, bf16[960,128]{1,0:T(8,128)(2,1)S(1)}, u32[]{:S(2)}, u32[]{:S(2)}) collective-permute-start(bf16[960,128]{1,0:T(8,128)(2,1)S(1)} %bitcast.125), channel_id=1, source_target_pairs={{0,16},{1,17},{10,26},{11,27},{20,4},{21,5},{30,14},{31,15},{2,24}... | collective-permute-start | bytes 737288 | tf_op jit(solution)/shard_map/ppermute | solution.py:380
  53.0 2.9 %collective-permute-done.11 = bf16[960,128]{1,0:T(8,128)(2,1)S(1)} collective-permute-done((bf16[960,128]{1,0:T(8,128)(2,1)S(1)}, bf16[960,128]{1,0:T(8,128)(2,1)S(1)}, u32[]{:S(2)}, u32[]{:S(2)}) %collective-permute-start.11) | collective-permute-done | bytes 245792 | tf_op jit(solution)/shard_map/ppermute | solution.py:54
  56.5 2.7 %collective-permute-done.9 = bf16[960,128]{1,0:T(8,128)(2,1)S(1)} collective-permute-done((bf16[960,128]{1,0:T(8,128)(2,1)S(1)}, bf16[960,128]{1,0:T(8,128)(2,1)S(1)}, u32[]{:S(2)}, u32[]{:S(2)}) %collective-permute-start.9) | collective-permute-done | bytes 245792 | tf_op jit(solution)/shard_map/ppermute | solution.py:380
  59.6 1.5 %collective-permute-start.12 = (bf16[960,128]{1,0:T(8,128)(2,1)S(1)}, bf16[960,128]{1,0:T(8,128)(2,1)S(1)}, u32[]{:S(2)}, u32[]{:S(2)}) collective-permute-start(bf16[960,128]{1,0:T(8,128)(2,1)S(1)} %collective-permute-done.10.near), channel_id=1, source_target_pairs={{0,1},{1,0},{2,3},{3,2},{4,5},{5,4},{6,7},{7,6},{8,9},{9,8},{10,11... | collective-permute-start | bytes 737288 | tf_op jit(solution)/shard_map/ppermute | solution.py:54
  61.5 7.7 %shard_map.52 = (f32[3840,1920]{1,0:T(8,128)}, f32[128,896]{1,0:T(8,128)S(1)}, bf16[960,896]{1,0:T(8,128)(2,1)S(1)}) custom-call(s32[4]{0:T(128)S(1)} %pad_add_fusion.places, bf16[1920,128]{1,0:T(8,128)(2,1)S(1)} %pad_maximum_fusion.pair, bf16[960,128]{1,0:T(8,128)(2,1)S(1)} %collective-permute-done.10.near, bf16[1920,128]{1,0:T(8,128)(2,1)S(1)} %pad_maximum_fusion.1.cols, ...), custom_call_target="tpu_custom_call" | custom-call | flops 943718400 | bytes 14745600 | tf_op jit(solution)/shard_map/pallas_call | solution.py:272
  69.9 2.5 %collective-permute-start.15 = (f32[32,896]{1,0:T(8,128)S(1)}, f32[32,896]{1,0:T(8,128)S(1)}, u32[]{:S(2)}, u32[]{:S(2)}) collective-permute-start(f32[32,896]{1,0:T(8,128)S(1)} %get-tuple-element.89), channel_id=1, source_target_pairs={{0,16},{1,17},{2,18},{3,19},{4,20},{5,21},{6,22},{7,23},{8,24},{9,... | collective-permute-start | bytes 344072 | tf_op jit(solution)/shard_map/ppermute | solution.py:54
  72.4 6.3 %shard_map.54 = f32[3840,1920]{1,0:T(8,128)} custom-call(s32[4]{0:T(128)S(1)} %pad_add_fusion.places, bf16[960,128]{1,0:T(8,128)(2,1)S(1)} %collective-permute-done.10.near, bf16[960,128]{1,0:T(8,128)(2,1)S(1)} %collective-permute-done.12.far, bf16[1920,128]{1,0:T(8,128)(2,1)S(1)} %pad_maximum_fusion.1.cols, ...), custom_call_target="tpu_custom_call", output_to_operand_aliasing={{}: (4, {})} | custom-call | flops 943718400 | bytes 14745600 | tf_op jit(solution)/shard_map/pallas_call | solution.py:300
  78.8 0.7 fusion.6
  (70 shorter events, 5.0 us)
Async XLA Ops:
  4.2 4.7 %collective-permute-start = (f16[297,16,128]{2,1,0:T(8,128)(2,1)S(1)}, f16[297,16,128]{2,1,0:T(8,128)(2,1)S(1)}, u32[]{:S(2)}, u32[]{:S(2)}) collective-permute-start(f16[297,16,128]{2,1,0:T(8,128)(2,1)S(1)} %convert_element_type.284), channel_id=1, source_target_pairs={{0,8},{1,9},{2,10},{3,11},{4,12},{5,13},{6,14},{7,15},{8,0},{9,1},... | collective-permute-start | bytes 3649544 | tf_op jit(solution)/shard_map/ppermute | solution.py:54
  5.7 3.3 %collective-permute-start.1 = (f16[185,16,128]{2,1,0:T(8,128)(2,1)}, f16[185,16,128]{2,1,0:T(8,128)(2,1)S(1)}, u32[]{:S(2)}, u32[]{:S(2)}) collective-permute-start(f16[185,16,128]{2,1,0:T(8,128)(2,1)} %convert_element_type.287), channel_id=1, source_target_pairs={{0,8},{1,9},{2,10},{3,11},{4,12},{5,13},{6,14},{7,15},{8,0},{9,1},... | collective-permute-start | bytes 2273288 | tf_op jit(solution)/shard_map/ppermute | solution.py:54
  9.6 13.2 %collective-permute-start.3 = (f16[93,16,128]{2,1,0:T(8,128)(2,1)S(1)}, f16[93,16,128]{2,1,0:T(8,128)(2,1)S(1)}, u32[]{:S(2)}, u32[]{:S(2)}) collective-permute-start(f16[93,16,128]{2,1,0:T(8,128)(2,1)S(1)} %select_convert_fusion.1), channel_id=1, source_target_pairs={{0,2},{1,3},{2,0},{3,1},{4,6},{5,7},{6,4},{7,5},{8,10},{9,11},{10,... | collective-permute-start | bytes 1142792 | tf_op jit(solution)/shard_map/ppermute | solution.py:54
  12.6 10.1 %collective-permute-start.2 = (f16[149,16,128]{2,1,0:T(8,128)(2,1)S(1)}, f16[149,16,128]{2,1,0:T(8,128)(2,1)S(1)}, u32[]{:S(2)}, u32[]{:S(2)}) collective-permute-start(f16[149,16,128]{2,1,0:T(8,128)(2,1)S(1)} %select_convert_fusion), channel_id=1, source_target_pairs={{0,1},{1,0},{2,3},{3,2},{4,5},{5,4},{6,7},{7,6},{8,24},{9,25},{10,... | collective-permute-start | bytes 1830920 | tf_op jit(solution)/shard_map/ppermute | solution.py:54
  23.1 8.4 %collective-permute-start.5 = (f16[47,16,128]{2,1,0:T(8,128)(2,1)S(1)}, f16[47,16,128]{2,1,0:T(8,128)(2,1)S(1)}, u32[]{:S(2)}, u32[]{:S(2)}) collective-permute-start(f16[47,16,128]{2,1,0:T(8,128)(2,1)S(1)} %select_convert_fusion.3), channel_id=1, source_target_pairs={{0,16},{1,17},{2,18},{3,19},{4,20},{5,21},{6,22},{7,23},{8,24},{9,... | collective-permute-start | bytes 577544 | tf_op jit(solution)/shard_map/ppermute | solution.py:54
  24.7 6.9 %collective-permute-start.4 = (f16[75,16,128]{2,1,0:T(8,128)(2,1)S(1)}, f16[75,16,128]{2,1,0:T(8,128)(2,1)S(1)}, u32[]{:S(2)}, u32[]{:S(2)}) collective-permute-start(f16[75,16,128]{2,1,0:T(8,128)(2,1)S(1)} %select_convert_fusion.2), channel_id=1, source_target_pairs={{0,2},{1,3},{2,0},{3,1},{4,6},{5,7},{6,4},{7,5},{8,9},{9,8},{10,11... | collective-permute-start | bytes 921608 | tf_op jit(solution)/shard_map/ppermute | solution.py:54
  31.8 4.7 %collective-permute-start.7 = (f16[24,16,128]{2,1,0:T(8,128)(2,1)S(1)}, f16[24,16,128]{2,1,0:T(8,128)(2,1)S(1)}, u32[]{:S(2)}, u32[]{:S(2)}) collective-permute-start(f16[24,16,128]{2,1,0:T(8,128)(2,1)S(1)} %select_convert_fusion.6), channel_id=1, source_target_pairs={{0,1},{1,0},{2,3},{3,2},{4,5},{5,4},{6,7},{7,6},{8,9},{9,8},{10,11... | collective-permute-start | bytes 294920 | tf_op jit(solution)/shard_map/ppermute | solution.py:54
  33.4 5.2 %collective-permute-start.6 = (f16[38,16,128]{2,1,0:T(8,128)(2,1)S(1)}, f16[38,16,128]{2,1,0:T(8,128)(2,1)S(1)}, u32[]{:S(2)}, u32[]{:S(2)}) collective-permute-start(f16[38,16,128]{2,1,0:T(8,128)(2,1)S(1)} %select_convert_fusion.4), channel_id=1, source_target_pairs={{0,16},{1,17},{2,18},{3,19},{4,20},{5,21},{6,22},{7,23},{8,10},{9,... | collective-permute-start | bytes 466952 | tf_op jit(solution)/shard_map/ppermute | solution.py:54
  39.0 10.6 %collective-permute-start.8 = (f16[61,16,128]{2,1,0:T(8,128)(2,1)S(1)}, f16[61,16,128]{2,1,0:T(8,128)(2,1)S(1)}, u32[]{:S(2)}, u32[]{:S(2)}) collective-permute-start(f16[61,16,128]{2,1,0:T(8,128)(2,1)S(1)} %pad_maximum_fusion.2), channel_id=1, source_target_pairs={{0,4},{1,5},{2,6},{3,7},{4,0},{5,1},{6,2},{7,3},{8,12},{9,13},{10,... | collective-permute-start | bytes 749576 | tf_op jit(solution)/shard_map/ppermute | solution.py:54
  49.7 6.3 %collective-permute-start.11 = (bf16[960,128]{1,0:T(8,128)(2,1)S(1)}, bf16[960,128]{1,0:T(8,128)(2,1)S(1)}, u32[]{:S(2)}, u32[]{:S(2)}) collective-permute-start(bf16[960,128]{1,0:T(8,128)(2,1)S(1)} %bitcast.123), channel_id=1, source_target_pairs={{0,1},{1,0},{2,3},{3,2},{4,5},{5,4},{6,7},{7,6},{8,9},{9,8},{10,11... | collective-permute-start | bytes 737288 | tf_op jit(solution)/shard_map/ppermute | solution.py:54
  50.3 6.2 %collective-permute-start.10 = (bf16[960,128]{1,0:T(8,128)(2,1)S(1)}, bf16[960,128]{1,0:T(8,128)(2,1)S(1)}, u32[]{:S(2)}, u32[]{:S(2)}) collective-permute-start(bf16[960,128]{1,0:T(8,128)(2,1)S(1)} %bitcast.124), channel_id=1, source_target_pairs={{0,2},{1,3},{2,0},{3,1},{4,6},{5,7},{6,4},{7,5},{8,10},{9,11},{10,... | collective-permute-start | bytes 737288 | tf_op jit(solution)/shard_map/ppermute | solution.py:54
  50.4 8.7 %collective-permute-start.9 = (bf16[960,128]{1,0:T(8,128)(2,1)S(1)}, bf16[960,128]{1,0:T(8,128)(2,1)S(1)}, u32[]{:S(2)}, u32[]{:S(2)}) collective-permute-start(bf16[960,128]{1,0:T(8,128)(2,1)S(1)} %bitcast.125), channel_id=1, source_target_pairs={{0,16},{1,17},{10,26},{11,27},{20,4},{21,5},{30,14},{31,15},{2,24}... | collective-permute-start | bytes 737288 | tf_op jit(solution)/shard_map/ppermute | solution.py:380
  59.4 1.9 %collective-permute-start.13 = (bf16[1920,128]{1,0:T(8,128)(2,1)S(1)}, bf16[1920,128]{1,0:T(8,128)(2,1)S(1)}, u32[]{:S(2)}, u32[]{:S(2)}) collective-permute-start(bf16[1920,128]{1,0:T(8,128)(2,1)S(1)} %maximum_select_fusion), channel_id=1, source_target_pairs={{0,8},{1,9},{2,10},{3,11},{4,12},{5,13},{6,14},{7,15},{8,0},{9,1},... | collective-permute-start | bytes 1474568 | tf_op jit(solution)/shard_map/ppermute | solution.py:54
  59.6 9.6 %collective-permute-start.12 = (bf16[960,128]{1,0:T(8,128)(2,1)S(1)}, bf16[960,128]{1,0:T(8,128)(2,1)S(1)}, u32[]{:S(2)}, u32[]{:S(2)}) collective-permute-start(bf16[960,128]{1,0:T(8,128)(2,1)S(1)} %collective-permute-done.10.near), channel_id=1, source_target_pairs={{0,1},{1,0},{2,3},{3,2},{4,5},{5,4},{6,7},{7,6},{8,9},{9,8},{10,11... | collective-permute-start | bytes 737288 | tf_op jit(solution)/shard_map/ppermute | solution.py:54
  69.7 9.0 %collective-permute-start.16 = (f32[32,896]{1,0:T(8,128)S(1)}, f32[32,896]{1,0:T(8,128)S(1)}, u32[]{:S(2)}, u32[]{:S(2)}) collective-permute-start(f32[32,896]{1,0:T(8,128)S(1)} %get-tuple-element.88), channel_id=1, source_target_pairs={{0,8},{1,9},{2,10},{3,11},{4,12},{5,13},{6,14},{7,15},{8,0},{9,1},... | collective-permute-start | bytes 344072 | tf_op jit(solution)/shard_map/ppermute | solution.py:54
  69.9 8.8 %collective-permute-start.15 = (f32[32,896]{1,0:T(8,128)S(1)}, f32[32,896]{1,0:T(8,128)S(1)}, u32[]{:S(2)}, u32[]{:S(2)}) collective-permute-start(f32[32,896]{1,0:T(8,128)S(1)} %get-tuple-element.89), channel_id=1, source_target_pairs={{0,16},{1,17},{2,18},{3,19},{4,20},{5,21},{6,22},{7,23},{8,24},{9,... | collective-permute-start | bytes 344072 | tf_op jit(solution)/shard_map/ppermute | solution.py:54
  72.4 6.3 %collective-permute-start.14 = (f32[32,896]{1,0:T(8,128)S(1)}, f32[32,896]{1,0:T(8,128)S(1)}, u32[]{:S(2)}, u32[]{:S(2)}) collective-permute-start(f32[32,896]{1,0:T(8,128)S(1)} %get-tuple-element.90), channel_id=1, source_target_pairs={{0,24},{1,25},{2,26},{3,27},{4,28},{5,29},{6,30},{7,31},{8,16},{9,... | collective-permute-start | bytes 344072 | tf_op jit(solution)/shard_map/ppermute | solution.py:54

commit v6 on v5

--- a/solution.py
+++ b/solution.py
@@ -397,7 +397,7 @@
     partial = project(far, ahead, partial)
     partial = partial.reshape(4, virtuals // 4, -1)
     share = lambda flip: lax.dynamic_index_in_dim(partial, row_index ^ flip, 0, keepdims=False)
-    parts = [flipped(share(flip), (flip, 0), (flip, 0)) for flip in (3, 2, 1)]
+    parts = [flipped(share(flip), (flip, 0), (flip, 0)) for flip in (2, 1, 3)]
     gram = gram_rest(sizes, places, near, far, columns, gram)
     parts, gram = lax.optimization_barrier((parts, gram))
     naf_ints = share(0) + parts[0] + parts[1] + parts[2]

time: 79.6 us -> 79.7 us (level)
  no operation moved by 1% of the time
where the time goes in v6:
time: 79.7 us; the launch traced here: 79.5 us
  waiting for transfers between devices  33.1 us (42%)
  Pallas kernels  21 us (26%)
  starting transfers between devices  19.9 us (25%)
  other arithmetic  4.45 us (6%)
  between operations  1.05 us (1%)
    ppermute x16, waiting for transfers between devices, flipped(): return lax.ppermute(value, AXES, pairs)  30.4 us
    ppermute x16, starting transfers between devices, flipped(): return lax.ppermute(value, AXES, pairs)  17.3 us
    pallas_call x1, Pallas kernels, gram_first(): pl.pallas_call(functools.partial(gram_first_kernel, sizes, 1.0 / virtuals...  7.67 us
    pallas_call x1, Pallas kernels, gram_rest(): pl.pallas_call(functools.partial(gram_rest_kernel, sizes, 1.0 / virtuals)...  6.3 us
    pallas_call x1, Pallas kernels, half_pieces(): pl.pallas_call(functools.partial(half_first_kernel, sizes), grid_spec=plt...  3.39 us
    pallas_call x1, Pallas kernels, rest(): pl.pallas_call(functools.partial(half_rest_kernel, sizes), grid_spec=pltp...  3.11 us
    ppermute x1, waiting for transfers between devices, shards_4x8(): from_x = lax.ppermute(own, AXES, over_x)  2.7 us
    ppermute x1, starting transfers between devices, shards_4x8(): from_x = lax.ppermute(own, AXES, over_x)  2.6 us
  transfers between devices with their start and end apart: 17, of which 9 were waited for; matrix products, arithmetic and copies ran while one was open for 2% of the time, Pallas kernels for 21%

profile of v6, /device:TPU:0, one launch (start us, length us, event | category | flops | bytes accessed | tf_op | source)
XLA Modules:
  0.0 79.5 jit_solution(8491404407969358285)
XLA Ops:
  0.6 3.4 %shard_map.51 = (f32[297,16,128]{2,1,0:T(8,128)S(1)}, f32[185,16,128]{2,1,0:T(8,128)S(1)}) custom-call(s32[1]{0:T(128)} %bitcast.1.bits, bf16[160,128]{1,0:T(8,128)(2,1)} %vir.3, bf16[160,15360]{1,0:T(8,128)(2,1)} %ao.3), custom_call_target="tpu_custom_call" | custom-call | flops 314572800 | bytes 6389760 | tf_op jit(solution)/shard_map/pallas_call | solution.py:129
  4.7 1.0 %convert_element_type.287 = f16[185,16,128]{2,1,0:T(8,128)(2,1)} convert(f32[185,16,128]{2,1,0:T(8,128)S(1)} %get-tuple-element.42) | non-fusion elementwise | flops 378880 | bytes 2273280 | tf_op jit(solution)/shard_map/convert_element_type | solution.py:344
  5.8 3.1 %shard_map.50 = (f32[297,16,128]{2,1,0:T(8,128)S(1)}, f32[185,16,128]{2,1,0:T(8,128)S(1)}, f32[8,128]{1,0:T(8,128)S(1)}) custom-call(s32[1]{0:T(128)} %bitcast.bits, bf16[160,128]{1,0:T(8,128)(2,1)} %vir.3, bf16[160,15360]{1,0:T(8,128)(2,1)} %ao.3), custom_call_target="tpu_custom_call" | custom-call | flops 314572800 | bytes 6389760 | tf_op jit(solution)/shard_map/pallas_call | solution.py:146
  9.6 3.1 %collective-permute-start.3 = (f16[93,16,128]{2,1,0:T(8,128)(2,1)S(1)}, f16[93,16,128]{2,1,0:T(8,128)(2,1)S(1)}, u32[]{:S(2)}, u32[]{:S(2)}) collective-permute-start(f16[93,16,128]{2,1,0:T(8,128)(2,1)S(1)} %select_convert_fusion.1), channel_id=1, source_target_pairs={{0,2},{1,3},{2,0},{3,1},{4,6},{5,7},{6,4},{7,5},{8,10},{9,11},{10,... | collective-permute-start | bytes 1142792 | tf_op jit(solution)/shard_map/ppermute | solution.py:54
  12.6 1.5 %collective-permute-start.2 = (f16[149,16,128]{2,1,0:T(8,128)(2,1)S(1)}, f16[149,16,128]{2,1,0:T(8,128)(2,1)S(1)}, u32[]{:S(2)}, u32[]{:S(2)}) collective-permute-start(f16[149,16,128]{2,1,0:T(8,128)(2,1)S(1)} %select_convert_fusion), channel_id=1, source_target_pairs={{0,1},{1,0},{2,3},{3,2},{4,5},{5,4},{6,7},{7,6},{8,24},{9,25},{10,... | collective-permute-start | bytes 1830920 | tf_op jit(solution)/shard_map/ppermute | solution.py:54
  14.5 8.2 %collective-permute-done.2 = f16[149,16,128]{2,1,0:T(8,128)(2,1)S(1)} collective-permute-done((f16[149,16,128]{2,1,0:T(8,128)(2,1)S(1)}, f16[149,16,128]{2,1,0:T(8,128)(2,1)S(1)}, u32[]{:S(2)}, u32[]{:S(2)}) %collective-permute-start.2) | collective-permute-done | bytes 610336 | tf_op jit(solution)/shard_map/ppermute | solution.py:54
  23.1 1.6 %collective-permute-start.5 = (f16[47,16,128]{2,1,0:T(8,128)(2,1)S(1)}, f16[47,16,128]{2,1,0:T(8,128)(2,1)S(1)}, u32[]{:S(2)}, u32[]{:S(2)}) collective-permute-start(f16[47,16,128]{2,1,0:T(8,128)(2,1)S(1)} %select_convert_fusion.3), channel_id=1, source_target_pairs={{0,16},{1,17},{2,18},{3,19},{4,20},{5,21},{6,22},{7,23},{8,24},{9,... | collective-permute-start | bytes 577544 | tf_op jit(solution)/shard_map/ppermute | solution.py:54
  24.7 0.7 collective-permute-start.4
  25.5 6.0 %collective-permute-done.4 = f16[75,16,128]{2,1,0:T(8,128)(2,1)S(1)} collective-permute-done((f16[75,16,128]{2,1,0:T(8,128)(2,1)S(1)}, f16[75,16,128]{2,1,0:T(8,128)(2,1)S(1)}, u32[]{:S(2)}, u32[]{:S(2)}) %collective-permute-start.4) | collective-permute-done | bytes 307232 | tf_op jit(solution)/shard_map/ppermute | solution.py:54
  31.8 1.6 %collective-permute-start.7 = (f16[24,16,128]{2,1,0:T(8,128)(2,1)S(1)}, f16[24,16,128]{2,1,0:T(8,128)(2,1)S(1)}, u32[]{:S(2)}, u32[]{:S(2)}) collective-permute-start(f16[24,16,128]{2,1,0:T(8,128)(2,1)S(1)} %select_convert_fusion.6), channel_id=1, source_target_pairs={{0,1},{1,0},{2,3},{3,2},{4,5},{5,4},{6,7},{7,6},{8,9},{9,8},{10,11... | collective-permute-start | bytes 294920 | tf_op jit(solution)/shard_map/ppermute | solution.py:54
  33.4 0.5 collective-permute-start.6
  34.0 2.5 %collective-permute-done.7 = f16[24,16,128]{2,1,0:T(8,128)(2,1)S(1)} collective-permute-done((f16[24,16,128]{2,1,0:T(8,128)(2,1)S(1)}, f16[24,16,128]{2,1,0:T(8,128)(2,1)S(1)}, u32[]{:S(2)}, u32[]{:S(2)}) %collective-permute-start.7) | collective-permute-done | bytes 98336 | tf_op jit(solution)/shard_map/ppermute | solution.py:54
  36.5 2.1 %collective-permute-done.6 = f16[38,16,128]{2,1,0:T(8,128)(2,1)S(1)} collective-permute-done((f16[38,16,128]{2,1,0:T(8,128)(2,1)S(1)}, f16[38,16,128]{2,1,0:T(8,128)(2,1)S(1)}, u32[]{:S(2)}, u32[]{:S(2)}) %collective-permute-start.6) | collective-permute-done | bytes 155680 | tf_op jit(solution)/shard_map/ppermute | solution.py:54
  39.0 2.7 %collective-permute-start.8 = (f16[61,16,128]{2,1,0:T(8,128)(2,1)S(1)}, f16[61,16,128]{2,1,0:T(8,128)(2,1)S(1)}, u32[]{:S(2)}, u32[]{:S(2)}) collective-permute-start(f16[61,16,128]{2,1,0:T(8,128)(2,1)S(1)} %pad_maximum_fusion.2), channel_id=1, source_target_pairs={{0,4},{1,5},{2,6},{3,7},{4,0},{5,1},{6,2},{7,3},{8,12},{9,13},{10,... | collective-permute-start | bytes 749576 | tf_op jit(solution)/shard_map/ppermute | solution.py:54
  41.6 7.9 %collective-permute-done.8 = f16[61,16,128]{2,1,0:T(8,128)(2,1)S(1)} collective-permute-done((f16[61,16,128]{2,1,0:T(8,128)(2,1)S(1)}, f16[61,16,128]{2,1,0:T(8,128)(2,1)S(1)}, u32[]{:S(2)}, u32[]{:S(2)}) %collective-permute-start.8) | collective-permute-done | bytes 249888 | tf_op jit(solution)/shard_map/ppermute | solution.py:54
  49.7 0.6 collective-permute-start.11
  50.4 2.6 %collective-permute-start.9 = (bf16[960,128]{1,0:T(8,128)(2,1)S(1)}, bf16[960,128]{1,0:T(8,128)(2,1)S(1)}, u32[]{:S(2)}, u32[]{:S(2)}) collective-permute-start(bf16[960,128]{1,0:T(8,128)(2,1)S(1)} %bitcast.125), channel_id=1, source_target_pairs={{0,16},{1,17},{10,26},{11,27},{20,4},{21,5},{30,14},{31,15},{2,24}... | collective-permute-start | bytes 737288 | tf_op jit(solution)/shard_map/ppermute | solution.py:380
  53.0 2.9 %collective-permute-done.11 = bf16[960,128]{1,0:T(8,128)(2,1)S(1)} collective-permute-done((bf16[960,128]{1,0:T(8,128)(2,1)S(1)}, bf16[960,128]{1,0:T(8,128)(2,1)S(1)}, u32[]{:S(2)}, u32[]{:S(2)}) %collective-permute-start.11) | collective-permute-done | bytes 245792 | tf_op jit(solution)/shard_map/ppermute | solution.py:54
  56.5 2.7 %collective-permute-done.9 = bf16[960,128]{1,0:T(8,128)(2,1)S(1)} collective-permute-done((bf16[960,128]{1,0:T(8,128)(2,1)S(1)}, bf16[960,128]{1,0:T(8,128)(2,1)S(1)}, u32[]{:S(2)}, u32[]{:S(2)}) %collective-permute-start.9) | collective-permute-done | bytes 245792 | tf_op jit(solution)/shard_map/ppermute | solution.py:380
  59.6 1.5 %collective-permute-start.12 = (bf16[960,128]{1,0:T(8,128)(2,1)S(1)}, bf16[960,128]{1,0:T(8,128)(2,1)S(1)}, u32[]{:S(2)}, u32[]{:S(2)}) collective-permute-start(bf16[960,128]{1,0:T(8,128)(2,1)S(1)} %collective-permute-done.10.near), channel_id=1, source_target_pairs={{0,1},{1,0},{2,3},{3,2},{4,5},{5,4},{6,7},{7,6},{8,9},{9,8},{10,11... | collective-permute-start | bytes 737288 | tf_op jit(solution)/shard_map/ppermute | solution.py:54
  61.5 7.7 %shard_map.52 = (f32[3840,1920]{1,0:T(8,128)}, f32[128,896]{1,0:T(8,128)S(1)}, bf16[960,896]{1,0:T(8,128)(2,1)S(1)}) custom-call(s32[4]{0:T(128)S(1)} %pad_add_fusion.places, bf16[1920,128]{1,0:T(8,128)(2,1)S(1)} %pad_maximum_fusion.pair, bf16[960,128]{1,0:T(8,128)(2,1)S(1)} %collective-permute-done.10.near, bf16[1920,128]{1,0:T(8,128)(2,1)S(1)} %pad_maximum_fusion.1.cols, ...), custom_call_target="tpu_custom_call" | custom-call | flops 943718400 | bytes 14745600 | tf_op jit(solution)/shard_map/pallas_call | solution.py:272
  69.7 2.3 %collective-permute-start.16 = (f32[32,896]{1,0:T(8,128)S(1)}, f32[32,896]{1,0:T(8,128)S(1)}, u32[]{:S(2)}, u32[]{:S(2)}) collective-permute-start(f32[32,896]{1,0:T(8,128)S(1)} %get-tuple-element.88), channel_id=1, source_target_pairs={{0,24},{1,25},{2,26},{3,27},{4,28},{5,29},{6,30},{7,31},{8,16},{9,... | collective-permute-start | bytes 344072 | tf_op jit(solution)/shard_map/ppermute | solution.py:54
  72.5 6.3 %shard_map.54 = f32[3840,1920]{1,0:T(8,128)} custom-call(s32[4]{0:T(128)S(1)} %pad_add_fusion.places, bf16[960,128]{1,0:T(8,128)(2,1)S(1)} %collective-permute-done.10.near, bf16[960,128]{1,0:T(8,128)(2,1)S(1)} %collective-permute-done.12.far, bf16[1920,128]{1,0:T(8,128)(2,1)S(1)} %pad_maximum_fusion.1.cols, ...), custom_call_target="tpu_custom_call", output_to_operand_aliasing={{}: (4, {})} | custom-call | flops 943718400 | bytes 14745600 | tf_op jit(solution)/shard_map/pallas_call | solution.py:300
  78.8 0.7 fusion.6
  (70 shorter events, 5.3 us)
Async XLA Ops:
  4.2 4.7 %collective-permute-start = (f16[297,16,128]{2,1,0:T(8,128)(2,1)S(1)}, f16[297,16,128]{2,1,0:T(8,128)(2,1)S(1)}, u32[]{:S(2)}, u32[]{:S(2)}) collective-permute-start(f16[297,16,128]{2,1,0:T(8,128)(2,1)S(1)} %convert_element_type.284), channel_id=1, source_target_pairs={{0,8},{1,9},{2,10},{3,11},{4,12},{5,13},{6,14},{7,15},{8,0},{9,1},... | collective-permute-start | bytes 3649544 | tf_op jit(solution)/shard_map/ppermute | solution.py:54
  5.7 3.3 %collective-permute-start.1 = (f16[185,16,128]{2,1,0:T(8,128)(2,1)}, f16[185,16,128]{2,1,0:T(8,128)(2,1)S(1)}, u32[]{:S(2)}, u32[]{:S(2)}) collective-permute-start(f16[185,16,128]{2,1,0:T(8,128)(2,1)} %convert_element_type.287), channel_id=1, source_target_pairs={{0,8},{1,9},{2,10},{3,11},{4,12},{5,13},{6,14},{7,15},{8,0},{9,1},... | collective-permute-start | bytes 2273288 | tf_op jit(solution)/shard_map/ppermute | solution.py:54
  9.6 13.2 %collective-permute-start.3 = (f16[93,16,128]{2,1,0:T(8,128)(2,1)S(1)}, f16[93,16,128]{2,1,0:T(8,128)(2,1)S(1)}, u32[]{:S(2)}, u32[]{:S(2)}) collective-permute-start(f16[93,16,128]{2,1,0:T(8,128)(2,1)S(1)} %select_convert_fusion.1), channel_id=1, source_target_pairs={{0,2},{1,3},{2,0},{3,1},{4,6},{5,7},{6,4},{7,5},{8,10},{9,11},{10,... | collective-permute-start | bytes 1142792 | tf_op jit(solution)/shard_map/ppermute | solution.py:54
  12.6 10.1 %collective-permute-start.2 = (f16[149,16,128]{2,1,0:T(8,128)(2,1)S(1)}, f16[149,16,128]{2,1,0:T(8,128)(2,1)S(1)}, u32[]{:S(2)}, u32[]{:S(2)}) collective-permute-start(f16[149,16,128]{2,1,0:T(8,128)(2,1)S(1)} %select_convert_fusion), channel_id=1, source_target_pairs={{0,1},{1,0},{2,3},{3,2},{4,5},{5,4},{6,7},{7,6},{8,24},{9,25},{10,... | collective-permute-start | bytes 1830920 | tf_op jit(solution)/shard_map/ppermute | solution.py:54
  23.1 8.4 %collective-permute-start.5 = (f16[47,16,128]{2,1,0:T(8,128)(2,1)S(1)}, f16[47,16,128]{2,1,0:T(8,128)(2,1)S(1)}, u32[]{:S(2)}, u32[]{:S(2)}) collective-permute-start(f16[47,16,128]{2,1,0:T(8,128)(2,1)S(1)} %select_convert_fusion.3), channel_id=1, source_target_pairs={{0,16},{1,17},{2,18},{3,19},{4,20},{5,21},{6,22},{7,23},{8,24},{9,... | collective-permute-start | bytes 577544 | tf_op jit(solution)/shard_map/ppermute | solution.py:54
  24.7 6.9 %collective-permute-start.4 = (f16[75,16,128]{2,1,0:T(8,128)(2,1)S(1)}, f16[75,16,128]{2,1,0:T(8,128)(2,1)S(1)}, u32[]{:S(2)}, u32[]{:S(2)}) collective-permute-start(f16[75,16,128]{2,1,0:T(8,128)(2,1)S(1)} %select_convert_fusion.2), channel_id=1, source_target_pairs={{0,2},{1,3},{2,0},{3,1},{4,6},{5,7},{6,4},{7,5},{8,9},{9,8},{10,11... | collective-permute-start | bytes 921608 | tf_op jit(solution)/shard_map/ppermute | solution.py:54
  31.8 4.7 %collective-permute-start.7 = (f16[24,16,128]{2,1,0:T(8,128)(2,1)S(1)}, f16[24,16,128]{2,1,0:T(8,128)(2,1)S(1)}, u32[]{:S(2)}, u32[]{:S(2)}) collective-permute-start(f16[24,16,128]{2,1,0:T(8,128)(2,1)S(1)} %select_convert_fusion.6), channel_id=1, source_target_pairs={{0,1},{1,0},{2,3},{3,2},{4,5},{5,4},{6,7},{7,6},{8,9},{9,8},{10,11... | collective-permute-start | bytes 294920 | tf_op jit(solution)/shard_map/ppermute | solution.py:54
  33.4 5.2 %collective-permute-start.6 = (f16[38,16,128]{2,1,0:T(8,128)(2,1)S(1)}, f16[38,16,128]{2,1,0:T(8,128)(2,1)S(1)}, u32[]{:S(2)}, u32[]{:S(2)}) collective-permute-start(f16[38,16,128]{2,1,0:T(8,128)(2,1)S(1)} %select_convert_fusion.4), channel_id=1, source_target_pairs={{0,16},{1,17},{2,18},{3,19},{4,20},{5,21},{6,22},{7,23},{8,10},{9,... | collective-permute-start | bytes 466952 | tf_op jit(solution)/shard_map/ppermute | solution.py:54
  39.0 10.6 %collective-permute-start.8 = (f16[61,16,128]{2,1,0:T(8,128)(2,1)S(1)}, f16[61,16,128]{2,1,0:T(8,128)(2,1)S(1)}, u32[]{:S(2)}, u32[]{:S(2)}) collective-permute-start(f16[61,16,128]{2,1,0:T(8,128)(2,1)S(1)} %pad_maximum_fusion.2), channel_id=1, source_target_pairs={{0,4},{1,5},{2,6},{3,7},{4,0},{5,1},{6,2},{7,3},{8,12},{9,13},{10,... | collective-permute-start | bytes 749576 | tf_op jit(solution)/shard_map/ppermute | solution.py:54
  49.7 6.3 %collective-permute-start.11 = (bf16[960,128]{1,0:T(8,128)(2,1)S(1)}, bf16[960,128]{1,0:T(8,128)(2,1)S(1)}, u32[]{:S(2)}, u32[]{:S(2)}) collective-permute-start(bf16[960,128]{1,0:T(8,128)(2,1)S(1)} %bitcast.123), channel_id=1, source_target_pairs={{0,1},{1,0},{2,3},{3,2},{4,5},{5,4},{6,7},{7,6},{8,9},{9,8},{10,11... | collective-permute-start | bytes 737288 | tf_op jit(solution)/shard_map/ppermute | solution.py:54
  50.3 6.2 %collective-permute-start.10 = (bf16[960,128]{1,0:T(8,128)(2,1)S(1)}, bf16[960,128]{1,0:T(8,128)(2,1)S(1)}, u32[]{:S(2)}, u32[]{:S(2)}) collective-permute-start(bf16[960,128]{1,0:T(8,128)(2,1)S(1)} %bitcast.124), channel_id=1, source_target_pairs={{0,2},{1,3},{2,0},{3,1},{4,6},{5,7},{6,4},{7,5},{8,10},{9,11},{10,... | collective-permute-start | bytes 737288 | tf_op jit(solution)/shard_map/ppermute | solution.py:54
  50.4 8.7 %collective-permute-start.9 = (bf16[960,128]{1,0:T(8,128)(2,1)S(1)}, bf16[960,128]{1,0:T(8,128)(2,1)S(1)}, u32[]{:S(2)}, u32[]{:S(2)}) collective-permute-start(bf16[960,128]{1,0:T(8,128)(2,1)S(1)} %bitcast.125), channel_id=1, source_target_pairs={{0,16},{1,17},{10,26},{11,27},{20,4},{21,5},{30,14},{31,15},{2,24}... | collective-permute-start | bytes 737288 | tf_op jit(solution)/shard_map/ppermute | solution.py:380
  59.4 1.9 %collective-permute-start.13 = (bf16[1920,128]{1,0:T(8,128)(2,1)S(1)}, bf16[1920,128]{1,0:T(8,128)(2,1)S(1)}, u32[]{:S(2)}, u32[]{:S(2)}) collective-permute-start(bf16[1920,128]{1,0:T(8,128)(2,1)S(1)} %maximum_select_fusion), channel_id=1, source_target_pairs={{0,8},{1,9},{2,10},{3,11},{4,12},{5,13},{6,14},{7,15},{8,0},{9,1},... | collective-permute-start | bytes 1474568 | tf_op jit(solution)/shard_map/ppermute | solution.py:54
  59.6 9.6 %collective-permute-start.12 = (bf16[960,128]{1,0:T(8,128)(2,1)S(1)}, bf16[960,128]{1,0:T(8,128)(2,1)S(1)}, u32[]{:S(2)}, u32[]{:S(2)}) collective-permute-start(bf16[960,128]{1,0:T(8,128)(2,1)S(1)} %collective-permute-done.10.near), channel_id=1, source_target_pairs={{0,1},{1,0},{2,3},{3,2},{4,5},{5,4},{6,7},{7,6},{8,9},{9,8},{10,11... | collective-permute-start | bytes 737288 | tf_op jit(solution)/shard_map/ppermute | solution.py:54
  69.7 9.1 %collective-permute-start.16 = (f32[32,896]{1,0:T(8,128)S(1)}, f32[32,896]{1,0:T(8,128)S(1)}, u32[]{:S(2)}, u32[]{:S(2)}) collective-permute-start(f32[32,896]{1,0:T(8,128)S(1)} %get-tuple-element.88), channel_id=1, source_target_pairs={{0,24},{1,25},{2,26},{3,27},{4,28},{5,29},{6,30},{7,31},{8,16},{9,... | collective-permute-start | bytes 344072 | tf_op jit(solution)/shard_map/ppermute | solution.py:54
  72.0 6.8 %collective-permute-start.15 = (f32[32,896]{1,0:T(8,128)S(1)}, f32[32,896]{1,0:T(8,128)S(1)}, u32[]{:S(2)}, u32[]{:S(2)}) collective-permute-start(f32[32,896]{1,0:T(8,128)S(1)} %get-tuple-element.89), channel_id=1, source_target_pairs={{0,8},{1,9},{2,10},{3,11},{4,12},{5,13},{6,14},{7,15},{8,0},{9,1},... | collective-permute-start | bytes 344072 | tf_op jit(solution)/shard_map/ppermute | solution.py:54
  72.4 6.4 %collective-permute-start.14 = (f32[32,896]{1,0:T(8,128)S(1)}, f32[32,896]{1,0:T(8,128)S(1)}, u32[]{:S(2)}, u32[]{:S(2)}) collective-permute-start(f32[32,896]{1,0:T(8,128)S(1)} %get-tuple-element.90), channel_id=1, source_target_pairs={{0,16},{1,17},{2,18},{3,19},{4,20},{5,21},{6,22},{7,23},{8,24},{9,... | collective-permute-start | bytes 344072 | tf_op jit(solution)/shard_map/ppermute | solution.py:54
